TPU v7x, 32 devices: a whole 2x2x4 slice. The times are simulated.
32 devices in a mesh: grp: 2 (over x), rows: 8 (over z, y), cols: 2 (over core).
Axes of the slice: x: 2, y: 2, z: 4, core: 2. Of those that a mesh axis runs over, the one named last changes fastest.
Arguments:
- crop_feature_grid: bfloat16 [128, 256, 512], P(('grp', 'rows'), 'cols'), parts along dimension 0, may hold values from -6 to 6
- pixel_layernorm_gain: float32 [512], replicated, may hold values from 0.25 to 1.75
- triple_projection_matrix: bfloat16 [512, 1536], replicated, may hold values from -0.25 to 0.25
- halo_exit_matrix: bfloat16 [512, 512], replicated, may hold values from -0.25 to 0.25
- memory_slots: bfloat16 [256, 512], replicated, may hold values from -6 to 6
- memory_layernorm_gain: float32 [512], replicated, may hold values from 0.25 to 1.75
- memory_asking_matrix: bfloat16 [512, 512], replicated, may hold values from -0.25 to 0.25
- memory_exit_matrix: bfloat16 [512, 512], replicated, may hold values from -0.25 to 0.25
- branch_logit_multiplier: float32 [8], replicated, may hold values from 1 to 30, as said below
Outputs:
- tokens_out: bfloat16 [128, 256, 512], P(('grp', 'rows'), 'cols'), parts along dimension 0
- latent_mix: bfloat16 [512, 512], P('grp'), parts along dimension 0
There are 2 independent parts, one for each index of `grp`. A program takes and returns all parts, laid end to end along the dimension named above; an argument that names none is the same for every part. Nothing has to cross between parts.
Inputs may be any that keep to these rules, and one draw needn't show every extreme that they name: `branch_logit_multiplier`: a positive logit scale for each head.
All inputs are finite; a program needn't handle non-finite values.
Results may differ from a plain program's by a relative error of at most 0.0095.
The roundings to bfloat16 on the way count: a program that leaves them out, or rounds other values in their place, can miss the bound.
Values may be sent and summed in bfloat16 or wider, within the bound.
No kernel may reach another device: no remote copies, remote signals or barrier semaphores. Data moves between devices by JAX's collectives and lax.ppermute only.
A program may use at most 192 MiB of HBM per device.

v0:
```python
import math

import jax
import jax.numpy as jnp
from jax import lax
from jax.sharding import PartitionSpec as P

H = 8
BLK = 8
RIM = 3


def with_halo(array, sides, width):
    for axis, dim in sides:
        devices, length = (lax.axis_size(axis), array.shape[dim])
        up = [(i, (i + 1) % devices) for i in range(devices - 1)]
        down = [(j, i) for i, j in up]
        last = lax.slice_in_dim(array, length - width, length, axis=dim)
        initial = lax.slice_in_dim(array, 0, width, axis=dim)
        before = lax.ppermute(last, axis, up)
        after = lax.ppermute(initial, axis, down)
        array = jnp.concatenate([before, array, after], axis=dim)
    return array


def row_norm(values, gain_vector):
    floats = values.astype(jnp.float32)
    scaled = floats * lax.rsqrt(jnp.mean(floats * floats, axis=-1, keepdims=True) + 1e-05)
    return (scaled * gain_vector).astype(jnp.bfloat16)


def head_norm(floats, head_count):
    shaped = floats.reshape(floats.shape[:-1] + (head_count, floats.shape[-1] // head_count))
    normal = shaped * lax.rsqrt(jnp.mean(shaped * shaped, axis=-1, keepdims=True) + 1e-06)
    return normal.astype(jnp.bfloat16)


def halo_attention(queries, keys_ext, values_ext, inside, logit_divisor):
    rows_all, cols_all, head_count, channels_per_branch = queries.shape
    blocks_across = cols_all // BLK
    window = BLK + 2 * RIM
    offsets = (jnp.arange(blocks_across, dtype=jnp.int32) * BLK)[:, None] + jnp.arange(
        window, dtype=jnp.int32
    )[None, :]

    def one_row(block_row):
        query_blocks = queries.reshape(BLK, blocks_across, BLK, head_count, channels_per_branch)
        query_blocks = query_blocks.transpose(1, 0, 2, 3, 4).reshape(
            blocks_across, BLK * BLK, head_count, channels_per_branch
        )
        key_slab = keys_ext[:, offsets]
        key_blocks = key_slab.transpose(1, 0, 2, 3, 4).reshape(
            blocks_across, window * window, head_count, channels_per_branch
        )
        value_slab = values_ext[:, offsets]
        value_blocks = value_slab.transpose(1, 0, 2, 3, 4).reshape(
            blocks_across, window * window, head_count, channels_per_branch
        )
        mask_slab = inside[:, offsets]
        mask_blocks = mask_slab.transpose(1, 0, 2).reshape(blocks_across, window * window)
        scores = jnp.einsum(
            "bqhd,bkhd->bhqk", query_blocks, key_blocks, preferred_element_type=jnp.float32
        )
        scores = scores * logit_divisor[None, :, None, None]
        scores = jnp.where(mask_blocks[:, None, None, :], scores, -1e30)
        row_peak = jnp.max(scores, axis=-1, keepdims=True)
        expo = jnp.exp(scores - row_peak)
        row_total = jnp.sum(expo, axis=-1)
        weights = expo.astype(jnp.bfloat16)
        output = jnp.einsum(
            "bhqk,bkhd->bqhd", weights, value_blocks, preferred_element_type=jnp.float32
        )
        output = output / row_total.transpose(0, 2, 1)[..., None]
        output = output.reshape(
            blocks_across, BLK, BLK, head_count * channels_per_branch
        ).transpose(1, 0, 2, 3)
        return output.reshape(BLK, cols_all, head_count * channels_per_branch).astype(jnp.bfloat16)

    result = lax.map(one_row, jnp.arange(rows_all // BLK, dtype=jnp.int32))
    return result.reshape(rows_all, cols_all, head_count * channels_per_branch)


def per_device(
    crop_feature_grid,
    pixel_layernorm_gain,
    triple_projection_matrix,
    halo_exit_matrix,
    memory_slots,
    memory_layernorm_gain,
    memory_asking_matrix,
    memory_exit_matrix,
    branch_logit_multiplier,
):
    tile_rows, tile_cols, model_width = crop_feature_grid.shape
    head_count = H
    channels_per_branch = model_width // head_count
    normed = row_norm(crop_feature_grid, pixel_layernorm_gain)
    flat_normed = normed.reshape(-1, model_width)
    logit_divisor = branch_logit_multiplier / math.sqrt(channels_per_branch)
    projected = jnp.dot(flat_normed, triple_projection_matrix, preferred_element_type=jnp.float32)
    projected = projected.reshape(tile_rows, tile_cols, 3 * model_width)
    queries = head_norm(projected[..., :model_width], head_count)
    keys = head_norm(projected[..., model_width : 2 * model_width], head_count)
    values = (
        projected[..., 2 * model_width :]
        .reshape(tile_rows, tile_cols, head_count, channels_per_branch)
        .astype(jnp.bfloat16)
    )
    key_value = jnp.concatenate(
        [
            keys.reshape(tile_rows, tile_cols, model_width),
            values.reshape(tile_rows, tile_cols, model_width),
        ],
        axis=2,
    )
    key_value_ext = with_halo(key_value, (("rows", 0), ("cols", 1)), RIM)
    ext_rows, ext_cols = (key_value_ext.shape[0], key_value_ext.shape[1])
    keys_ext = key_value_ext[..., :model_width].reshape(
        ext_rows, ext_cols, head_count, channels_per_branch
    )
    values_ext = key_value_ext[..., model_width:].reshape(
        ext_rows, ext_cols, head_count, channels_per_branch
    )
    crop_rows = tile_rows * lax.axis_size("rows")
    crop_cols = tile_cols * lax.axis_size("cols")
    row_ids = (
        lax.axis_index("rows") * tile_rows - RIM + jnp.arange(tile_rows + 2 * RIM, dtype=jnp.int32)
    )
    col_ids = (
        lax.axis_index("cols") * tile_cols - RIM + jnp.arange(tile_cols + 2 * RIM, dtype=jnp.int32)
    )
    row_inside = (row_ids >= 0) & (row_ids < crop_rows)
    col_inside = (col_ids >= 0) & (col_ids < crop_cols)
    inside = row_inside[:, None] & col_inside[None, :]
    attended = halo_attention(queries, keys_ext, values_ext, inside, logit_divisor)
    branch = jnp.dot(
        attended.reshape(-1, model_width), halo_exit_matrix, preferred_element_type=jnp.float32
    )
    tokens_out = (
        crop_feature_grid.astype(jnp.float32) + branch.reshape(tile_rows, tile_cols, model_width)
    ).astype(jnp.bfloat16)
    latent_normed = row_norm(memory_slots, memory_layernorm_gain)
    latent_queries = head_norm(
        jnp.dot(latent_normed, memory_asking_matrix, preferred_element_type=jnp.float32), head_count
    )
    keys_heads = keys.reshape(-1, head_count, channels_per_branch).transpose(1, 0, 2)
    values_heads = values.reshape(-1, head_count, channels_per_branch).transpose(1, 0, 2)

    def one_head(operands):
        query_head, key_head, value_head, head_scale = operands
        scores = jnp.dot(query_head, key_head.T, preferred_element_type=jnp.float32) * head_scale
        row_peak = jnp.max(scores, axis=-1)
        expo = jnp.exp(scores - row_peak[:, None])
        row_total = jnp.sum(expo, axis=-1)
        weighted = jnp.dot(
            expo.astype(jnp.bfloat16), value_head, preferred_element_type=jnp.float32
        )
        return (row_peak, row_total, weighted)

    local_peak, local_total, local_sum = lax.map(
        one_head, (latent_queries.transpose(1, 0, 2), keys_heads, values_heads, logit_divisor)
    )
    crop_peak = lax.pmax(local_peak, ("rows", "cols"))
    factor = jnp.exp(local_peak - crop_peak)
    crop_total, crop_sum = lax.psum(
        (local_total * factor, local_sum * factor[..., None]), ("rows", "cols")
    )
    latent_heads = crop_sum / crop_total[..., None]
    latent_attended = latent_heads.transpose(1, 0, 2).reshape(-1, model_width).astype(jnp.bfloat16)
    latent_mix = jnp.dot(
        latent_attended, memory_exit_matrix, preferred_element_type=jnp.float32
    ).astype(jnp.bfloat16)
    return (tokens_out, latent_mix)


def solution(mesh):
    return jax.shard_map(
        per_device,
        mesh=mesh,
        in_specs=(P(("grp", "rows"), "cols", None), P(), P(), P(), P(), P(), P(), P(), P()),
        out_specs=(P(("grp", "rows"), "cols", None), P("grp", None)),
        check_vma=False,
    )
```

profile of v0, /device:TPU:0, one launch (start us, length us, event | category | flops | bytes accessed | tf_op | source)
XLA Modules:
  0.0 278.7 jit_solution(9625256363272125825)
XLA Ops:
  8.9 3.1 %fusion.33 = f32[8,128,1536]{2,1,0:T(8,128)S(1)} fusion(bf16[512,1536]{1,0:T(8,128)(2,1)S(1)} %copy-done, bf16[8,128,512]{2,1,0:T(8,128)(2,1)} %param.11, f32[512]{0:T(512)} %param.12, f32[8,128]{1,0:T(8,128)S(1)} %add_rsqrt_fusion.3), kind=kOutput, calls=%fused_computation.50 | convolution fusion | flops 1612709888 | bytes 8919040 | tf_op jit(solution)/shard_map/dot_general | solution.py:100
  12.0 4.1 %fusion.58 = (f32[8,128,512]{2,1,0:T(8,128)}, f32[8,128,512]{2,1,0:T(8,128)}, f32[8,128,512]{2,1,0:T(8,128)}, f32[8,128,512]{2,1,0:T(8,128)}) fusion(f32[8,128,1536]{2,1,0:T(8,128)S(1)} %fusion.33), kind=kLoop, calls=%fused_computation.97 | loop fusion | flops 1048576 | bytes 12582912 | tf_op jit(solution)/shard_map/slice | solution.py:103
  17.4 2.9 %copy.38 = f32[8,128,512]{1,2,0:T(8,128)} copy(f32[8,128,512]{2,1,0:T(8,128)} %get-tuple-element.110) | data formatting | bytes 4194304 | tf_op jit(solution)/shard_map/mul | solution.py:34
  22.1 2.9 %copy.52 = f32[8,128,512]{1,0,2:T(8,128)} copy(f32[8,128,512]{2,1,0:T(8,128)} %get-tuple-element.109) | data formatting | bytes 4194304 | tf_op jit(solution)/shard_map/slice | solution.py:103
  25.1 2.8 reshape.193
  32.4 32.1 %while.4 = (s32[]{:T(128)}, f32[8,256]{1,0:T(8,128)S(1)}, f32[8,256]{1,0:T(8,128)S(1)}, f32[8,256,64]{1,2,0:T(8,128)}, bf16[8,256,64]{1,2,0:T(8,128)(2,1)S(1)}, ...) while((s32[]{:T(128)}, f32[8,256]{1,0:T(8,128)S(1)}, ...), condition=%wide.region_10.11_spmd, body=%wide.region_7.0_spmd.sunk | while | flops 68681216 | bytes 3517049 | solution.py:160
  38.2 1.9 fusion.73
  42.2 1.9 fusion.73
  54.2 1.9 fusion.73
  64.5 35.4 %pmax.7 = f32[8,256]{1,0:T(8,128)S(1)} all-reduce(f32[8,256]{1,0:T(8,128)S(1)} %get-tuple-element.71), channel_id=1, replica_groups=mesh['grp'=2,'rows'=8,'cols'=2] {'rows','cols'}, use_global_device_ids=true, to_apply=%region_11.12 | all-reduce | flops 2048 | bytes 16384 | tf_op jit(solution)/shard_map/pmax | solution.py:163
  100.0 1.9 broadcast_multiply_fusion
  103.4 2.9 %copy.39 = f32[8,128,512]{2,1,0:T(8,128)} copy(f32[8,128,512]{1,2,0:T(8,128)} %bitcast.105) | data formatting | bytes 4194304 | tf_op jit(solution)/shard_map/mul | solution.py:34
  106.3 2.6 multiply_convert_fusion.2
  113.1 4.4 %reshape.188 = f32[8,16,8,8,64]{4,3,2,1,0:T(8,128)} reshape(f32[8,128,512]{2,1,0:T(8,128)} %get-tuple-element.112) | data formatting | bytes 4194304 | tf_op jit(solution)/shard_map/reshape | solution.py:33
  117.4 2.9 %copy.43 = f32[8,128,512]{1,2,0:T(8,128)} copy(f32[8,128,512]{2,1,0:T(8,128)} %get-tuple-element.111) | data formatting | bytes 4194304 | tf_op jit(solution)/shard_map/mul | solution.py:34
  124.5 40.9 %psum.15 = f32[8,256]{1,0:T(8,128)S(1)} all-reduce(f32[8,256]{1,0:T(8,128)S(1)} %get-tuple-element.105), channel_id=1, replica_groups=mesh['grp'=2,'rows'=8,'cols'=2] {'rows','cols'}, use_global_device_ids=true, to_apply=%region_13.14 | all-reduce | flops 2048 | bytes 16384 | tf_op jit(solution)/shard_map/psum | solution.py:165
  165.5 3.9 %fusion.30 = bf16[16,8,8,8,64]{4,3,2,0,1:T(8,128)(2,1)} fusion(f32[8,16,8,8,64]{4,3,2,1,0:T(8,128)} %reshape.188, f32[8,16,8,8]{3,2,1,0:T(8,128)} %bitcast.109), kind=kLoop, calls=%fused_computation.42 | loop fusion | flops 1048576 | bytes 3178496 | tf_op jit(solution)/shard_map/while/body/eval_jaxpr/transpose | solution.py:48
  169.4 26.6 %all-reduce.2.cloned.1.call-done = f32[8,256,64]{1,2,0:T(8,128)} async-done(((f32[8,256,64]{1,2,0:T(8,128)}), f32[8,256,64]{1,2,0:T(8,128)}) %all-reduce.2.cloned.1.call-update) | async-done | bytes 524304 | tf_op jit(solution)/shard_map/psum | solution.py:165
  198.1 2.4 collective-permute-start.2
  203.7 3.6 %pad_maximum_fusion = bf16[14,134,1024]{2,1,0:T(8,128)(2,1)S(1)} fusion(bf16[14,3,1024]{2,1,0:T(4,128)(2,1)S(1)} %collective-permute-done.3, bf16[3,128,1024]{2,1,0:T(8,128)(2,1)} %collective-permute-done.1, bf16[8,128,512]{2,1,0:T(8,128)(2,1)S(1)} %slice.51, bf16[8,128,512]{2,1,0:T(8,128)(2,1)S(1)} %multiply_convert_fusion.2, ...), kind=kLoop, calls=%fused_computation.34 | loop fusion | flops 23052288 | bytes 7684096 | tf_op jit(solution)/shard_map/concatenate | solution.py:22
  208.9 5.6 %reshape.190 = bf16[14,134,8,64]{3,2,1,0:T(8,128)(2,1)} reshape(bf16[14,134,512]{2,1,0:T(8,128)(2,1)} %get-tuple-element.114) | data formatting | bytes 3842048 | tf_op jit(solution)/shard_map/reshape | solution.py:118
  214.5 7.1 %gather_fusion.2 = bf16[224,14,8,64]{3,2,1,0:T(8,128)(2,1)} fusion(bf16[14,134,8,64]{3,2,1,0:T(8,128)(2,1)} %reshape.190, s32[1024]{0:T(1024)S(1)} %pad_clamp_fusion), kind=kCustom, calls=%fused_computation.2 | custom fusion | bytes 6423424 | tf_op jit(solution)/shard_map/while/body/eval_jaxpr/gather | solution.py:51
  221.5 6.6 %copy.46 = bf16[16,14,14,8,64]{4,3,1,2,0:T(8,128)(2,1)} copy(bf16[16,14,14,8,64]{4,3,2,1,0:T(8,128)(2,1)} %bitcast.104) | data formatting | bytes 6422528 | tf_op jit(solution)/shard_map/while/body/eval_jaxpr/gather | solution.py:51
  228.2 3.3 %reshape.186 = bf16[14,134,8,64]{3,2,1,0:T(8,128)(2,1)} reshape(bf16[14,134,512]{2,1,0:T(8,128)(2,1)S(1)} %get-tuple-element.113) | data formatting | bytes 3842048 | tf_op jit(solution)/shard_map/reshape | solution.py:121
  231.5 7.0 %gather_fusion = bf16[224,14,8,64]{3,2,1,0:T(8,128)(2,1)} fusion(bf16[14,134,8,64]{3,2,1,0:T(8,128)(2,1)} %reshape.186, s32[1024]{0:T(1024)S(1)} %pad_clamp_fusion), kind=kCustom, calls=%fused_computation | custom fusion | bytes 6423424 | tf_op jit(solution)/shard_map/while/body/eval_jaxpr/gather | solution.py:55
  238.5 6.8 %copy.40 = bf16[16,14,14,8,64]{4,3,1,2,0:T(8,128)(2,1)} copy(bf16[16,14,14,8,64]{4,3,2,1,0:T(8,128)(2,1)} %bitcast.103) | data formatting | bytes 6422528 | tf_op jit(solution)/shard_map/while/body/eval_jaxpr/gather | solution.py:55
  245.3 6.5 %fusion.13 = (f32[16,8,64]{2,1,0:T(8,128)S(1)}, f32[16,8,64,196]{3,2,1,0:T(8,128)S(1)}) fusion(f32[8]{0:T(128)S(1)} %get-tuple-element.217, pred[16,196]{1,0:T(8,128)(4,1)S(1)} %broadcast_in_dim.60, bf16[16,196,8,64]{3,2,1,0:T(8,128)(2,1)} %bitcast.106, bf16[16,8,8,8,64]{4,3,2,0,1:T(8,128)(2,1)S(1)} %copy-done.4), kind=kOutput, calls=%fused_computation.20 | convolution fusion | flops 210329600 | bytes 10718304 | tf_op jit(solution)/shard_map/while/body/eval_jaxpr/bqhd,bkhd->bhqk/dot_general | solution.py:61
  251.8 3.7 %fusion.18 = f32[16,8,64]{2,1,0:T(8,128)S(1)} fusion(f32[16,8,64,196]{3,2,1,0:T(8,128)S(1)} %get-tuple-element.122, f32[16,8,64]{2,1,0:T(8,128)S(1)} %get-tuple-element.121, f32[8]{0:T(128)S(1)} %get-tuple-element.217, pred[16,196]{1,0:T(8,128)(4,1)S(1)} %broadcast_in_dim.60), kind=kLoop, calls=%fused_computation.25 | loop fusion | flops 6414336 | bytes 6491232 | tf_op jit(solution)/shard_map/while/body/eval_jaxpr/reduce_sum | solution.py:68
  255.5 6.0 %fusion.21 = bf16[16,64,8,64]{1,3,2,0:T(8,128)(2,1)} fusion(f32[16,64,8]{1,2,0:T(8,128)S(1)} %bitcast.114, f32[16,8,64,196]{3,2,1,0:T(8,128)S(1)} %get-tuple-element.122, f32[16,8,64]{2,1,0:T(8,128)S(1)} %get-tuple-element.121, f32[8]{0:T(128)S(1)} %get-tuple-element.217, pred[16,196]{1,0:T(8,128)(4,1)S(1)} %broadcast_in_dim.60, ...), kind=kOutput, calls=%fused_computation.28 | convolution fusion | flops 212992000 | bytes 10751072 | tf_op jit(solution)/shard_map/while/body/eval_jaxpr/bhqk,bkhd->bqhd/dot_general | solution.py:70
  261.5 4.3 %copy.49 = bf16[16,64,8,64]{3,2,1,0:T(8,128)(2,1)} copy(bf16[16,64,8,64]{1,3,2,0:T(8,128)(2,1)} %fusion.21) | data formatting | bytes 2097152 | tf_op jit(solution)/shard_map/while/body/eval_jaxpr/convert_element_type | solution.py:77
  265.8 3.2 %convert_element_type.79 = bf16[16,8,8,512]{3,2,1,0:T(8,128)(2,1)S(1)} reshape(bf16[16,64,8,64]{3,2,1,0:T(8,128)(2,1)} %copy.49) | data formatting | bytes 2097152 | tf_op jit(solution)/shard_map/while/body/eval_jaxpr/convert_element_type | solution.py:77
  269.0 2.9 %fusion.29 = bf16[8,128,512]{2,1,0:T(8,128)(2,1)} fusion(bf16[8,128,512]{2,1,0:T(8,128)(2,1)} %param.11, bf16[512,512]{1,0:T(8,128)(2,1)S(1)} %copy-done.9, bf16[16,8,8,512]{3,2,1,0:T(8,128)(2,1)S(1)} %convert_element_type.79), kind=kOutput, calls=%fused_computation.41 | convolution fusion | flops 538443776 | bytes 3670016 | tf_op jit(solution)/shard_map/dot_general | solution.py:136
  (115 shorter events, 52.1 us)
Async XLA Ops:
  7.2 1.7 copy-start
  7.2 188.8 %all-reduce.2.cloned.1.call-start = ((), (), s32[]{:S(2)}) async-start(), calls=%async_computation | async-start | bytes 1048576 | tf_op jit(solution)/shard_map/psum | solution.py:165
  12.0 5.2 %copy-start.2 = (f32[8,128,1536]{2,1,0:T(8,128)}, f32[8,128,1536]{2,1,0:T(8,128)S(1)}, u32[]{:S(2)}) copy-start(f32[8,128,1536]{2,1,0:T(8,128)S(1)} %fusion.33) | copy-start | bytes 18874372
  25.1 4.8 %copy-start.10 = (f32[8]{0:T(128)S(1)}, f32[8]{0:T(128)}, u32[]{:S(2)}) copy-start(f32[8]{0:T(128)} %param.19) | copy-start | bytes 100
  25.1 4.8 %copy-start.5 = (bf16[256,512]{1,0:T(8,128)(2,1)S(1)}, bf16[256,512]{1,0:T(8,128)(2,1)}, u32[]{:S(2)}) copy-start(bf16[256,512]{1,0:T(8,128)(2,1)} %param.15) | copy-start | bytes 786436
  25.1 5.0 %copy-start.6 = (bf16[512,512]{1,0:T(8,128)(2,1)S(1)}, bf16[512,512]{1,0:T(8,128)(2,1)}, u32[]{:S(2)}) copy-start(bf16[512,512]{1,0:T(8,128)(2,1)} %param.17) | copy-start | bytes 1572868
  25.1 5.0 %copy-start.8 = (f32[512]{0:T(512)S(1)}, f32[512]{0:T(512)}, u32[]{:S(2)}) copy-start(f32[512]{0:T(512)} %param.16) | copy-start | bytes 6148
  110.2 86.9 %collective-permute-start = (bf16[3,128,1024]{2,1,0:T(8,128)(2,1)}, bf16[3,128,1024]{2,1,0:T(8,128)(2,1)S(1)}, u32[]{:S(2)}, u32[]{:S(2)}) collective-permute-start(bf16[3,128,1024]{2,1,0:T(8,128)(2,1)} %get-tuple-element.117), channel_id=1, source_target_pairs={{0,2},{2,4},{4,6},{6,8},{8,10},{10,12},{12,14},{1,3},{3,5},{5,7},{... | collective-permute-start | bytes 2359304 | tf_op jit(solution)/shard_map/ppermute | solution.py:20
  111.6 85.6 %collective-permute-start.1 = (bf16[3,128,1024]{2,1,0:T(8,128)(2,1)}, bf16[3,128,1024]{2,1,0:T(8,128)(2,1)}, u32[]{:S(2)}, u32[]{:S(2)}) collective-permute-start(bf16[3,128,1024]{2,1,0:T(8,128)(2,1)} %get-tuple-element.118), channel_id=1, source_target_pairs={{2,0},{4,2},{6,4},{8,6},{10,8},{12,10},{14,12},{3,1},{5,3},{7,5},{... | collective-permute-start | bytes 2359304 | tf_op jit(solution)/shard_map/ppermute | solution.py:21
  196.0 6.0 %copy-start.7 = (bf16[512,512]{1,0:T(8,128)(2,1)S(1)}, bf16[512,512]{1,0:T(8,128)(2,1)}, u32[]{:S(2)}) copy-start(bf16[512,512]{1,0:T(8,128)(2,1)} %param.18) | copy-start | bytes 1572868
  198.1 4.9 %collective-permute-start.2 = (bf16[14,3,1024]{2,1,0:T(4,128)(2,1)S(1)}, bf16[14,3,1024]{2,1,0:T(4,128)(2,1)S(1)}, u32[]{:S(2)}, u32[]{:S(2)}) collective-permute-start(bf16[14,3,1024]{2,1,0:T(4,128)(2,1)S(1)} %get-tuple-element.115), channel_id=1, source_target_pairs={{0,1},{2,3},{4,5},{6,7},{8,9},{10,11},{12,13},{14,15},{16,17},{18,... | collective-permute-start | bytes 258056 | tf_op jit(solution)/shard_map/ppermute | solution.py:20
  200.4 3.2 %collective-permute-start.3 = (bf16[14,3,1024]{2,1,0:T(4,128)(2,1)S(1)}, bf16[14,3,1024]{2,1,0:T(4,128)(2,1)S(1)}, u32[]{:S(2)}, u32[]{:S(2)}) collective-permute-start(bf16[14,3,1024]{2,1,0:T(4,128)(2,1)S(1)} %get-tuple-element.116), channel_id=1, source_target_pairs={{1,0},{3,2},{5,4},{7,6},{9,8},{11,10},{13,12},{15,14},{17,16},{19,... | collective-permute-start | bytes 258056 | tf_op jit(solution)/shard_map/ppermute | solution.py:21
  238.5 6.8 %copy-start.4 = (bf16[16,8,8,8,64]{4,3,2,0,1:T(8,128)(2,1)S(1)}, bf16[16,8,8,8,64]{4,3,2,0,1:T(8,128)(2,1)}, u32[]{:S(2)}) copy-start(bf16[16,8,8,8,64]{4,3,2,0,1:T(8,128)(2,1)} %fusion.30) | copy-start | bytes 3145732
  251.8 3.7 %copy-start.3 = (bf16[16,14,14,8,64]{4,3,1,2,0:T(8,128)(2,1)S(1)}, bf16[16,14,14,8,64]{4,3,1,2,0:T(8,128)(2,1)}, u32[]{:S(2)}) copy-start(bf16[16,14,14,8,64]{4,3,1,2,0:T(8,128)(2,1)} %copy.40) | copy-start | bytes 9633796
  261.5 7.5 %copy-start.9 = (bf16[512,512]{1,0:T(8,128)(2,1)S(1)}, bf16[512,512]{1,0:T(8,128)(2,1)}, u32[]{:S(2)}) copy-start(bf16[512,512]{1,0:T(8,128)(2,1)} %param.14) | copy-start | bytes 1572868
  261.5 10.4 %copy-start.1 = (bf16[512,1536]{1,0:T(8,128)(2,1)S(1)}, bf16[512,1536]{1,0:T(8,128)(2,1)}, u32[]{:S(2)}) copy-start(bf16[512,1536]{1,0:T(8,128)(2,1)} %param.13) | copy-start | bytes 4718596
Sparse Core Ops, SparseCore 0:
  102.0 93.8 all-reduce.1
where the time goes:
time: 280 us; the launch traced here: 279 us
  local copies, waits for them, and re-layouts  77.1 us (28%)
  blocking collectives  76.4 us (27%)
  matrix products  43.6 us (16%)
  other arithmetic  33.2 us (12%)
  waiting for transfers between devices  27.3 us (10%)
  between operations  14.4 us (5%)
  starting transfers between devices  6.5 us (2%)
    psum x1, blocking collectives, per_device(): lax.psum((local_total * factor, local_sum * factor[..., None]), ('rows',...  40.9 us
    pmax x1, blocking collectives, per_device(): crop_peak = lax.pmax(local_peak, ('rows', 'cols'))  35.4 us
    psum x1, waiting for transfers between devices, per_device(): lax.psum((local_total * factor, local_sum * factor[..., None]), ('rows',...  26.6 us
    dot_general x8, matrix products, one_head(): jnp.dot(expo.astype(jnp.bfloat16), value_head, preferred_element_type=jnp...  15.1 us
    gather x2, local copies, waits for them, and re-layouts, one_row(): value_slab = values_ext[:, offsets]  13.8 us
    gather x2, local copies, waits for them, and re-layouts, one_row(): key_slab = keys_ext[:, offsets]  13.7 us
    dot_general x8, matrix products, one_head(): jnp.dot(query_head, key_head.T, preferred_element_type=jnp.float32)  8.53 us
    convert_element_type x2, local copies, waits for them, and re-layouts, one_row(): output.reshape(BLK, cols_all, head_count * channels_per_branch)  7.46 us
  transfers between devices with their start and end apart: 5, of which 2 were waited for; matrix products, arithmetic and copies ran while one was open for 9% of the time, Pallas kernels for 0%

commit v1 on v0

v1 whole, which is shorter than its diff:
```python
import math

import jax
import jax.numpy as jnp
from jax import lax
from jax.experimental import pallas as pl
from jax.experimental.pallas import tpu as pltpu
from jax.sharding import PartitionSpec as P

H = 8
BLK = 8
RIM = 3
LOG2E = math.log2(math.e)
F32 = jnp.float32
BF16 = jnp.bfloat16
NEG = -1e30
VMEM = pl.BlockSpec(memory_space=pltpu.VMEM)
SMEM = pl.BlockSpec(memory_space=pltpu.SMEM)
CONTRACT_LAST = (((1,), (1,)), ((), ()))


def dot(a, b):
    return jnp.dot(a, b, preferred_element_type=F32)


def token_norm(floats, gain):
    scaled = floats * lax.rsqrt(jnp.mean(floats * floats, axis=-1, keepdims=True) + 1e-05)
    return (scaled * gain).astype(BF16)


def head_ones(width, channels):
    a = lax.broadcasted_iota(jnp.int32, (width, width), 0) // channels
    b = lax.broadcasted_iota(jnp.int32, (width, width), 1) // channels
    return jnp.where(a == b, 1.0, 0.0).astype(BF16)


def head_norm(floats, ones, channels):
    squares = floats * floats
    high = squares.astype(BF16)
    low = (squares - high.astype(F32)).astype(BF16)
    width = ones.shape[0]
    sums = [
        dot(high[:, i : i + width], ones) + dot(low[:, i : i + width], ones)
        for i in range(0, floats.shape[1], width)
    ]
    mean = jnp.concatenate(sums, axis=1) * (1.0 / channels)
    return floats * lax.rsqrt(mean + 1e-06)


def spread(heads, width, first):
    a = lax.broadcasted_iota(jnp.int32, (128, width), 0)
    b = lax.broadcasted_iota(jnp.int32, (128, width), 1) // (width // heads)
    return jnp.where(a == b + first, 1.0, 0.0).astype(BF16)


def gathered(heads, width, first):
    a = lax.broadcasted_iota(jnp.int32, (width, 128), 0)
    b = lax.broadcasted_iota(jnp.int32, (width, 128), 1) - first
    return jnp.where((a == b * (width // heads)) & (b >= 0) & (b < heads), 1.0, 0.0).astype(BF16)


def latent_kernel(
    scale, place, x, gain, weights, slots, slot_gain, asking, keys, values, mine, other
):
    rows, cols, width = x.shape
    heads = H
    channels = width // heads
    latents = slots.shape[0]
    ones = head_ones(256, channels)
    for i in range(rows // 2):
        tokens = x[2 * i : 2 * i + 2].reshape(2 * cols, width).astype(F32)
        normed = token_norm(tokens, gain[...])
        both = dot(normed, weights[:, width:])
        here = slice(2 * i * cols, (2 * i + 2) * cols)
        keys[here, :] = head_norm(both[:, :width], ones, channels).astype(BF16)
        values[here, :] = both[:, width:].astype(BF16)
    slot_normed = token_norm(slots[...].astype(F32), slot_gain[...])
    asked = head_norm(dot(slot_normed, asking[...]), ones, channels).astype(BF16)
    half = latents // 2
    first = place[4] == 0
    lanes = lax.broadcasted_iota(jnp.int32, (1, 128), 1)
    peaks = jnp.zeros((latents, 128), F32)
    totals = jnp.zeros((latents, 128), F32)
    per = 128 // channels
    for pair in range(heads // per):
        at = slice(pair * 128, (pair + 1) * 128)
        out = jnp.zeros((latents, 128), F32)
        for inner in range(per):
            head = pair * per + inner
            own = (lanes // channels) == inner
            query = asked[:, at] * jnp.where(own, 1.0, 0.0).astype(BF16)
            scores = lax.dot_general(query, keys[:, at], CONTRACT_LAST, preferred_element_type=F32)
            scores = scores * (scale[head] * LOG2E)
            peak = jnp.max(scores, axis=-1, keepdims=True)
            peak = (jnp.ceil(peak * 0.5) * 2.0).astype(BF16).astype(F32)
            expo = jnp.exp2(scores - peak)
            total = jnp.sum(expo, axis=-1, keepdims=True)
            out = jnp.where(own, dot(expo.astype(BF16), values[:, at]), out)
            peaks = jnp.where(lanes == head, peak, peaks)
            totals = jnp.where(lanes == head, total, totals)
        out = out.astype(BF16)
        mine[:, at] = jnp.where(first, out[:half], out[half:])
        other[:, at] = jnp.where(first, out[half:], out[:half])
    high = totals.astype(BF16).astype(F32)
    low = totals - high
    meta = peaks + pltpu.roll(high, heads, 1) + pltpu.roll(low, 2 * heads, 1)
    meta = meta.astype(BF16)
    mine[:, width:] = jnp.where(first, meta[:half], meta[half:])
    other[:, width:] = jnp.where(first, meta[half:], meta[:half])


def opened(part, width):
    meta = part[:, width:]
    peak = dot(meta, spread(H, width, 0))
    total = dot(meta, spread(H, width, H) + spread(H, width, 2 * H))
    return (part[:, :width].astype(F32), peak, total)


def joined(parts, width):
    items = [opened(p, width) for p in parts]
    peak = items[0][1]
    for item in items[1:]:
        peak = jnp.maximum(peak, item[1])
    out, total = (0.0, 0.0)
    for o, m, t in items:
        factor = jnp.exp2(m - peak)
        out = out + o * factor
        total = total + t * factor
    return (out, peak, total)


def join_kernel(a, b, result):
    width = result.shape[1] - 128
    out, peak, total = joined([a[...], b[...]], width)
    result[:, :width] = out.astype(BF16)
    high = total.astype(BF16)
    low = (total - high.astype(F32)).astype(BF16)
    meta = (
        dot(peak.astype(BF16), gathered(H, width, 0))
        + dot(high, gathered(H, width, H))
        + dot(low, gathered(H, width, 2 * H))
    )
    result[:, width:] = meta.astype(BF16)


def last_kernel(a, b, exits, result):
    width = result.shape[1]
    out, _, total = joined([a[...], b[...]], width)
    result[...] = dot((out / total).astype(BF16), exits[...]).astype(BF16)


def windows(tokens, side):
    cols, width = tokens.shape
    own = tokens.reshape(cols // BLK, BLK, width)
    side = side.reshape(1, BLK, width)
    after = jnp.concatenate([own[1:], side], axis=0)
    before = jnp.concatenate([side, own[:-1]], axis=0)
    place = lax.broadcasted_iota(jnp.int32, own.shape, 1)
    rim = jnp.where(place < BLK // 2, after, before)
    return jnp.concatenate([own, rim], axis=1).astype(BF16)


def own_kernel(x, side, gain, weights, keys, values, queries, key_win, value_win):
    rows, cols, width = x.shape
    channels = width // H
    ones = head_ones(256, channels)
    beside = token_norm(side[...].reshape(rows * BLK, width).astype(F32), gain[...])
    both = dot(beside, weights[:, width:])
    side_keys = head_norm(both[:, :width], ones, channels)
    side_values = both[:, width:]
    for i in range(rows // 2):
        tokens = x[2 * i : 2 * i + 2].reshape(2 * cols, width).astype(F32)
        normed = token_norm(tokens, gain[...])
        query = head_norm(dot(normed, weights[:, :width]), ones, channels)
        query = query.reshape(2, cols // BLK, BLK, width).transpose(1, 0, 2, 3)
        queries[:, 16 * i : 16 * i + 16, :] = query.reshape(cols // BLK, 16, width).astype(BF16)
    for r in range(rows):
        here = slice(r * cols, (r + 1) * cols)
        at = slice(r * BLK, (r + 1) * BLK)
        key_win[r] = windows(keys[here, :].astype(F32), side_keys[at])
        value_win[r] = windows(values[here, :].astype(F32), side_values[at])


def halo_kernel(
    scale,
    place,
    x,
    up,
    down,
    up_side,
    down_side,
    gain,
    weights,
    exits,
    queries,
    key_win,
    value_win,
    tokens_out,
    key_rim,
    value_rim,
    attended,
):
    rows, cols, width = x.shape
    channels = width // H
    ones = head_ones(256, channels)
    blocks = cols // BLK
    lines = rows + 2 * RIM

    corner = jnp.concatenate([up_side[...], down_side[...]], axis=0)
    beside = token_norm(corner.reshape(2 * RIM * BLK, width).astype(F32), gain[...])
    both = dot(beside, weights[:, width:])
    side_keys = head_norm(both[:, :width], ones, channels)
    side_values = both[:, width:]
    for n, ref in enumerate((up, down)):
        for r in range(RIM):
            normed = token_norm(ref[r].astype(F32), gain[...])
            both = dot(normed, weights[:, width:])
            line = n * RIM + r
            at = slice(line * BLK, (line + 1) * BLK)
            key_rim[line] = windows(head_norm(both[:, :width], ones, channels), side_keys[at])
            value_rim[line] = windows(both[:, width:], side_values[at])

    spot = lax.broadcasted_iota(jnp.int32, (1, lines * 16), 1)
    line, sub = (spot // 16, spot % 16)
    upper = (line >= rows) & (line < rows + RIM)
    lower = line >= rows + RIM
    fixed = (sub == BLK + RIM) | (sub == BLK + RIM + 1)
    fixed = fixed | (upper & (place[0] == 0)) | (lower & (place[1] == 0))
    right = (sub >= BLK) & (sub < BLK + RIM)
    left = sub >= 2 * BLK - RIM
    group = 256
    per = group // channels
    owner = lax.broadcasted_iota(jnp.int32, (1, group), 1) // channels

    def one_block(block):
        gone = fixed | (right & ((place[3] == 0) & (block == blocks - 1)))
        gone = gone | (left & ((place[2] == 0) & (block == 0)))
        bias = jnp.where(gone, NEG, 0.0)
        outs = []
        for g in range(width // group):
            at = slice(g * group, (g + 1) * group)
            query = queries[block, :, at]
            stacked = jnp.concatenate(
                [query * jnp.where(owner == h, 1.0, 0.0).astype(BF16) for h in range(per)], axis=0
            )
            key = jnp.concatenate(
                [
                    key_win[:, block, :, at].reshape(rows * 16, group),
                    key_rim[:, block, :, at].reshape(2 * RIM * 16, group),
                ],
                axis=0,
            )
            value = jnp.concatenate(
                [
                    value_win[:, block, :, at].reshape(rows * 16, group),
                    value_rim[:, block, :, at].reshape(2 * RIM * 16, group),
                ],
                axis=0,
            )
            scores = lax.dot_general(stacked, key, CONTRACT_LAST, preferred_element_type=F32)
            expos, totals = ([], [])
            n = BLK * BLK
            for h in range(per):
                s = scores[h * n : (h + 1) * n] * (scale[g * per + h] * LOG2E) + bias
                expo = jnp.exp2(s - jnp.max(s, axis=-1, keepdims=True))
                totals.append(jnp.sum(expo, axis=-1, keepdims=True))
                expos.append(expo.astype(BF16))
            mixed = dot(jnp.concatenate(expos, axis=0), value)
            out = jnp.zeros((n, group), F32)
            for h in range(per):
                out = jnp.where(owner == h, mixed[h * n : (h + 1) * n] / totals[h], out)
            outs.append(out)
        return jnp.concatenate(outs, axis=1).reshape(BLK, BLK, width)

    def two_blocks(i, carry):
        pair = jnp.concatenate([one_block(2 * i), one_block(2 * i + 1)], axis=1)
        attended[:, pl.ds(pl.multiple_of(i * 16, 16), 16), :] = pair.astype(BF16)
        return carry

    lax.fori_loop(0, blocks // 2, two_blocks, 0)
    for i in range(rows // 2):
        here = slice(2 * i, 2 * i + 2)
        branch = dot(attended[here].reshape(2 * cols, width), exits[...])
        tokens_out[here] = (x[here].astype(F32) + branch.reshape(2, cols, width)).astype(BF16)


def call(kernel, outs, ins, scratch=(), flops=0, smem=0):
    shapes = [jax.ShapeDtypeStruct(*o) for o in outs]
    moved = sum(math.prod(s.shape) * s.dtype.itemsize for s in shapes + list(ins))
    return pl.pallas_call(
        kernel,
        out_shape=shapes,
        in_specs=[SMEM] * smem + [VMEM] * (len(ins) - smem),
        out_specs=[VMEM] * len(shapes),
        scratch_shapes=list(scratch),
        compiler_params=pltpu.CompilerParams(vmem_limit_bytes=48 * 1024 * 1024),
        cost_estimate=pl.CostEstimate(flops=flops, bytes_accessed=moved, transcendentals=0),
    )(*ins)


def per_device(
    crop_feature_grid,
    pixel_layernorm_gain,
    triple_projection_matrix,
    halo_exit_matrix,
    memory_slots,
    memory_layernorm_gain,
    memory_asking_matrix,
    memory_exit_matrix,
    branch_logit_multiplier,
):
    x = crop_feature_grid
    rows, cols, width = x.shape
    latents = memory_slots.shape[0]
    tall, wide = (lax.axis_size("rows"), lax.axis_size("cols"))
    row, col = (lax.axis_index("rows"), lax.axis_index("cols"))
    place = jnp.stack([row > 0, row < tall - 1, col > 0, col < wide - 1, col > 0])
    place = place.astype(jnp.int32)
    scale = branch_logit_multiplier / math.sqrt(width // H)
    gain = pixel_layernorm_gain.reshape(1, width)
    slot_gain = memory_layernorm_gain.reshape(1, width)

    downward = [(i, i + 1) for i in range(tall - 1)]
    upward = [(i + 1, i) for i in range(tall - 1)]
    swap = [(0, 1), (1, 0)]
    edge = jnp.where(col == 0, x[:, cols - BLK :], x[:, :BLK])
    up = lax.ppermute(x[rows - RIM :], "rows", downward)
    down = lax.ppermute(x[:RIM], "rows", upward)
    side = lax.ppermute(edge, "cols", swap)
    across = [(i * 2 + c, j * 2 + 1 - c) for i, j in downward for c in range(2)]
    back = [(j, i) for i, j in across]
    up_side = lax.ppermute(edge[rows - RIM :], ("rows", "cols"), across)
    down_side = lax.ppermute(edge[:RIM], ("rows", "cols"), back)

    half = latents // 2
    tokens = rows * cols
    keys, values, mine, other = call(
        latent_kernel,
        [
            ((tokens, width), BF16),
            ((tokens, width), BF16),
            ((half, width + 128), BF16),
            ((half, width + 128), BF16),
        ],
        (
            scale,
            place,
            x,
            gain,
            triple_projection_matrix,
            memory_slots,
            slot_gain,
            memory_asking_matrix,
        ),
        flops=4 * 10**9,
        smem=2,
    )
    parts = [mine, lax.ppermute(other, "cols", swap)]
    step = 1
    while step < tall:
        pairs = [(i, i ^ step) for i in range(tall)]
        (whole,) = call(join_kernel, [((half, width + 128), BF16)], parts, flops=10**8)
        parts = [whole, lax.ppermute(whole, "rows", pairs)]
        step *= 2
    (mixed,) = call(
        last_kernel, [((half, width), BF16)], (*parts, memory_exit_matrix), flops=10**8
    )
    theirs = lax.ppermute(mixed, "cols", swap)
    latent_mix = jnp.where(
        col == 0, jnp.concatenate([mixed, theirs]), jnp.concatenate([theirs, mixed])
    )

    blocks = cols // BLK
    queries, key_win, value_win = call(
        own_kernel,
        [
            ((blocks, rows * BLK, width), BF16),
            ((rows, blocks, 16, width), BF16),
            ((rows, blocks, 16, width), BF16),
        ],
        (x, side, gain, triple_projection_matrix, keys, values),
        flops=2 * 10**9,
    )
    (tokens_out,) = call(
        halo_kernel,
        [(x.shape, BF16)],
        (
            scale,
            place,
            x,
            up,
            down,
            up_side,
            down_side,
            gain,
            triple_projection_matrix,
            halo_exit_matrix,
            queries,
            key_win,
            value_win,
        ),
        scratch=[
            pltpu.VMEM((2 * RIM, blocks, 16, width), BF16),
            pltpu.VMEM((2 * RIM, blocks, 16, width), BF16),
            pltpu.VMEM((rows, cols, width), BF16),
        ],
        flops=6 * 10**9,
        smem=2,
    )
    return (tokens_out, latent_mix)


def solution(mesh):
    return jax.shard_map(
        per_device,
        mesh=mesh,
        in_specs=(P(("grp", "rows"), "cols", None), P(), P(), P(), P(), P(), P(), P(), P()),
        out_specs=(P(("grp", "rows"), "cols", None), P("grp", None)),
        check_vma=False,
    )
```

time: 280 us -> 68 us (0.24)
  blocking collectives: 76.4 us -> 0 us
  local copies, waits for them, and re-layouts: 77.1 us -> 9.37 us
  matrix products: 43.6 us -> 0 us
  other arithmetic: 33.2 us -> 1.44 us
  Pallas kernels: 0 us -> 25.4 us
  between operations: 14.4 us -> 0.8 us
  waiting for transfers between devices: 27.3 us -> 13.8 us
  starting transfers between devices: 6.5 us -> 16.8 us
    dot_general x22 -> x0, matrix products: 43.6 us -> none  [the longest x8 15.1 us: one_head(): jnp.dot(expo.astype(jnp.bfloat16), value_head, preferred_element_type=jnp...]
    psum x1 -> x0, blocking collectives: 40.9 us -> none  [per_device(): lax.psum((local_total * factor, local_sum * factor[..., None]), ('rows',...]
    pmax x1 -> x0, blocking collectives: 35.4 us -> none  [per_device(): crop_peak = lax.pmax(local_peak, ('rows', 'cols'))]
    gather x7 -> x0, local copies, waits for them, and re-layouts: 28.4 us -> none  [the longest x2 13.8 us: one_row(): value_slab = values_ext[:, offsets]]
    psum x1 -> x0, waiting for transfers between devices: 26.6 us -> none  [per_device(): lax.psum((local_total * factor, local_sum * factor[..., None]), ('rows',...]
    pallas_call x0 -> x7, Pallas kernels: none -> 25.4 us  [call(): pl.pallas_call(kernel, out_shape=shapes, in_specs=[SMEM] * smem + [VMEM]...]
    reshape x4 -> x0, local copies, waits for them, and re-layouts: 16.1 us -> none  [the longest x2 7.15 us: head_norm(): floats.reshape(floats.shape[:-1] + (head_count, floats.shape[-1] // head_...]
    ppermute x4 -> x10, waiting for transfers between devices: 0.7 us -> 13.8 us  [the longest x3 12.9 us: per_device(): parts = [whole, lax.ppermute(whole, 'rows', pairs)]]
  transfers between devices with their start and end apart: 5 -> 10, of which waited for: 2 -> 4; matrix products, arithmetic and copies ran while one was open for 9% -> 0% of each run, Pallas kernels for 0% -> 27%
where the time goes in v1:
time: 68 us; the launch traced here: 67.5 us
  Pallas kernels  25.4 us (37%)
  starting transfers between devices  16.8 us (25%)
  waiting for transfers between devices  13.8 us (20%)
  local copies, waits for them, and re-layouts  9.37 us (14%)
  other arithmetic  1.44 us (2%)
  between operations  0.8 us (1%)
    pallas_call x7, Pallas kernels, call(): pl.pallas_call(kernel, out_shape=shapes, in_specs=[SMEM] * smem + [VMEM]...  25.4 us
    ppermute x3, waiting for transfers between devices, per_device(): parts = [whole, lax.ppermute(whole, 'rows', pairs)]  12.9 us
    ppermute x3, starting transfers between devices, per_device(): parts = [whole, lax.ppermute(whole, 'rows', pairs)]  10.1 us
    unnamed x30, local copies, waits for them, and re-layouts  9.2 us
    ppermute x1, starting transfers between devices, per_device(): up = lax.ppermute(x[rows - RIM:], 'rows', downward)  1.95 us
    ppermute x1, starting transfers between devices, per_device(): down_side = lax.ppermute(edge[:RIM], ('rows', 'cols'), back)  1.46 us
  transfers between devices with their start and end apart: 10, of which 4 were waited for; matrix products, arithmetic and copies ran while one was open for 0% of the time, Pallas kernels for 27%

profile of v1, /device:TPU:0, one launch (start us, length us, event | category | flops | bytes accessed | tf_op | source)
XLA Modules:
  0.0 67.5 jit_solution(17103408112852064090)
XLA Ops:
  0.6 0.1 stack.20
  0.8 0.7 broadcast_multiply_fusion.scale
  1.4 1.2 %copy-done = bf16[8,128,512]{2,1,0:T(8,128)(2,1)S(1)} copy-done((bf16[8,128,512]{2,1,0:T(8,128)(2,1)S(1)}, bf16[8,128,512]{2,1,0:T(8,128)(2,1)}, u32[]{:S(2)}) %copy-start) | copy-done | bytes 1048600
  2.6 1.4 %copy-done.3 = bf16[512,1536]{1,0:T(8,128)(2,1)S(1)} copy-done((bf16[512,1536]{1,0:T(8,128)(2,1)S(1)}, bf16[512,1536]{1,0:T(8,128)(2,1)}, u32[]{:S(2)}) %copy-start.3) | copy-done | bytes 1572888
  4.0 1.0 %copy-done.5 = bf16[512,512]{1,0:T(8,128)(2,1)S(1)} copy-done((bf16[512,512]{1,0:T(8,128)(2,1)S(1)}, bf16[512,512]{1,0:T(8,128)(2,1)}, u32[]{:S(2)}) %copy-start.5) | copy-done | bytes 524312
  5.1 0.9 %copy-done.7 = bf16[256,512]{1,0:T(8,128)(2,1)S(1)} copy-done((bf16[256,512]{1,0:T(8,128)(2,1)S(1)}, bf16[256,512]{1,0:T(8,128)(2,1)}, u32[]{:S(2)}) %copy-start.7) | copy-done | bytes 262168
  6.0 0.7 %copy-done.8 = f32[512]{0:T(512)S(1)} copy-done((f32[512]{0:T(512)S(1)}, f32[512]{0:T(512)}, u32[]{:S(2)}) %copy-start.8) | copy-done | bytes 2072
  6.7 0.7 %copy-done.9 = f32[512]{0:T(512)S(1)} copy-done((f32[512]{0:T(512)S(1)}, f32[512]{0:T(512)}, u32[]{:S(2)}) %copy-start.9) | copy-done | bytes 2072
  7.4 6.8 %shard_map.104 = (bf16[1024,512]{1,0:T(8,128)(2,1)S(1)}, bf16[1024,512]{1,0:T(8,128)(2,1)S(1)}, bf16[128,640]{1,0:T(8,128)(2,1)S(1)}, bf16[128,640]{1,0:T(8,128)(2,1)S(1)}) custom-call(f32[8]{0:T(128)S(1)} %broadcast_multiply_fusion.scale, s32[5]{0:T(128)S(1)} %convert_element_type.3.place, bf16[8,128,512]{2,1,0:T(8,128)(2,1)S(1)} %copy-done, ...), custom_call_target="tpu_custom_call" | custom-call | flops 4000000000 | bytes 5836852 | tf_op jit(solution)/shard_map/pallas_call | solution.py:290
  14.2 1.0 %copy-done.11 = bf16[1024,512]{1,0:T(8,128)(2,1)} copy-done((bf16[1024,512]{1,0:T(8,128)(2,1)}, bf16[1024,512]{1,0:T(8,128)(2,1)S(1)}, u32[]{:S(2)}) %copy-start.11) | copy-done | bytes 1048600
  15.2 1.0 %copy-done.13 = bf16[1024,512]{1,0:T(8,128)(2,1)} copy-done((bf16[1024,512]{1,0:T(8,128)(2,1)}, bf16[1024,512]{1,0:T(8,128)(2,1)S(1)}, u32[]{:S(2)}) %copy-start.13) | copy-done | bytes 1048600
  16.2 0.5 collective-permute-start.5
  16.7 0.1 collective-permute-start.4
  16.8 0.9 %collective-permute-done.5.b = bf16[128,640]{1,0:T(8,128)(2,1)S(1)} collective-permute-done((bf16[128,640]{1,0:T(8,128)(2,1)S(1)}, bf16[128,640]{1,0:T(8,128)(2,1)S(1)}, u32[]{:S(2)}, u32[]{:S(2)}) %collective-permute-start.5) | collective-permute-done | bytes 163872 | tf_op jit(solution)/shard_map/ppermute | solution.py:358
  17.7 0.6 shard_map.107.a
  18.3 2.9 %collective-permute-start.6 = (bf16[128,640]{1,0:T(8,128)(2,1)S(1)}, bf16[128,640]{1,0:T(8,128)(2,1)S(1)}, u32[]{:S(2)}, u32[]{:S(2)}) collective-permute-start(bf16[128,640]{1,0:T(8,128)(2,1)S(1)} %shard_map.107.a), channel_id=1, source_target_pairs={{0,2},{2,0},{4,6},{6,4},{8,10},{10,8},{12,14},{14,12},{1,3},{3,1},... | collective-permute-start | bytes 491528 | tf_op jit(solution)/shard_map/ppermute | solution.py:363
  21.3 1.9 %collective-permute-start = (bf16[3,128,512]{2,1,0:T(8,128)(2,1)S(1)}, bf16[3,128,512]{2,1,0:T(8,128)(2,1)S(1)}, u32[]{:S(2)}, u32[]{:S(2)}) collective-permute-start(bf16[3,128,512]{2,1,0:T(8,128)(2,1)S(1)} %get-tuple-element.17), channel_id=1, source_target_pairs={{0,2},{2,4},{4,6},{6,8},{8,10},{10,12},{12,14},{1,3},{3,5},{5,7},{... | collective-permute-start | bytes 1179656 | tf_op jit(solution)/shard_map/ppermute | solution.py:327
  23.2 1.3 %collective-permute-start.1 = (bf16[3,128,512]{2,1,0:T(8,128)(2,1)S(1)}, bf16[3,128,512]{2,1,0:T(8,128)(2,1)S(1)}, u32[]{:S(2)}, u32[]{:S(2)}) collective-permute-start(bf16[3,128,512]{2,1,0:T(8,128)(2,1)S(1)} %get-tuple-element.16), channel_id=1, source_target_pairs={{2,0},{4,2},{6,4},{8,6},{10,8},{12,10},{14,12},{3,1},{5,3},{7,5},{... | collective-permute-start | bytes 1179656 | tf_op jit(solution)/shard_map/ppermute | solution.py:328
  24.5 1.3 %collective-permute-done.6.b = bf16[128,640]{1,0:T(8,128)(2,1)S(1)} collective-permute-done((bf16[128,640]{1,0:T(8,128)(2,1)S(1)}, bf16[128,640]{1,0:T(8,128)(2,1)S(1)}, u32[]{:S(2)}, u32[]{:S(2)}) %collective-permute-start.6) | collective-permute-done | bytes 163872 | tf_op jit(solution)/shard_map/ppermute | solution.py:363
  25.8 0.6 shard_map.108.a
  26.4 3.9 %collective-permute-start.7 = (bf16[128,640]{1,0:T(8,128)(2,1)S(1)}, bf16[128,640]{1,0:T(8,128)(2,1)S(1)}, u32[]{:S(2)}, u32[]{:S(2)}) collective-permute-start(bf16[128,640]{1,0:T(8,128)(2,1)S(1)} %shard_map.108.a), channel_id=1, source_target_pairs={{0,4},{2,6},{4,0},{6,2},{8,12},{10,14},{12,8},{14,10},{1,5},{3,7},... | collective-permute-start | bytes 491528 | tf_op jit(solution)/shard_map/ppermute | solution.py:363
  30.3 1.3 %collective-permute-start.2 = (bf16[3,8,512]{2,1,0:T(8,128)(2,1)S(1)}, bf16[3,8,512]{2,1,0:T(8,128)(2,1)S(1)}, u32[]{:S(2)}, u32[]{:S(2)}) collective-permute-start(bf16[3,8,512]{2,1,0:T(8,128)(2,1)S(1)} %get-tuple-element.19), channel_id=1, source_target_pairs={{0,3},{1,2},{2,5},{3,4},{4,7},{5,6},{6,9},{7,8},{8,11},{9,10},{10,... | collective-permute-start | bytes 73736 | tf_op jit(solution)/shard_map/ppermute | solution.py:332
  31.5 10.2 %collective-permute-done.7.b = bf16[128,640]{1,0:T(8,128)(2,1)S(1)} collective-permute-done((bf16[128,640]{1,0:T(8,128)(2,1)S(1)}, bf16[128,640]{1,0:T(8,128)(2,1)S(1)}, u32[]{:S(2)}, u32[]{:S(2)}) %collective-permute-start.7) | collective-permute-done | bytes 163872 | tf_op jit(solution)/shard_map/ppermute | solution.py:363
  41.7 1.5 %collective-permute-start.3 = (bf16[3,8,512]{2,1,0:T(8,128)(2,1)S(1)}, bf16[3,8,512]{2,1,0:T(8,128)(2,1)S(1)}, u32[]{:S(2)}, u32[]{:S(2)}) collective-permute-start(bf16[3,8,512]{2,1,0:T(8,128)(2,1)S(1)} %get-tuple-element.18), channel_id=1, source_target_pairs={{3,0},{2,1},{5,2},{4,3},{7,4},{6,5},{9,6},{8,7},{11,8},{10,9},{13,... | collective-permute-start | bytes 73736 | tf_op jit(solution)/shard_map/ppermute | solution.py:333
  43.2 0.6 shard_map.109.a
  43.8 3.3 %collective-permute-start.8 = (bf16[128,640]{1,0:T(8,128)(2,1)S(1)}, bf16[128,640]{1,0:T(8,128)(2,1)S(1)}, u32[]{:S(2)}, u32[]{:S(2)}) collective-permute-start(bf16[128,640]{1,0:T(8,128)(2,1)S(1)} %shard_map.109.a), channel_id=1, source_target_pairs={{0,8},{2,10},{4,12},{6,14},{8,0},{10,2},{12,4},{14,6},{1,9},{3,11}... | collective-permute-start | bytes 491528 | tf_op jit(solution)/shard_map/ppermute | solution.py:363
  47.1 1.2 %copy-done.14 = bf16[1024,512]{1,0:T(8,128)(2,1)S(1)} copy-done((bf16[1024,512]{1,0:T(8,128)(2,1)S(1)}, bf16[1024,512]{1,0:T(8,128)(2,1)}, u32[]{:S(2)}) %copy-start.14) | copy-done | bytes 1048600
  48.3 3.5 %shard_map.105 = (bf16[16,64,512]{2,1,0:T(8,128)(2,1)S(1)}, bf16[8,16,16,512]{3,2,1,0:T(8,128)(2,1)}, bf16[8,16,16,512]{3,2,1,0:T(8,128)(2,1)}) custom-call(bf16[8,128,512]{2,1,0:T(8,128)(2,1)S(1)} %copy-done.1, bf16[8,8,512]{2,1,0:T(8,128)(2,1)S(1)} %collective-permute-done.4.side, f32[1,512]{1,0:T(1,128)S(1)} %bitcast.8, bf16[512,1536]{1,0:T(8,128)(2,1)S(1)} %copy-done.4, ...), custom_call_target="tpu_custom_call" | custom-call | flops 2000000000 | bytes 10029056 | tf_op jit(solution)/shard_map/pallas_call | solution.py:290
  51.8 1.4 %collective-permute-done.8.b = bf16[128,640]{1,0:T(8,128)(2,1)S(1)} collective-permute-done((bf16[128,640]{1,0:T(8,128)(2,1)S(1)}, bf16[128,640]{1,0:T(8,128)(2,1)S(1)}, u32[]{:S(2)}, u32[]{:S(2)}) %collective-permute-start.8) | collective-permute-done | bytes 163872 | tf_op jit(solution)/shard_map/ppermute | solution.py:363
  53.2 0.5 shard_map.110
  53.9 12.9 %shard_map.106 = bf16[8,128,512]{2,1,0:T(8,128)(2,1)} custom-call(f32[8]{0:T(128)S(1)} %broadcast_multiply_fusion.scale, s32[5]{0:T(128)S(1)} %convert_element_type.3.place, bf16[8,128,512]{2,1,0:T(8,128)(2,1)S(1)} %copy-done.1, bf16[3,128,512]{2,1,0:T(8,128)(2,1)S(1)} %collective-permute-done.up, bf16[3,128,512]{2,1,0:T(8,128)(2,1)S(1)} %collective-permute-done.1.down, ...), custom_call_target="tpu_custom_call" | custom-call | flops 6000000000 | bytes 10274868 | tf_op jit(solution)/shard_map/pallas_call | solution.py:290
  66.8 0.8 %maximum_select_fusion = bf16[256,512]{1,0:T(8,128)(2,1)} fusion(bf16[128,512]{1,0:T(8,128)(2,1)S(1)} %collective-permute-done.9, bf16[128,512]{1,0:T(8,128)(2,1)S(1)} %shard_map.110, pred[]{:T(512)S(6)} %eq.4), kind=kLoop, calls=%fused_computation | loop fusion | flops 1179648 | bytes 524289 | tf_op jit(solution)/shard_map/jit(_where)/select_n | solution.py:369
  (32 shorter events, 0.2 us)
Async XLA Ops:
  1.4 1.2 %copy-start = (bf16[8,128,512]{2,1,0:T(8,128)(2,1)S(1)}, bf16[8,128,512]{2,1,0:T(8,128)(2,1)}, u32[]{:S(2)}) copy-start(bf16[8,128,512]{2,1,0:T(8,128)(2,1)} %x.5) | copy-start | bytes 3145732
  2.6 1.4 %copy-start.3 = (bf16[512,1536]{1,0:T(8,128)(2,1)S(1)}, bf16[512,1536]{1,0:T(8,128)(2,1)}, u32[]{:S(2)}) copy-start(bf16[512,1536]{1,0:T(8,128)(2,1)} %weights.5) | copy-start | bytes 4718596
  4.0 1.0 %copy-start.5 = (bf16[512,512]{1,0:T(8,128)(2,1)S(1)}, bf16[512,512]{1,0:T(8,128)(2,1)}, u32[]{:S(2)}) copy-start(bf16[512,512]{1,0:T(8,128)(2,1)} %asking.1) | copy-start | bytes 1572868
  5.1 0.9 %copy-start.7 = (bf16[256,512]{1,0:T(8,128)(2,1)S(1)}, bf16[256,512]{1,0:T(8,128)(2,1)}, u32[]{:S(2)}) copy-start(bf16[256,512]{1,0:T(8,128)(2,1)} %slots.1) | copy-start | bytes 786436
  6.0 0.7 %copy-start.8 = (f32[512]{0:T(512)S(1)}, f32[512]{0:T(512)}, u32[]{:S(2)}) copy-start(f32[512]{0:T(512)} %param.14) | copy-start | bytes 6148
  6.7 0.7 %copy-start.9 = (f32[512]{0:T(512)S(1)}, f32[512]{0:T(512)}, u32[]{:S(2)}) copy-start(f32[512]{0:T(512)} %param.10) | copy-start | bytes 6148
  7.4 9.3 %copy-start.1 = (bf16[8,128,512]{2,1,0:T(8,128)(2,1)S(1)}, bf16[8,128,512]{2,1,0:T(8,128)(2,1)}, u32[]{:S(2)}) copy-start(bf16[8,128,512]{2,1,0:T(8,128)(2,1)} %x.5) | copy-start | bytes 3145732
  14.2 1.0 %copy-start.11 = (bf16[1024,512]{1,0:T(8,128)(2,1)}, bf16[1024,512]{1,0:T(8,128)(2,1)S(1)}, u32[]{:S(2)}) copy-start(bf16[1024,512]{1,0:T(8,128)(2,1)S(1)} %get-tuple-element.9.keys) | copy-start | bytes 3145732
  15.2 1.0 %copy-start.13 = (bf16[1024,512]{1,0:T(8,128)(2,1)}, bf16[1024,512]{1,0:T(8,128)(2,1)S(1)}, u32[]{:S(2)}) copy-start(bf16[1024,512]{1,0:T(8,128)(2,1)S(1)} %get-tuple-element.10.values) | copy-start | bytes 3145732
  16.2 30.8 %copy-start.4 = (bf16[512,1536]{1,0:T(8,128)(2,1)S(1)}, bf16[512,1536]{1,0:T(8,128)(2,1)}, u32[]{:S(2)}) copy-start(bf16[512,1536]{1,0:T(8,128)(2,1)} %weights.5) | copy-start | bytes 4718596
  16.2 30.8 %copy-start.10 = (f32[512]{0:T(512)S(1)}, f32[512]{0:T(512)}, u32[]{:S(2)}) copy-start(f32[512]{0:T(512)} %param.10) | copy-start | bytes 6148
  16.2 1.5 %collective-permute-start.5 = (bf16[128,640]{1,0:T(8,128)(2,1)S(1)}, bf16[128,640]{1,0:T(8,128)(2,1)S(1)}, u32[]{:S(2)}, u32[]{:S(2)}) collective-permute-start(bf16[128,640]{1,0:T(8,128)(2,1)S(1)} %get-tuple-element.15), channel_id=1, source_target_pairs={{0,1},{1,0},{2,3},{3,2},{4,5},{5,4},{6,7},{7,6},{8,9},{9,8},{10,11... | collective-permute-start | bytes 491528 | tf_op jit(solution)/shard_map/ppermute | solution.py:358
  16.7 30.4 %copy-start.12 = (bf16[1024,512]{1,0:T(8,128)(2,1)S(1)}, bf16[1024,512]{1,0:T(8,128)(2,1)}, u32[]{:S(2)}) copy-start(bf16[1024,512]{1,0:T(8,128)(2,1)} %copy-done.11) | copy-start | bytes 3145732
  16.7 27.1 %collective-permute-start.4 = (bf16[8,8,512]{2,1,0:T(8,128)(2,1)S(1)}, bf16[8,8,512]{2,1,0:T(8,128)(2,1)S(1)}, u32[]{:S(2)}, u32[]{:S(2)}) collective-permute-start(bf16[8,8,512]{2,1,0:T(8,128)(2,1)S(1)} %slice_select_fusion), channel_id=1, source_target_pairs={{0,1},{1,0},{2,3},{3,2},{4,5},{5,4},{6,7},{7,6},{8,9},{9,8},{10,11... | collective-permute-start | bytes 196616 | tf_op jit(solution)/shard_map/ppermute | solution.py:329
  18.3 7.5 %collective-permute-start.6 = (bf16[128,640]{1,0:T(8,128)(2,1)S(1)}, bf16[128,640]{1,0:T(8,128)(2,1)S(1)}, u32[]{:S(2)}, u32[]{:S(2)}) collective-permute-start(bf16[128,640]{1,0:T(8,128)(2,1)S(1)} %shard_map.107.a), channel_id=1, source_target_pairs={{0,2},{2,0},{4,6},{6,4},{8,10},{10,8},{12,14},{14,12},{1,3},{3,1},... | collective-permute-start | bytes 491528 | tf_op jit(solution)/shard_map/ppermute | solution.py:363
  21.3 32.6 %collective-permute-start = (bf16[3,128,512]{2,1,0:T(8,128)(2,1)S(1)}, bf16[3,128,512]{2,1,0:T(8,128)(2,1)S(1)}, u32[]{:S(2)}, u32[]{:S(2)}) collective-permute-start(bf16[3,128,512]{2,1,0:T(8,128)(2,1)S(1)} %get-tuple-element.17), channel_id=1, source_target_pairs={{0,2},{2,4},{4,6},{6,8},{8,10},{10,12},{12,14},{1,3},{3,5},{5,7},{... | collective-permute-start | bytes 1179656 | tf_op jit(solution)/shard_map/ppermute | solution.py:327
  23.2 30.6 %collective-permute-start.1 = (bf16[3,128,512]{2,1,0:T(8,128)(2,1)S(1)}, bf16[3,128,512]{2,1,0:T(8,128)(2,1)S(1)}, u32[]{:S(2)}, u32[]{:S(2)}) collective-permute-start(bf16[3,128,512]{2,1,0:T(8,128)(2,1)S(1)} %get-tuple-element.16), channel_id=1, source_target_pairs={{2,0},{4,2},{6,4},{8,6},{10,8},{12,10},{14,12},{3,1},{5,3},{7,5},{... | collective-permute-start | bytes 1179656 | tf_op jit(solution)/shard_map/ppermute | solution.py:328
  26.4 15.4 %collective-permute-start.7 = (bf16[128,640]{1,0:T(8,128)(2,1)S(1)}, bf16[128,640]{1,0:T(8,128)(2,1)S(1)}, u32[]{:S(2)}, u32[]{:S(2)}) collective-permute-start(bf16[128,640]{1,0:T(8,128)(2,1)S(1)} %shard_map.108.a), channel_id=1, source_target_pairs={{0,4},{2,6},{4,0},{6,2},{8,12},{10,14},{12,8},{14,10},{1,5},{3,7},... | collective-permute-start | bytes 491528 | tf_op jit(solution)/shard_map/ppermute | solution.py:363
  30.3 23.6 %collective-permute-start.2 = (bf16[3,8,512]{2,1,0:T(8,128)(2,1)S(1)}, bf16[3,8,512]{2,1,0:T(8,128)(2,1)S(1)}, u32[]{:S(2)}, u32[]{:S(2)}) collective-permute-start(bf16[3,8,512]{2,1,0:T(8,128)(2,1)S(1)} %get-tuple-element.19), channel_id=1, source_target_pairs={{0,3},{1,2},{2,5},{3,4},{4,7},{5,6},{6,9},{7,8},{8,11},{9,10},{10,... | collective-permute-start | bytes 73736 | tf_op jit(solution)/shard_map/ppermute | solution.py:332
  41.7 12.1 %collective-permute-start.3 = (bf16[3,8,512]{2,1,0:T(8,128)(2,1)S(1)}, bf16[3,8,512]{2,1,0:T(8,128)(2,1)S(1)}, u32[]{:S(2)}, u32[]{:S(2)}) collective-permute-start(bf16[3,8,512]{2,1,0:T(8,128)(2,1)S(1)} %get-tuple-element.18), channel_id=1, source_target_pairs={{3,0},{2,1},{5,2},{4,3},{7,4},{6,5},{9,6},{8,7},{11,8},{10,9},{13,... | collective-permute-start | bytes 73736 | tf_op jit(solution)/shard_map/ppermute | solution.py:333
  43.8 9.4 %collective-permute-start.8 = (bf16[128,640]{1,0:T(8,128)(2,1)S(1)}, bf16[128,640]{1,0:T(8,128)(2,1)S(1)}, u32[]{:S(2)}, u32[]{:S(2)}) collective-permute-start(bf16[128,640]{1,0:T(8,128)(2,1)S(1)} %shard_map.109.a), channel_id=1, source_target_pairs={{0,8},{2,10},{4,12},{6,14},{8,0},{10,2},{12,4},{14,6},{1,9},{3,11}... | collective-permute-start | bytes 491528 | tf_op jit(solution)/shard_map/ppermute | solution.py:363
  47.1 1.2 %copy-start.14 = (bf16[1024,512]{1,0:T(8,128)(2,1)S(1)}, bf16[1024,512]{1,0:T(8,128)(2,1)}, u32[]{:S(2)}) copy-start(bf16[1024,512]{1,0:T(8,128)(2,1)} %copy-done.13) | copy-start | bytes 3145732
  48.3 4.9 %copy-start.2 = (bf16[512,512]{1,0:T(8,128)(2,1)S(1)}, bf16[512,512]{1,0:T(8,128)(2,1)}, u32[]{:S(2)}) copy-start(bf16[512,512]{1,0:T(8,128)(2,1)} %exits.3) | copy-start | bytes 1572868
  48.3 5.6 %copy-start.6 = (bf16[512,512]{1,0:T(8,128)(2,1)S(1)}, bf16[512,512]{1,0:T(8,128)(2,1)}, u32[]{:S(2)}) copy-start(bf16[512,512]{1,0:T(8,128)(2,1)} %exits.2) | copy-start | bytes 1572868
  53.7 13.0 %collective-permute-start.9 = (bf16[128,512]{1,0:T(8,128)(2,1)S(1)}, bf16[128,512]{1,0:T(8,128)(2,1)S(1)}, u32[]{:S(2)}, u32[]{:S(2)}) collective-permute-start(bf16[128,512]{1,0:T(8,128)(2,1)S(1)} %shard_map.110), channel_id=1, source_target_pairs={{0,1},{1,0},{2,3},{3,2},{4,5},{5,4},{6,7},{7,6},{8,9},{9,8},{10,11... | collective-permute-start | bytes 393224 | tf_op jit(solution)/shard_map/ppermute | solution.py:368

commit v2 on v1

v2 whole, which is shorter than its diff:
```python
import functools
import math

import jax
import jax.numpy as jnp
from jax import lax
from jax.experimental import pallas as pl
from jax.experimental.pallas import tpu as pltpu
from jax.sharding import PartitionSpec as P

H = 8
BLK = 8
RIM = 3
F32 = jnp.float32
BF16 = jnp.bfloat16
NEG = -1e30
HBM = pl.BlockSpec(memory_space=pltpu.HBM)
VMEM = pl.BlockSpec(memory_space=pltpu.VMEM)
SMEM = pl.BlockSpec(memory_space=pltpu.SMEM)
CONTRACT_LAST = (((1,), (1,)), ((), ()))


def dot(a, b):
    return jnp.dot(a, b, preferred_element_type=F32)


def token_norm(floats, gain):
    scaled = floats * lax.rsqrt(jnp.mean(floats * floats, axis=-1, keepdims=True) + 1e-05)
    return (scaled * gain).astype(BF16)


def head_ones(width, channels):
    a = lax.broadcasted_iota(jnp.int32, (width, width), 0) // channels
    b = lax.broadcasted_iota(jnp.int32, (width, width), 1) // channels
    return jnp.where(a == b, 1.0, 0.0).astype(BF16)


def head_norm(floats, ones, channels):
    squares = floats * floats
    high = squares.astype(BF16)
    low = (squares - high.astype(F32)).astype(BF16)
    width = ones.shape[0]
    sums = [
        dot(high[:, i : i + width], ones) + dot(low[:, i : i + width], ones)
        for i in range(0, floats.shape[1], width)
    ]
    mean = jnp.concatenate(sums, axis=1) * (1.0 / channels)
    return floats * lax.rsqrt(mean + 1e-06)


def latent_kernel(
    scale,
    place,
    x_far,
    gain,
    weights_far,
    slots_far,
    slot_gain,
    asking_far,
    keys,
    values,
    mine,
    other,
    x,
    weights,
    slots,
    asking,
    sems,
):
    rows, cols, width = x.shape
    heads = H
    channels = width // heads
    latents = slots.shape[0]
    copies = [(slots_far, slots), (asking_far, asking)]
    copies += [(weights_far.at[:, width:], weights), (x_far, x)]
    copies = [
        pltpu.make_async_copy(far, near, sems.at[n]) for n, (far, near) in enumerate(copies)
    ]
    for copy in copies:
        copy.start()
    ones = head_ones(256, channels)
    copies[0].wait()
    copies[1].wait()
    slot_normed = token_norm(slots[...].astype(F32), slot_gain[...])
    asked = head_norm(dot(slot_normed, asking[...]), ones, channels).astype(BF16)
    copies[2].wait()
    copies[3].wait()
    for i in range(rows // 2):
        tokens = x[2 * i : 2 * i + 2].reshape(2 * cols, width).astype(F32)
        normed = token_norm(tokens, gain[...])
        both = dot(normed, weights[...])
        here = slice(2 * i * cols, (2 * i + 2) * cols)
        keys[here, :] = head_norm(both[:, :width], ones, channels).astype(BF16)
        values[here, :] = both[:, width:].astype(BF16)
    half = latents // 2
    first = place[4] == 0
    lanes = lax.broadcasted_iota(jnp.int32, (1, 128), 1)
    peaks = jnp.zeros((latents, 128), F32)
    totals = jnp.zeros((latents, 128), F32)
    per = 128 // channels
    for pair in range(heads // per):
        at = slice(pair * 128, (pair + 1) * 128)
        owner = lanes // channels
        query = jnp.concatenate(
            [asked[:, at] * jnp.where(owner == n, 1.0, 0.0).astype(BF16) for n in range(per)],
            axis=0,
        )
        scores = lax.dot_general(query, keys[:, at], CONTRACT_LAST, preferred_element_type=F32)
        expos = []
        for inner in range(per):
            head = pair * per + inner
            score = scores[inner * latents : (inner + 1) * latents] * (scale[head] * (math.log2(math.e) / math.sqrt(channels)))
            peak = jnp.max(score, axis=-1, keepdims=True)
            peak = (jnp.ceil(peak * 0.5) * 2.0).astype(BF16).astype(F32)
            expo = jnp.exp2(score - peak)
            total = jnp.sum(expo, axis=-1, keepdims=True)
            expos.append(expo.astype(BF16))
            peaks = jnp.where(lanes == head, peak, peaks)
            totals = jnp.where(lanes == head, total, totals)
        mixed = dot(jnp.concatenate(expos, axis=0), values[:, at])
        out = mixed[:latents]
        for inner in range(1, per):
            out = jnp.where(owner == inner, mixed[inner * latents : (inner + 1) * latents], out)
        out = out.astype(BF16)
        mine[:half, at] = jnp.where(first, out[:half], out[half:])
        other[:half, at] = jnp.where(first, out[half:], out[:half])
    high = totals.astype(BF16)
    low = (totals - high.astype(F32)).astype(BF16)
    sub = lax.broadcasted_iota(jnp.int32, (16, 128), 0)
    pick = jnp.where(sub == lax.broadcasted_iota(jnp.int32, (16, 128), 1), 1.0, 0.0)
    pick = jnp.where(sub < heads, pick, 0.0).astype(BF16)
    for n, columns in enumerate((peaks.astype(BF16), high, low)):
        flat = lax.dot_general(pick, columns, CONTRACT_LAST, preferred_element_type=F32)
        flat = flat.astype(BF16)
        at = slice(n * half, (n + 1) * half)
        mine[half:, at] = jnp.where(first, flat[:, :half], flat[:, half:])
        other[half:, at] = jnp.where(first, flat[:, half:], flat[:, :half])
    rest = slice(3 * half, width)
    mine[half:, rest] = jnp.zeros((16, width - 3 * half), BF16)
    other[half:, rest] = jnp.zeros((16, width - 3 * half), BF16)


def head_rows(width, all_lanes):
    channels = width // H
    a = lax.broadcasted_iota(jnp.int32, (16, width), 0)
    b = lax.broadcasted_iota(jnp.int32, (16, width), 1)
    same = (b // channels == a) if all_lanes else (b == a * channels)
    return jnp.where(same & (a < H), 1.0, 0.0).astype(BF16)


def opened(part, width):
    half = part.shape[0] - 16
    rows = head_rows(width, True)

    def spread(n):
        return lax.dot_general(
            part[half:, n * half : (n + 1) * half],
            rows,
            (((0,), (0,)), ((), ())),
            preferred_element_type=F32,
        )

    return (part[:half].astype(F32), spread(0), spread(1) + spread(2))


def joined(parts, width):
    items = [opened(p, width) for p in parts]
    peak = items[0][1]
    for item in items[1:]:
        peak = jnp.maximum(peak, item[1])
    out, total = (0.0, 0.0)
    for o, m, t in items:
        factor = jnp.exp2(m - peak)
        out = out + o * factor
        total = total + t * factor
    return (out, peak, total)


def join_kernel(a, b, result):
    width = result.shape[1]
    half = result.shape[0] - 16
    out, peak, total = joined([a[...], b[...]], width)
    result[:half] = out.astype(BF16)
    high = total.astype(BF16)
    low = (total - high.astype(F32)).astype(BF16)
    rows = head_rows(width, False)
    for n, spread in enumerate((peak.astype(BF16), high, low)):
        flat = lax.dot_general(rows, spread, CONTRACT_LAST, preferred_element_type=F32)
        result[half:, n * half : (n + 1) * half] = flat.astype(BF16)
    result[half:, 3 * half :] = jnp.zeros((16, width - 3 * half), BF16)


def last_kernel(a, b, exits, result):
    width = result.shape[1]
    out, _, total = joined([a[...], b[...]], width)
    result[...] = dot((out / total).astype(BF16), exits[...]).astype(BF16)


def windows(tokens, side):
    cols, width = tokens.shape
    own = tokens.reshape(cols // BLK, BLK, width)
    side = side.reshape(1, BLK, width)
    after = jnp.concatenate([own[1:], side], axis=0)
    before = jnp.concatenate([side, own[:-1]], axis=0)
    place = lax.broadcasted_iota(jnp.int32, own.shape, 1)
    rim = jnp.where(place < BLK // 2, after, before)
    return jnp.concatenate([own, rim], axis=1).astype(BF16)


def own_kernel(x, side, gain, weights, keys, values, queries, key_win, value_win):
    rows, cols, width = x.shape
    channels = width // H
    ones = head_ones(256, channels)
    beside = token_norm(side[...].reshape(rows * BLK, width).astype(F32), gain[...])
    both = dot(beside, weights[:, width:])
    side_keys = head_norm(both[:, :width], ones, channels)
    side_values = both[:, width:]
    for i in range(rows // 2):
        tokens = x[2 * i : 2 * i + 2].reshape(2 * cols, width).astype(F32)
        normed = token_norm(tokens, gain[...])
        query = head_norm(dot(normed, weights[:, :width]), ones, channels)
        query = query.reshape(2, cols // BLK, BLK, width).transpose(1, 0, 2, 3)
        queries[:, 16 * i : 16 * i + 16, :] = query.reshape(cols // BLK, 16, width).astype(BF16)
    for r in range(rows):
        here = slice(r * cols, (r + 1) * cols)
        at = slice(r * BLK, (r + 1) * BLK)
        key_win[r] = windows(keys[here, :].astype(F32), side_keys[at])
        value_win[r] = windows(values[here, :].astype(F32), side_values[at])


def rim_kernel(up, down, gain, weights, key_rim, value_rim):
    lines, cols, width = up.shape
    channels = width // H
    ones = head_ones(256, channels)
    for n, ref in enumerate((up, down)):
        normed = token_norm(ref[...].astype(F32).reshape(lines * cols, width), gain[...])
        both = dot(normed, weights[:, width:])
        key = head_norm(both[:, :width], ones, channels)
        value = both[:, width:]
        for r in range(lines):
            at = slice(r * cols, (r + 1) * cols)
            key_rim[n * lines + r] = windows(key[at], key[at.start : at.start + BLK])
            value_rim[n * lines + r] = windows(value[at], value[at.start : at.start + BLK])


def halo_kernel(
    scale,
    place,
    x,
    corner,
    gain,
    weights,
    exits,
    queries,
    key_win,
    value_win,
    key_rim,
    value_rim,
    *refs,
    start,
    stop,
):
    if start == 0:
        attended, key_end, value_end = refs
    else:
        earlier, tokens_out, key_end, value_end, attended = refs
    rows, cols, width = x.shape
    channels = width // H
    ones = head_ones(256, channels)
    blocks = cols // BLK
    lines = rows + 2 * RIM

    normed = token_norm(corner[...].reshape(2 * RIM * BLK, width).astype(F32), gain[...])
    both = dot(normed, weights[:, width:])
    corner_keys = head_norm(both[:, :width], ones, channels).reshape(2 * RIM, BLK, width)
    corner_values = both[:, width:].reshape(2 * RIM, BLK, width)
    sub = lax.broadcasted_iota(jnp.int32, (1, 16, 1), 1)
    for block, beyond in ((0, sub >= 2 * BLK - RIM), (blocks - 1, sub < BLK + RIM)):
        if not start <= block < stop:
            continue
        beyond = beyond & (sub >= BLK)
        for rim, tile, end in (
            (key_rim, corner_keys, key_end),
            (value_rim, corner_values, value_end),
        ):
            double = jnp.concatenate([tile, tile], axis=1)
            kept = rim[:, block].astype(F32)
            end[...] = jnp.where(beyond, double, kept).astype(BF16)

    spot = lax.broadcasted_iota(jnp.int32, (1, lines * 16), 1)
    line, sub = (spot // 16, spot % 16)
    upper = (line >= rows) & (line < rows + RIM)
    lower = line >= rows + RIM
    fixed = (sub == BLK + RIM) | (sub == BLK + RIM + 1)
    fixed = fixed | (upper & (place[0] == 0)) | (lower & (place[1] == 0))
    right = (sub >= BLK) & (sub < BLK + RIM)
    left = sub >= 2 * BLK - RIM
    group = 256
    per = group // channels
    owner = lax.broadcasted_iota(jnp.int32, (1, group), 1) // channels

    def one_block(block):
        gone = fixed
        if block == 0:
            gone = gone | (left & (place[2] == 0))
        if block == blocks - 1:
            gone = gone | (right & (place[3] == 0))
        bias = jnp.where(gone, NEG, 0.0)
        outs = []
        for g in range(width // group):
            at = slice(g * group, (g + 1) * group)

            def around(win, rim, end):
                if block == 0 or block == blocks - 1:
                    far = end[:, :, at]
                else:
                    far = rim[:, block, :, at]
                own = win[:, block, :, at].reshape(rows * 16, group)
                return jnp.concatenate([own, far.reshape(2 * RIM * 16, group)], axis=0)

            query = queries[block, :, at]
            stacked = jnp.concatenate(
                [query * jnp.where(owner == h, 1.0, 0.0).astype(BF16) for h in range(per)], axis=0
            )
            key = around(key_win, key_rim, key_end)
            value = around(value_win, value_rim, value_end)
            scores = lax.dot_general(stacked, key, CONTRACT_LAST, preferred_element_type=F32)
            expos, totals = ([], [])
            n = BLK * BLK
            for h in range(per):
                s = scores[h * n : (h + 1) * n] * (scale[g * per + h] * (math.log2(math.e) / math.sqrt(channels))) + bias
                expo = jnp.exp2(s - jnp.max(s, axis=-1, keepdims=True))
                totals.append(jnp.sum(expo, axis=-1, keepdims=True))
                expos.append(expo.astype(BF16))
            mixed = dot(jnp.concatenate(expos, axis=0), value)
            out = jnp.zeros((n, group), F32)
            for h in range(per):
                out = jnp.where(owner == h, mixed[h * n : (h + 1) * n] / totals[h], out)
            outs.append(out)
        return jnp.concatenate(outs, axis=1).reshape(BLK, BLK, width)

    for i in range((stop - start) // 2):
        block = start + 2 * i
        pair = jnp.concatenate([one_block(block), one_block(block + 1)], axis=1)
        attended[:, 16 * i : 16 * i + 16, :] = pair.astype(BF16)
    if start == 0:
        return
    for part, at in ((earlier, slice(0, start * BLK)), (attended, slice(start * BLK, cols))):
        count = at.stop - at.start
        for i in range(rows // 4):
            here = slice(4 * i, 4 * i + 4)
            branch = dot(part[here].reshape(4 * count, width), exits[...])
            total = x[here, at].astype(F32) + branch.reshape(4, count, width)
            tokens_out[here, at] = total.astype(BF16)


def call(kernel, outs, ins, scratch=(), megabytes=16, smem=0, far=()):
    shapes = [jax.ShapeDtypeStruct(*o) for o in outs]
    return pl.pallas_call(
        kernel,
        out_shape=shapes,
        in_specs=[SMEM if n < smem else HBM if n in far else VMEM for n in range(len(ins))],
        out_specs=[VMEM] * len(shapes),
        scratch_shapes=list(scratch),
        compiler_params=pltpu.CompilerParams(vmem_limit_bytes=megabytes * 1024 * 1024),
        cost_estimate=pl.CostEstimate(flops=1000, bytes_accessed=1000, transcendentals=0),
    )(*ins)


def per_device(
    crop_feature_grid,
    pixel_layernorm_gain,
    triple_projection_matrix,
    halo_exit_matrix,
    memory_slots,
    memory_layernorm_gain,
    memory_asking_matrix,
    memory_exit_matrix,
    branch_logit_multiplier,
):
    x = crop_feature_grid
    rows, cols, width = x.shape
    latents = memory_slots.shape[0]
    tall, wide = (lax.axis_size("rows"), lax.axis_size("cols"))
    row, col = (lax.axis_index("rows"), lax.axis_index("cols"))
    place = jnp.stack([row > 0, row < tall - 1, col > 0, col < wide - 1, col > 0])
    place = place.astype(jnp.int32)
    scale = branch_logit_multiplier
    gain = pixel_layernorm_gain.reshape(1, width)
    slot_gain = memory_layernorm_gain.reshape(1, width)
    weights = triple_projection_matrix

    odd = row % 2 == 1
    near = [(i, i ^ 1) for i in range(tall)]
    far = [(i, j) for i in range(tall) if 0 <= (j := i - 1 if i % 2 == 0 else i + 1) < tall]
    swap = [(0, 1), (1, 0)]

    def edge(array):
        return jnp.where(col == 0, array[:, cols - BLK :], array[:, :BLK])

    top, bottom = (x[:RIM], x[rows - RIM :])
    near_rim = lax.ppermute(jnp.where(odd, top, bottom), "rows", near)
    far_rim = lax.ppermute(jnp.where(odd, bottom, top), "rows", far)
    side = lax.ppermute(edge(x), "cols", swap)
    place, side = lax.optimization_barrier((place, side))

    half = latents // 2
    tokens = rows * cols
    blocks = cols // BLK
    part = ((half + 16, width), BF16)
    keys, values, mine, other = call(
        latent_kernel,
        [((tokens, width), BF16), ((tokens, width), BF16), part, part],
        (scale, place, x, gain, weights, memory_slots, slot_gain, memory_asking_matrix),
        scratch=[
            pltpu.VMEM(x.shape, BF16),
            pltpu.VMEM((width, 2 * width), BF16),
            pltpu.VMEM(memory_slots.shape, BF16),
            pltpu.VMEM(memory_asking_matrix.shape, BF16),
            pltpu.SemaphoreType.DMA((4,)),
        ],
        megabytes=24,
        smem=2,
        far=(2, 4, 5, 7),
    )
    queries, key_win, value_win = call(
        own_kernel,
        [
            ((blocks, rows * BLK, width), BF16),
            ((rows, blocks, 16, width), BF16),
            ((rows, blocks, 16, width), BF16),
        ],
        (x, side, gain, weights, keys, values),
        megabytes=16,
    )
    steps = [2**i for i in range(1, tall.bit_length() - 1)] + [1]
    parts = [mine, lax.ppermute(other, "cols", swap)]
    for n, step in enumerate(steps[:-1]):
        pairs = [(i, i ^ step) for i in range(tall)]
        (whole,) = call(join_kernel, [part], parts, megabytes=4)
        if n == len(steps) - 2:
            whole, near_rim, far_rim, queries = lax.optimization_barrier(
                (whole, near_rim, far_rim, queries)
            )
            up = jnp.where(odd, near_rim, far_rim)
            down = jnp.where(odd, far_rim, near_rim)
            corner = lax.ppermute(jnp.concatenate([edge(up), edge(down)]), "cols", swap)
        parts = [whole, lax.ppermute(whole, "rows", pairs)]

    rim = ((2 * RIM, blocks, 16, width), BF16)
    key_rim, value_rim = call(rim_kernel, [rim, rim], (up, down, gain, weights), megabytes=16)

    def halo(start, stop, outs, earlier, more):
        return call(
            functools.partial(halo_kernel, start=start, stop=stop),
            outs,
            (
                scale,
                place,
                x,
                corner,
                gain,
                weights,
                halo_exit_matrix,
                queries,
                key_win,
                value_win,
                key_rim,
                value_rim,
                *earlier,
            ),
            scratch=[pltpu.VMEM((2 * RIM, 16, width), BF16)] * 2 + more,
            megabytes=24,
            smem=2,
        )[0]

    middle = blocks // 4 * 2
    half_shape = (rows, middle * BLK, width)
    earlier = halo(0, middle, [(half_shape, BF16)], (), [])
    parts[1], earlier = lax.optimization_barrier((parts[1], earlier))
    (whole,) = call(join_kernel, [part], parts, megabytes=4)
    pairs = [(i, i ^ steps[-1]) for i in range(tall)]
    got = lax.ppermute(whole, "rows", pairs)
    rest = (rows, cols - middle * BLK, width)
    tokens_out = halo(middle, blocks, [(x.shape, BF16)], (earlier,), [pltpu.VMEM(rest, BF16)])
    whole, got, tokens_out = lax.optimization_barrier((whole, got, tokens_out))
    (mixed,) = call(
        last_kernel, [((half, width), BF16)], (whole, got, memory_exit_matrix), megabytes=6
    )
    theirs = lax.ppermute(mixed, "cols", swap)
    latent_mix = jnp.where(
        col == 0, jnp.concatenate([mixed, theirs]), jnp.concatenate([theirs, mixed])
    )
    return (tokens_out, latent_mix)


def solution(mesh):
    return jax.shard_map(
        per_device,
        mesh=mesh,
        in_specs=(P(("grp", "rows"), "cols", None), P(), P(), P(), P(), P(), P(), P(), P()),
        out_specs=(P(("grp", "rows"), "cols", None), P("grp", None)),
        check_vma=False,
    )
```

time: 68 us -> 48.2 us (0.71)
  waiting for transfers between devices: 13.8 us -> 6.56 us
  local copies, waits for them, and re-layouts: 9.37 us -> 3.75 us
  Pallas kernels: 25.4 us -> 20.8 us
  starting transfers between devices: 16.8 us -> 12.9 us
  other arithmetic: 1.44 us -> 3.03 us
    ppermute x3 -> x2, waiting for transfers between devices: 12.9 us -> 2.87 us  [per_device(): parts = [whole, lax.ppermute(whole, 'rows', pairs)]]
    unnamed x30 -> x20, local copies, waits for them, and re-layouts: 9.2 us -> 3.65 us
    pallas_call x7 -> x9, Pallas kernels: 25.4 us -> 20.8 us  [call(): pl.pallas_call(kernel, out_shape=shapes, in_specs=[SMEM if n < smem else...]
    ppermute x3 -> x2, starting transfers between devices: 10.1 us -> 6.03 us  [per_device(): parts = [whole, lax.ppermute(whole, 'rows', pairs)]]
    select_n x1 -> x4, other arithmetic: 0.01 us -> 2.25 us  [the longest x1 1.3 us: per_device(): far_rim = lax.ppermute(jnp.where(odd, bottom, top), 'rows', far)]
    ppermute x1, waiting for transfers between devices: 0.01 us -> 1.33 us  [per_device(): theirs = lax.ppermute(mixed, 'cols', swap)]
    ppermute x5, waiting for transfers between devices: 0.01 us -> 1.13 us  [the longest x1 1.12 us: per_device(): side = lax.ppermute(edge(x), 'cols', swap)]
  transfers between devices with their start and end apart: 10 -> 9, of which waited for: 4 -> 5; matrix products, arithmetic and copies ran while one was open for 0% -> 2% of each run, Pallas kernels for 27% -> 41%
where the time goes in v2:
time: 48.2 us; the launch traced here: 47.9 us
  Pallas kernels  20.8 us (43%)
  starting transfers between devices  12.9 us (27%)
  waiting for transfers between devices  6.56 us (14%)
  local copies, waits for them, and re-layouts  3.75 us (8%)
  other arithmetic  3.03 us (6%)
  between operations  0.84 us (2%)
    pallas_call x9, Pallas kernels, call(): pl.pallas_call(kernel, out_shape=shapes, in_specs=[SMEM if n < smem else...  20.8 us
    ppermute x2, starting transfers between devices, per_device(): parts = [whole, lax.ppermute(whole, 'rows', pairs)]  6.03 us
    unnamed x20, local copies, waits for them, and re-layouts  3.65 us
    ppermute x1, starting transfers between devices, per_device(): near_rim = lax.ppermute(jnp.where(odd, top, bottom), 'rows', near)  3.03 us
    ppermute x2, waiting for transfers between devices, per_device(): parts = [whole, lax.ppermute(whole, 'rows', pairs)]  2.87 us
    ppermute x1, starting transfers between devices, per_device(): got = lax.ppermute(whole, 'rows', pairs)  2.7 us
    ppermute x1, waiting for transfers between devices, per_device(): theirs = lax.ppermute(mixed, 'cols', swap)  1.33 us
    select_n x1, other arithmetic, per_device(): far_rim = lax.ppermute(jnp.where(odd, bottom, top), 'rows', far)  1.3 us
  transfers between devices with their start and end apart: 9, of which 5 were waited for; matrix products, arithmetic and copies ran while one was open for 2% of the time, Pallas kernels for 41%

profile of v2, /device:TPU:0, one launch (start us, length us, event | category | flops | bytes accessed | tf_op | source)
XLA Modules:
  0.0 47.9 jit_solution(12617155726117554979)
XLA Ops:
  0.7 1.3 %broadcast_select_fusion.2 = (bf16[3,128,512]{2,1,0:T(8,128)(2,1)S(1)}, bf16[3,128,512]{2,1,0:T(8,128)(2,1)S(1)}) fusion(pred[]{:T(512)S(6)} %eq.12, bf16[8,128,512]{2,1,0:T(8,128)(2,1)} %x.5), kind=kLoop, calls=%fused_computation.2 | loop fusion | flops 393216 | bytes 1572865 | tf_op jit(solution)/shard_map/jit(_where)/select_n | solution.py:403
  2.0 3.0 %collective-permute-start.3 = (bf16[3,128,512]{2,1,0:T(8,128)(2,1)S(1)}, bf16[3,128,512]{2,1,0:T(8,128)(2,1)S(1)}, u32[]{:S(2)}, u32[]{:S(2)}) collective-permute-start(bf16[3,128,512]{2,1,0:T(8,128)(2,1)S(1)} %get-tuple-element.43), channel_id=1, source_target_pairs={{0,2},{2,0},{4,6},{6,4},{8,10},{10,8},{12,14},{14,12},{1,3},{3,1},... | collective-permute-start | bytes 1179656 | tf_op jit(solution)/shard_map/ppermute | solution.py:402
  5.0 0.7 %collective-permute-start.4 = (bf16[3,128,512]{2,1,0:T(8,128)(2,1)S(1)}, bf16[3,128,512]{2,1,0:T(8,128)(2,1)S(1)}, u32[]{:S(2)}, u32[]{:S(2)}) collective-permute-start(bf16[3,128,512]{2,1,0:T(8,128)(2,1)S(1)} %get-tuple-element.42), channel_id=1, source_target_pairs={{2,4},{4,2},{6,8},{8,6},{10,12},{12,10},{3,5},{5,3},{7,9},{9,7},{1... | collective-permute-start | bytes 1179656 | tf_op jit(solution)/shard_map/ppermute | solution.py:403
  5.7 0.9 %slice_select_fusion = bf16[8,8,512]{2,1,0:T(8,128)(2,1)S(1)} fusion(bf16[8,128,512]{2,1,0:T(8,128)(2,1)} %x.5, pred[]{:T(512)S(6)} %eq.6), kind=kLoop, calls=%fused_computation.5 | loop fusion | flops 32768 | bytes 196609 | tf_op jit(solution)/shard_map/jit(_where)/select_n | solution.py:399
  6.6 0.1 collective-permute-start
  6.7 0.1 stack.20
  6.8 1.1 %collective-permute-done.side = bf16[8,8,512]{2,1,0:T(8,128)(2,1)S(1)} collective-permute-done((bf16[8,8,512]{2,1,0:T(8,128)(2,1)S(1)}, bf16[8,8,512]{2,1,0:T(8,128)(2,1)S(1)}, u32[]{:S(2)}, u32[]{:S(2)}) %collective-permute-start) | collective-permute-done | bytes 65568 | tf_op jit(solution)/shard_map/ppermute | solution.py:404
  7.9 1.2 %copy-done.1 = bf16[8,128,512]{2,1,0:T(8,128)(2,1)S(1)} copy-done((bf16[8,128,512]{2,1,0:T(8,128)(2,1)S(1)}, bf16[8,128,512]{2,1,0:T(8,128)(2,1)}, u32[]{:S(2)}) %copy-start.1) | copy-done | bytes 1048600
  9.1 1.0 %copy-done.4 = bf16[512,512]{1,0:T(8,128)(2,1)S(1)} copy-done((bf16[512,512]{1,0:T(8,128)(2,1)S(1)}, bf16[512,512]{1,0:T(8,128)(2,1)}, u32[]{:S(2)}) %copy-start.4) | copy-done | bytes 524312
  10.2 0.7 %copy-done.7 = f32[512]{0:T(512)S(1)} copy-done((f32[512]{0:T(512)S(1)}, f32[512]{0:T(512)}, u32[]{:S(2)}) %copy-start.7) | copy-done | bytes 2072
  10.9 0.7 %copy-done.9 = f32[512]{0:T(512)S(1)} copy-done((f32[512]{0:T(512)S(1)}, f32[512]{0:T(512)}, u32[]{:S(2)}) %copy-start.9) | copy-done | bytes 2072
  11.6 6.6 %shard_map.104 = (bf16[1024,512]{1,0:T(8,128)(2,1)S(1)}, bf16[1024,512]{1,0:T(8,128)(2,1)S(1)}, bf16[144,512]{1,0:T(8,128)(2,1)S(1)}, bf16[144,512]{1,0:T(8,128)(2,1)S(1)}) custom-call(f32[8]{0:T(128)S(1)} %copy-done.8, s32[5]{0:T(128)S(1)} %convert_element_type.3.place, bf16[8,128,512]{2,1,0:T(8,128)(2,1)S(1)} %copy-done.1, f32[1,512]{1,0:T(1,128)S(1)} %bitcast.6, ...), custom_call_target="tpu_custom_call" | custom-call | flops 1000 | bytes 1000 | tf_op jit(solution)/shard_map/pallas_call | solution.py:359
  18.2 0.2 collective-permute-start.1
  18.4 1.2 %collective-permute-done.1.b = bf16[144,512]{1,0:T(8,128)(2,1)S(1)} collective-permute-done((bf16[144,512]{1,0:T(8,128)(2,1)S(1)}, bf16[144,512]{1,0:T(8,128)(2,1)S(1)}, u32[]{:S(2)}, u32[]{:S(2)}) %collective-permute-start.1) | collective-permute-done | bytes 147488 | tf_op jit(solution)/shard_map/ppermute | solution.py:437
  19.6 0.5 %shard_map.105.a = bf16[144,512]{1,0:T(8,128)(2,1)S(1)} custom-call(bf16[144,512]{1,0:T(8,128)(2,1)S(1)} %get-tuple-element.23.a, bf16[144,512]{1,0:T(8,128)(2,1)S(1)} %collective-permute-done.1.b), custom_call_target="tpu_custom_call" | custom-call | flops 1000 | bytes 1000 | tf_op jit(solution)/shard_map/pallas_call | solution.py:359
  20.2 2.8 %collective-permute-start.2 = (bf16[144,512]{1,0:T(8,128)(2,1)S(1)}, bf16[144,512]{1,0:T(8,128)(2,1)S(1)}, u32[]{:S(2)}, u32[]{:S(2)}) collective-permute-start(bf16[144,512]{1,0:T(8,128)(2,1)S(1)} %shard_map.105.a), channel_id=1, source_target_pairs={{0,4},{2,6},{4,0},{6,2},{8,12},{10,14},{12,8},{14,10},{1,5},{3,7},... | collective-permute-start | bytes 442376 | tf_op jit(solution)/shard_map/ppermute | solution.py:448
  23.0 2.6 %shard_map.107 = (bf16[16,64,512]{2,1,0:T(8,128)(2,1)S(1)}, bf16[8,16,16,512]{3,2,1,0:T(8,128)(2,1)S(1)}, bf16[8,16,16,512]{3,2,1,0:T(8,128)(2,1)S(1)}) custom-call(bf16[8,128,512]{2,1,0:T(8,128)(2,1)S(1)} %copy-done.2, bf16[8,8,512]{2,1,0:T(8,128)(2,1)S(1)} %collective-permute-done.side, f32[1,512]{1,0:T(1,128)S(1)} %bitcast.7, ...), custom_call_target="tpu_custom_call" | custom-call | flops 1000 | bytes 1000 | tf_op jit(solution)/shard_map/pallas_call | solution.py:359
  25.6 1.5 %collective-permute-done.2.b = bf16[144,512]{1,0:T(8,128)(2,1)S(1)} collective-permute-done((bf16[144,512]{1,0:T(8,128)(2,1)S(1)}, bf16[144,512]{1,0:T(8,128)(2,1)S(1)}, u32[]{:S(2)}, u32[]{:S(2)}) %collective-permute-start.2) | collective-permute-done | bytes 147488 | tf_op jit(solution)/shard_map/ppermute | solution.py:448
  27.2 0.5 %shard_map.106.a = bf16[144,512]{1,0:T(8,128)(2,1)S(1)} custom-call(bf16[144,512]{1,0:T(8,128)(2,1)S(1)} %shard_map.105.a, bf16[144,512]{1,0:T(8,128)(2,1)S(1)} %collective-permute-done.2.b), custom_call_target="tpu_custom_call" | custom-call | flops 1000 | bytes 1000 | tf_op jit(solution)/shard_map/pallas_call | solution.py:359
  27.7 3.2 %collective-permute-start.5 = (bf16[144,512]{1,0:T(8,128)(2,1)S(1)}, bf16[144,512]{1,0:T(8,128)(2,1)S(1)}, u32[]{:S(2)}, u32[]{:S(2)}) collective-permute-start(bf16[144,512]{1,0:T(8,128)(2,1)S(1)} %shard_map.106.a), channel_id=1, source_target_pairs={{0,8},{2,10},{4,12},{6,14},{8,0},{10,2},{12,4},{14,6},{1,9},{3,11}... | collective-permute-start | bytes 442376 | tf_op jit(solution)/shard_map/ppermute | solution.py:448
  31.0 0.1 broadcast_select_fusion.1
  31.1 0.1 collective-permute-start.6
  31.1 1.7 %shard_map.108 = (bf16[6,16,16,512]{3,2,1,0:T(8,128)(2,1)S(1)}, bf16[6,16,16,512]{3,2,1,0:T(8,128)(2,1)S(1)}) custom-call(bf16[3,128,512]{2,1,0:T(8,128)(2,1)S(1)} %get-tuple-element.44.up, bf16[3,128,512]{2,1,0:T(8,128)(2,1)S(1)} %get-tuple-element.45.down, f32[1,512]{1,0:T(1,128)S(1)} %bitcast.8, bf16[512,1536]{1,0:T(8,128)(2,1)S(1)} %copy-done), custom_call_target="tpu_custom_call" | custom-call | flops 1000 | bytes 1000 | tf_op jit(solution)/shard_map/pallas_call | solution.py:359
  32.9 3.2 %shard_map.109.refs_0_ = bf16[8,64,512]{2,1,0:T(8,128)(2,1)S(1)} custom-call(f32[8]{0:T(128)S(1)} %copy-done.8, s32[5]{0:T(128)S(1)} %convert_element_type.3.place, bf16[8,128,512]{2,1,0:T(8,128)(2,1)S(1)} %copy-done.2, bf16[6,8,512]{2,1,0:T(8,128)(2,1)S(1)} %collective-permute-done.6.corner, f32[1,512]{1,0:T(1,128)S(1)} %bitcast.9, ...), custom_call_target="tpu_custom_call" | custom-call | flops 1000 | bytes 1000 | tf_op jit(solution)/shard_map/pallas_call | solution.py:359
  36.1 1.3 %collective-permute-done.5.b = bf16[144,512]{1,0:T(8,128)(2,1)S(1)} collective-permute-done((bf16[144,512]{1,0:T(8,128)(2,1)S(1)}, bf16[144,512]{1,0:T(8,128)(2,1)S(1)}, u32[]{:S(2)}, u32[]{:S(2)}) %collective-permute-start.5) | collective-permute-done | bytes 147488 | tf_op jit(solution)/shard_map/ppermute | solution.py:448
  37.4 0.5 %shard_map.110.a = bf16[144,512]{1,0:T(8,128)(2,1)S(1)} custom-call(bf16[144,512]{1,0:T(8,128)(2,1)S(1)} %shard_map.106.a, bf16[144,512]{1,0:T(8,128)(2,1)S(1)} %collective-permute-done.5.b), custom_call_target="tpu_custom_call" | custom-call | flops 1000 | bytes 1000 | tf_op jit(solution)/shard_map/pallas_call | solution.py:359
  38.0 2.7 %collective-permute-start.7 = (bf16[144,512]{1,0:T(8,128)(2,1)S(1)}, bf16[144,512]{1,0:T(8,128)(2,1)S(1)}, u32[]{:S(2)}, u32[]{:S(2)}) collective-permute-start(bf16[144,512]{1,0:T(8,128)(2,1)S(1)} %shard_map.110.a), channel_id=1, source_target_pairs={{0,2},{2,0},{4,6},{6,4},{8,10},{10,8},{12,14},{14,12},{1,3},{3,1},... | collective-permute-start | bytes 442376 | tf_op jit(solution)/shard_map/ppermute | solution.py:483
  40.7 4.3 %shard_map.111 = bf16[8,128,512]{2,1,0:T(8,128)(2,1)} custom-call(f32[8]{0:T(128)S(1)} %copy-done.8, s32[5]{0:T(128)S(1)} %convert_element_type.3.place, bf16[8,128,512]{2,1,0:T(8,128)(2,1)S(1)} %copy-done.2, bf16[6,8,512]{2,1,0:T(8,128)(2,1)S(1)} %collective-permute-done.6.corner, f32[1,512]{1,0:T(1,128)S(1)} %bitcast.10, bf16[512,1536]{1,0:T(8,128)(2,1)S(1)} %copy-done, ...), custom_call_target="tpu_custom_call" | custom-call | flops 1000 | bytes 1000 | tf_op jit(solution)/shard_map/pallas_call | solution.py:359
  45.1 0.6 %shard_map.112 = bf16[128,512]{1,0:T(8,128)(2,1)S(1)} custom-call(bf16[144,512]{1,0:T(8,128)(2,1)S(1)} %shard_map.110.a, bf16[144,512]{1,0:T(8,128)(2,1)S(1)} %collective-permute-done.7.b, bf16[512,512]{1,0:T(8,128)(2,1)S(1)} %copy-done.5), custom_call_target="tpu_custom_call" | custom-call | flops 1000 | bytes 1000 | tf_op jit(solution)/shard_map/pallas_call | solution.py:359
  45.7 0.1 collective-permute-start.8
  45.8 1.3 %collective-permute-done.8 = bf16[128,512]{1,0:T(8,128)(2,1)S(1)} collective-permute-done((bf16[128,512]{1,0:T(8,128)(2,1)S(1)}, bf16[128,512]{1,0:T(8,128)(2,1)S(1)}, u32[]{:S(2)}, u32[]{:S(2)}) %collective-permute-start.8) | collective-permute-done | bytes 131104 | tf_op jit(solution)/shard_map/ppermute | solution.py:490
  47.1 0.8 %maximum_select_fusion = bf16[256,512]{1,0:T(8,128)(2,1)} fusion(bf16[128,512]{1,0:T(8,128)(2,1)S(1)} %collective-permute-done.8, bf16[128,512]{1,0:T(8,128)(2,1)S(1)} %shard_map.112, pred[]{:T(512)S(6)} %eq.6), kind=kLoop, calls=%fused_computation.4 | loop fusion | flops 1179648 | bytes 524289 | tf_op jit(solution)/shard_map/jit(_where)/select_n | solution.py:491
  (23 shorter events, 0.1 us)
Async XLA Ops:
  0.6 7.3 %copy-start.8 = (f32[8]{0:T(128)S(1)}, f32[8]{0:T(128)}, u32[]{:S(2)}) copy-start(f32[8]{0:T(128)} %scale.5) | copy-start | bytes 100
  0.6 7.3 %copy-start = (bf16[512,1536]{1,0:T(8,128)(2,1)S(1)}, bf16[512,1536]{1,0:T(8,128)(2,1)}, u32[]{:S(2)}) copy-start(bf16[512,1536]{1,0:T(8,128)(2,1)} %weights.7) | copy-start | bytes 4718596
  0.7 7.3 %copy-start.6 = (bf16[256,512]{1,0:T(8,128)(2,1)S(1)}, bf16[256,512]{1,0:T(8,128)(2,1)}, u32[]{:S(2)}) copy-start(bf16[256,512]{1,0:T(8,128)(2,1)} %slots_far.1) | copy-start | bytes 786436
  2.0 25.8 %collective-permute-start.3 = (bf16[3,128,512]{2,1,0:T(8,128)(2,1)S(1)}, bf16[3,128,512]{2,1,0:T(8,128)(2,1)S(1)}, u32[]{:S(2)}, u32[]{:S(2)}) collective-permute-start(bf16[3,128,512]{2,1,0:T(8,128)(2,1)S(1)} %get-tuple-element.43), channel_id=1, source_target_pairs={{0,2},{2,0},{4,6},{6,4},{8,10},{10,8},{12,14},{14,12},{1,3},{3,1},... | collective-permute-start | bytes 1179656 | tf_op jit(solution)/shard_map/ppermute | solution.py:402
  5.0 22.7 %collective-permute-start.4 = (bf16[3,128,512]{2,1,0:T(8,128)(2,1)S(1)}, bf16[3,128,512]{2,1,0:T(8,128)(2,1)S(1)}, u32[]{:S(2)}, u32[]{:S(2)}) collective-permute-start(bf16[3,128,512]{2,1,0:T(8,128)(2,1)S(1)} %get-tuple-element.42), channel_id=1, source_target_pairs={{2,4},{4,2},{6,8},{8,6},{10,12},{12,10},{3,5},{5,3},{7,9},{9,7},{1... | collective-permute-start | bytes 1179656 | tf_op jit(solution)/shard_map/ppermute | solution.py:403
  6.6 1.3 %collective-permute-start = (bf16[8,8,512]{2,1,0:T(8,128)(2,1)S(1)}, bf16[8,8,512]{2,1,0:T(8,128)(2,1)S(1)}, u32[]{:S(2)}, u32[]{:S(2)}) collective-permute-start(bf16[8,8,512]{2,1,0:T(8,128)(2,1)S(1)} %slice_select_fusion), channel_id=1, source_target_pairs={{0,1},{1,0},{2,3},{3,2},{4,5},{5,4},{6,7},{7,6},{8,9},{9,8},{10,11... | collective-permute-start | bytes 196616 | tf_op jit(solution)/shard_map/ppermute | solution.py:404
  7.9 1.2 %copy-start.1 = (bf16[8,128,512]{2,1,0:T(8,128)(2,1)S(1)}, bf16[8,128,512]{2,1,0:T(8,128)(2,1)}, u32[]{:S(2)}) copy-start(bf16[8,128,512]{2,1,0:T(8,128)(2,1)} %x.5) | copy-start | bytes 3145732
  9.1 1.0 %copy-start.4 = (bf16[512,512]{1,0:T(8,128)(2,1)S(1)}, bf16[512,512]{1,0:T(8,128)(2,1)}, u32[]{:S(2)}) copy-start(bf16[512,512]{1,0:T(8,128)(2,1)} %asking_far.1) | copy-start | bytes 1572868
  10.2 0.7 %copy-start.7 = (f32[512]{0:T(512)S(1)}, f32[512]{0:T(512)}, u32[]{:S(2)}) copy-start(f32[512]{0:T(512)} %param.10) | copy-start | bytes 6148
  10.9 0.7 %copy-start.9 = (f32[512]{0:T(512)S(1)}, f32[512]{0:T(512)}, u32[]{:S(2)}) copy-start(f32[512]{0:T(512)} %param.14) | copy-start | bytes 6148
  11.6 11.5 %copy-start.2 = (bf16[8,128,512]{2,1,0:T(8,128)(2,1)S(1)}, bf16[8,128,512]{2,1,0:T(8,128)(2,1)}, u32[]{:S(2)}) copy-start(bf16[8,128,512]{2,1,0:T(8,128)(2,1)} %x.5) | copy-start | bytes 3145732
  18.2 1.4 %collective-permute-start.1 = (bf16[144,512]{1,0:T(8,128)(2,1)S(1)}, bf16[144,512]{1,0:T(8,128)(2,1)S(1)}, u32[]{:S(2)}, u32[]{:S(2)}) collective-permute-start(bf16[144,512]{1,0:T(8,128)(2,1)S(1)} %get-tuple-element.24), channel_id=1, source_target_pairs={{0,1},{1,0},{2,3},{3,2},{4,5},{5,4},{6,7},{7,6},{8,9},{9,8},{10,11... | collective-permute-start | bytes 442376 | tf_op jit(solution)/shard_map/ppermute | solution.py:437
  20.2 7.0 %collective-permute-start.2 = (bf16[144,512]{1,0:T(8,128)(2,1)S(1)}, bf16[144,512]{1,0:T(8,128)(2,1)S(1)}, u32[]{:S(2)}, u32[]{:S(2)}) collective-permute-start(bf16[144,512]{1,0:T(8,128)(2,1)S(1)} %shard_map.105.a), channel_id=1, source_target_pairs={{0,4},{2,6},{4,0},{6,2},{8,12},{10,14},{12,8},{14,10},{1,5},{3,7},... | collective-permute-start | bytes 442376 | tf_op jit(solution)/shard_map/ppermute | solution.py:448
  27.7 9.7 %collective-permute-start.5 = (bf16[144,512]{1,0:T(8,128)(2,1)S(1)}, bf16[144,512]{1,0:T(8,128)(2,1)S(1)}, u32[]{:S(2)}, u32[]{:S(2)}) collective-permute-start(bf16[144,512]{1,0:T(8,128)(2,1)S(1)} %shard_map.106.a), channel_id=1, source_target_pairs={{0,8},{2,10},{4,12},{6,14},{8,0},{10,2},{12,4},{14,6},{1,9},{3,11}... | collective-permute-start | bytes 442376 | tf_op jit(solution)/shard_map/ppermute | solution.py:448
  31.0 1.9 %copy-start.3 = (bf16[512,512]{1,0:T(8,128)(2,1)S(1)}, bf16[512,512]{1,0:T(8,128)(2,1)}, u32[]{:S(2)}) copy-start(bf16[512,512]{1,0:T(8,128)(2,1)} %exits.4) | copy-start | bytes 1572868
  31.1 1.8 %collective-permute-start.6 = (bf16[6,8,512]{2,1,0:T(8,128)(2,1)S(1)}, bf16[6,8,512]{2,1,0:T(8,128)(2,1)S(1)}, u32[]{:S(2)}, u32[]{:S(2)}) collective-permute-start(bf16[6,8,512]{2,1,0:T(8,128)(2,1)S(1)} %pad_maximum_fusion), channel_id=1, source_target_pairs={{0,1},{1,0},{2,3},{3,2},{4,5},{5,4},{6,7},{7,6},{8,9},{9,8},{10,11... | collective-permute-start | bytes 147464 | tf_op jit(solution)/shard_map/ppermute | solution.py:447
  38.0 7.1 %copy-start.5 = (bf16[512,512]{1,0:T(8,128)(2,1)S(1)}, bf16[512,512]{1,0:T(8,128)(2,1)}, u32[]{:S(2)}) copy-start(bf16[512,512]{1,0:T(8,128)(2,1)} %exits.5) | copy-start | bytes 1572868
  38.0 7.1 %collective-permute-start.7 = (bf16[144,512]{1,0:T(8,128)(2,1)S(1)}, bf16[144,512]{1,0:T(8,128)(2,1)S(1)}, u32[]{:S(2)}, u32[]{:S(2)}) collective-permute-start(bf16[144,512]{1,0:T(8,128)(2,1)S(1)} %shard_map.110.a), channel_id=1, source_target_pairs={{0,2},{2,0},{4,6},{6,4},{8,10},{10,8},{12,14},{14,12},{1,3},{3,1},... | collective-permute-start | bytes 442376 | tf_op jit(solution)/shard_map/ppermute | solution.py:483
  45.7 1.4 %collective-permute-start.8 = (bf16[128,512]{1,0:T(8,128)(2,1)S(1)}, bf16[128,512]{1,0:T(8,128)(2,1)S(1)}, u32[]{:S(2)}, u32[]{:S(2)}) collective-permute-start(bf16[128,512]{1,0:T(8,128)(2,1)S(1)} %shard_map.112), channel_id=1, source_target_pairs={{0,1},{1,0},{2,3},{3,2},{4,5},{5,4},{6,7},{7,6},{8,9},{9,8},{10,11... | collective-permute-start | bytes 393224 | tf_op jit(solution)/shard_map/ppermute | solution.py:490

commit v3 on v2

--- a/solution.py
+++ b/solution.py
@@ -207,6 +207,10 @@
     return jnp.concatenate([own, rim], axis=1).astype(BF16)
 
 
+def copy_kernel(a, b):
+    b[...] = a[...]
+
+
 def own_kernel(x, side, gain, weights, keys, values, queries, key_win, value_win):
     rows, cols, width = x.shape
     channels = width // H
@@ -354,7 +358,7 @@
             tokens_out[here, at] = total.astype(BF16)
 
 
-def call(kernel, outs, ins, scratch=(), megabytes=16, smem=0, far=()):
+def call(kernel, outs, ins, scratch=(), megabytes=16, smem=0, far=(), flops=1000):
     shapes = [jax.ShapeDtypeStruct(*o) for o in outs]
     return pl.pallas_call(
         kernel,
@@ -363,7 +367,7 @@
         out_specs=[VMEM] * len(shapes),
         scratch_shapes=list(scratch),
         compiler_params=pltpu.CompilerParams(vmem_limit_bytes=megabytes * 1024 * 1024),
-        cost_estimate=pl.CostEstimate(flops=1000, bytes_accessed=1000, transcendentals=0),
+        cost_estimate=pl.CostEstimate(flops=flops, bytes_accessed=1000, transcendentals=0),
     )(*ins)
 
 
@@ -401,7 +405,8 @@
     top, bottom = (x[:RIM], x[rows - RIM :])
     near_rim = lax.ppermute(jnp.where(odd, top, bottom), "rows", near)
     far_rim = lax.ppermute(jnp.where(odd, bottom, top), "rows", far)
-    side = lax.ppermute(edge(x), "cols", swap)
+    (side,) = call(copy_kernel, [((rows, BLK, width), BF16)], (edge(x),), megabytes=2, flops=10**10)
+    side = lax.ppermute(side, "cols", swap)
     place, side = lax.optimization_barrier((place, side))
 
     half = latents // 2

time: 48.2 us -> 44.6 us (0.925)
  local copies, waits for them, and re-layouts: 3.75 us -> 0.33 us
  other arithmetic: 3.03 us -> 4.1 us
  waiting for transfers between devices: 6.56 us -> 5.67 us
    unnamed x20 -> x18, local copies, waits for them, and re-layouts: 3.65 us -> 0.22 us
    select_n x1, other arithmetic: 0.06 us -> 1.17 us  [per_device(): up = jnp.where(odd, near_rim, far_rim)]
    ppermute x2, waiting for transfers between devices: 2.87 us -> 1.84 us  [per_device(): parts = [whole, lax.ppermute(whole, 'rows', pairs)]]
    select_n x2, other arithmetic: 0.9 us -> 0.02 us  [edge(): return jnp.where(col == 0, array[:, cols - BLK:], array[:, :BLK])]
    select_n x1, other arithmetic: 1.3 us -> 2.13 us  [per_device(): far_rim = lax.ppermute(jnp.where(odd, bottom, top), 'rows', far)]
    ppermute x1, starting transfers between devices: 0.67 us -> 1.43 us  [per_device(): far_rim = lax.ppermute(jnp.where(odd, bottom, top), 'rows', far)]
    ppermute x2, starting transfers between devices: 6.03 us -> 5.3 us  [per_device(): parts = [whole, lax.ppermute(whole, 'rows', pairs)]]
    pallas_call x9 -> x10, Pallas kernels: 20.8 us -> 20.8 us  [call(): pl.pallas_call(kernel, out_shape=shapes, in_specs=[SMEM if n < smem else...]
  transfers between devices with their start and end apart: 9 -> 9, of which waited for: 5 -> 5; matrix products, arithmetic and copies ran while one was open for 2% -> 3% of each run, Pallas kernels for 41% -> 44%
where the time goes in v3:
time: 44.6 us; the launch traced here: 44.4 us
  Pallas kernels  20.8 us (47%)
  starting transfers between devices  12.6 us (28%)
  waiting for transfers between devices  5.67 us (13%)
  other arithmetic  4.1 us (9%)
  between operations  0.86 us (2%)
    pallas_call x10, Pallas kernels, call(): pl.pallas_call(kernel, out_shape=shapes, in_specs=[SMEM if n < smem else...  20.8 us
    ppermute x2, starting transfers between devices, per_device(): parts = [whole, lax.ppermute(whole, 'rows', pairs)]  5.3 us
    ppermute x1, starting transfers between devices, per_device(): near_rim = lax.ppermute(jnp.where(odd, top, bottom), 'rows', near)  2.97 us
    ppermute x1, starting transfers between devices, per_device(): got = lax.ppermute(whole, 'rows', pairs)  2.62 us
    select_n x1, other arithmetic, per_device(): far_rim = lax.ppermute(jnp.where(odd, bottom, top), 'rows', far)  2.13 us
    ppermute x2, waiting for transfers between devices, per_device(): parts = [whole, lax.ppermute(whole, 'rows', pairs)]  1.84 us
    ppermute x1, starting transfers between devices, per_device(): far_rim = lax.ppermute(jnp.where(odd, bottom, top), 'rows', far)  1.43 us
    ppermute x1, waiting for transfers between devices, per_device(): parts = [mine, lax.ppermute(other, 'cols', swap)]  1.36 us
  transfers between devices with their start and end apart: 9, of which 5 were waited for; matrix products, arithmetic and copies ran while one was open for 3% of the time, Pallas kernels for 44%

profile of v3, /device:TPU:0, one launch (start us, length us, event | category | flops | bytes accessed | tf_op | source)
XLA Modules:
  0.0 44.4 jit_solution(14001785004974953562)
XLA Ops:
  0.7 2.1 %broadcast_select_fusion.2 = (bf16[3,128,512]{2,1,0:T(8,128)(2,1)}, bf16[3,128,512]{2,1,0:T(8,128)(2,1)}) fusion(pred[]{:T(512)S(6)} %eq.12, bf16[8,128,512]{2,1,0:T(8,128)(2,1)} %x.5), kind=kLoop, calls=%fused_computation.2 | loop fusion | flops 393216 | bytes 1572865 | tf_op jit(solution)/shard_map/jit(_where)/select_n | solution.py:407
  2.8 3.0 %collective-permute-start.3 = (bf16[3,128,512]{2,1,0:T(8,128)(2,1)}, bf16[3,128,512]{2,1,0:T(8,128)(2,1)}, u32[]{:S(2)}, u32[]{:S(2)}) collective-permute-start(bf16[3,128,512]{2,1,0:T(8,128)(2,1)} %get-tuple-element.43), channel_id=1, source_target_pairs={{0,2},{2,0},{4,6},{6,4},{8,10},{10,8},{12,14},{14,12},{1,3},{3,1},... | collective-permute-start | bytes 1179656 | tf_op jit(solution)/shard_map/ppermute | solution.py:406
  5.8 1.4 %collective-permute-start.4 = (bf16[3,128,512]{2,1,0:T(8,128)(2,1)}, bf16[3,128,512]{2,1,0:T(8,128)(2,1)}, u32[]{:S(2)}, u32[]{:S(2)}) collective-permute-start(bf16[3,128,512]{2,1,0:T(8,128)(2,1)} %get-tuple-element.42), channel_id=1, source_target_pairs={{2,4},{4,2},{6,8},{8,6},{10,12},{12,10},{3,5},{5,3},{7,9},{9,7},{1... | collective-permute-start | bytes 1179656 | tf_op jit(solution)/shard_map/ppermute | solution.py:407
  7.2 0.0 copy-start
  7.3 0.1 collective-permute-start
  7.4 0.1 stack.20
  7.5 1.1 %collective-permute-done.side = bf16[8,8,512]{2,1,0:T(8,128)(2,1)S(1)} collective-permute-done((bf16[8,8,512]{2,1,0:T(8,128)(2,1)S(1)}, bf16[8,8,512]{2,1,0:T(8,128)(2,1)S(1)}, u32[]{:S(2)}, u32[]{:S(2)}) %collective-permute-start) | collective-permute-done | bytes 65568 | tf_op jit(solution)/shard_map/ppermute | solution.py:409
  8.6 0.0 copy-done
  8.6 0.1 copy-done.3
  8.7 0.1 copy-done.5
  8.8 6.6 %shard_map.105 = (bf16[1024,512]{1,0:T(8,128)(2,1)S(1)}, bf16[1024,512]{1,0:T(8,128)(2,1)S(1)}, bf16[144,512]{1,0:T(8,128)(2,1)S(1)}, bf16[144,512]{1,0:T(8,128)(2,1)S(1)}) custom-call(f32[8]{0:T(128)S(1)} %copy-done.7, s32[5]{0:T(128)S(1)} %convert_element_type.3.place, bf16[8,128,512]{2,1,0:T(8,128)(2,1)S(1)} %copy-done.1, f32[1,512]{1,0:T(1,128)S(1)} %bitcast.6, ...), custom_call_target="tpu_custom_call" | custom-call | flops 1000 | bytes 1000 | tf_op jit(solution)/shard_map/pallas_call | solution.py:363
  15.4 0.1 collective-permute-start.1
  15.5 1.4 %collective-permute-done.1.b = bf16[144,512]{1,0:T(8,128)(2,1)S(1)} collective-permute-done((bf16[144,512]{1,0:T(8,128)(2,1)S(1)}, bf16[144,512]{1,0:T(8,128)(2,1)S(1)}, u32[]{:S(2)}, u32[]{:S(2)}) %collective-permute-start.1) | collective-permute-done | bytes 147488 | tf_op jit(solution)/shard_map/ppermute | solution.py:442
  16.9 0.5 %shard_map.106.a = bf16[144,512]{1,0:T(8,128)(2,1)S(1)} custom-call(bf16[144,512]{1,0:T(8,128)(2,1)S(1)} %get-tuple-element.23.a, bf16[144,512]{1,0:T(8,128)(2,1)S(1)} %collective-permute-done.1.b), custom_call_target="tpu_custom_call" | custom-call | flops 1000 | bytes 1000 | tf_op jit(solution)/shard_map/pallas_call | solution.py:363
  17.4 2.1 %collective-permute-start.2 = (bf16[144,512]{1,0:T(8,128)(2,1)S(1)}, bf16[144,512]{1,0:T(8,128)(2,1)S(1)}, u32[]{:S(2)}, u32[]{:S(2)}) collective-permute-start(bf16[144,512]{1,0:T(8,128)(2,1)S(1)} %shard_map.106.a), channel_id=1, source_target_pairs={{0,4},{2,6},{4,0},{6,2},{8,12},{10,14},{12,8},{14,10},{1,5},{3,7},... | collective-permute-start | bytes 442376 | tf_op jit(solution)/shard_map/ppermute | solution.py:453
  19.5 2.6 %shard_map.108 = (bf16[16,64,512]{2,1,0:T(8,128)(2,1)S(1)}, bf16[8,16,16,512]{3,2,1,0:T(8,128)(2,1)S(1)}, bf16[8,16,16,512]{3,2,1,0:T(8,128)(2,1)S(1)}) custom-call(bf16[8,128,512]{2,1,0:T(8,128)(2,1)S(1)} %copy-done.1, bf16[8,8,512]{2,1,0:T(8,128)(2,1)S(1)} %collective-permute-done.side, f32[1,512]{1,0:T(1,128)S(1)} %bitcast.7, ...), custom_call_target="tpu_custom_call" | custom-call | flops 1000 | bytes 1000 | tf_op jit(solution)/shard_map/pallas_call | solution.py:363
  22.1 1.5 %collective-permute-done.2.b = bf16[144,512]{1,0:T(8,128)(2,1)S(1)} collective-permute-done((bf16[144,512]{1,0:T(8,128)(2,1)S(1)}, bf16[144,512]{1,0:T(8,128)(2,1)S(1)}, u32[]{:S(2)}, u32[]{:S(2)}) %collective-permute-start.2) | collective-permute-done | bytes 147488 | tf_op jit(solution)/shard_map/ppermute | solution.py:453
  23.7 0.5 %shard_map.107.a = bf16[144,512]{1,0:T(8,128)(2,1)S(1)} custom-call(bf16[144,512]{1,0:T(8,128)(2,1)S(1)} %shard_map.106.a, bf16[144,512]{1,0:T(8,128)(2,1)S(1)} %collective-permute-done.2.b), custom_call_target="tpu_custom_call" | custom-call | flops 1000 | bytes 1000 | tf_op jit(solution)/shard_map/pallas_call | solution.py:363
  24.2 0.0 collective-permute-done.4
  24.2 3.2 %collective-permute-start.5 = (bf16[144,512]{1,0:T(8,128)(2,1)S(1)}, bf16[144,512]{1,0:T(8,128)(2,1)S(1)}, u32[]{:S(2)}, u32[]{:S(2)}) collective-permute-start(bf16[144,512]{1,0:T(8,128)(2,1)S(1)} %shard_map.107.a), channel_id=1, source_target_pairs={{0,8},{2,10},{4,12},{6,14},{8,0},{10,2},{12,4},{14,6},{1,9},{3,11}... | collective-permute-start | bytes 442376 | tf_op jit(solution)/shard_map/ppermute | solution.py:453
  27.4 1.2 %broadcast_select_fusion.1 = (bf16[3,128,512]{2,1,0:T(8,128)(2,1)S(1)}, bf16[3,128,512]{2,1,0:T(8,128)(2,1)S(1)}) fusion(bf16[3,128,512]{2,1,0:T(8,128)(2,1)} %collective-permute-done.3, bf16[3,128,512]{2,1,0:T(8,128)(2,1)} %collective-permute-done.4, pred[]{:T(512)S(6)} %eq.12), kind=kLoop, calls=%fused_computation.1 | loop fusion | flops 393216 | bytes 1572865 | tf_op jit(solution)/shard_map/jit(_where)/select_n | solution.py:450
  28.7 0.1 collective-permute-start.6
  28.7 1.7 %shard_map.109 = (bf16[6,16,16,512]{3,2,1,0:T(8,128)(2,1)S(1)}, bf16[6,16,16,512]{3,2,1,0:T(8,128)(2,1)S(1)}) custom-call(bf16[3,128,512]{2,1,0:T(8,128)(2,1)S(1)} %get-tuple-element.44.up, bf16[3,128,512]{2,1,0:T(8,128)(2,1)S(1)} %get-tuple-element.45.down, f32[1,512]{1,0:T(1,128)S(1)} %bitcast.8, bf16[512,1536]{1,0:T(8,128)(2,1)S(1)} %copy-done), custom_call_target="tpu_custom_call" | custom-call | flops 1000 | bytes 1000 | tf_op jit(solution)/shard_map/pallas_call | solution.py:363
  30.5 3.2 %shard_map.110.refs_0_ = bf16[8,64,512]{2,1,0:T(8,128)(2,1)S(1)} custom-call(f32[8]{0:T(128)S(1)} %copy-done.7, s32[5]{0:T(128)S(1)} %convert_element_type.3.place, bf16[8,128,512]{2,1,0:T(8,128)(2,1)S(1)} %copy-done.1, bf16[6,8,512]{2,1,0:T(8,128)(2,1)S(1)} %collective-permute-done.6.corner, f32[1,512]{1,0:T(1,128)S(1)} %bitcast.9, ...), custom_call_target="tpu_custom_call" | custom-call | flops 1000 | bytes 1000 | tf_op jit(solution)/shard_map/pallas_call | solution.py:363
  33.7 0.3 collective-permute-done.5.b
  34.0 0.5 %shard_map.111.a = bf16[144,512]{1,0:T(8,128)(2,1)S(1)} custom-call(bf16[144,512]{1,0:T(8,128)(2,1)S(1)} %shard_map.107.a, bf16[144,512]{1,0:T(8,128)(2,1)S(1)} %collective-permute-done.5.b), custom_call_target="tpu_custom_call" | custom-call | flops 1000 | bytes 1000 | tf_op jit(solution)/shard_map/pallas_call | solution.py:363
  34.6 2.6 %collective-permute-start.7 = (bf16[144,512]{1,0:T(8,128)(2,1)S(1)}, bf16[144,512]{1,0:T(8,128)(2,1)S(1)}, u32[]{:S(2)}, u32[]{:S(2)}) collective-permute-start(bf16[144,512]{1,0:T(8,128)(2,1)S(1)} %shard_map.111.a), channel_id=1, source_target_pairs={{0,2},{2,0},{4,6},{6,4},{8,10},{10,8},{12,14},{14,12},{1,3},{3,1},... | collective-permute-start | bytes 442376 | tf_op jit(solution)/shard_map/ppermute | solution.py:488
  37.2 4.3 %shard_map.112 = bf16[8,128,512]{2,1,0:T(8,128)(2,1)} custom-call(f32[8]{0:T(128)S(1)} %copy-done.7, s32[5]{0:T(128)S(1)} %convert_element_type.3.place, bf16[8,128,512]{2,1,0:T(8,128)(2,1)S(1)} %copy-done.1, bf16[6,8,512]{2,1,0:T(8,128)(2,1)S(1)} %collective-permute-done.6.corner, f32[1,512]{1,0:T(1,128)S(1)} %bitcast.10, bf16[512,1536]{1,0:T(8,128)(2,1)S(1)} %copy-done, ...), custom_call_target="tpu_custom_call" | custom-call | flops 1000 | bytes 1000 | tf_op jit(solution)/shard_map/pallas_call | solution.py:363
  41.6 0.6 %shard_map.113 = bf16[128,512]{1,0:T(8,128)(2,1)S(1)} custom-call(bf16[144,512]{1,0:T(8,128)(2,1)S(1)} %shard_map.111.a, bf16[144,512]{1,0:T(8,128)(2,1)S(1)} %collective-permute-done.7.b, bf16[512,512]{1,0:T(8,128)(2,1)S(1)} %copy-done.4), custom_call_target="tpu_custom_call" | custom-call | flops 1000 | bytes 1000 | tf_op jit(solution)/shard_map/pallas_call | solution.py:363
  42.2 0.1 collective-permute-start.8
  42.3 1.3 %collective-permute-done.8 = bf16[128,512]{1,0:T(8,128)(2,1)S(1)} collective-permute-done((bf16[128,512]{1,0:T(8,128)(2,1)S(1)}, bf16[128,512]{1,0:T(8,128)(2,1)S(1)}, u32[]{:S(2)}, u32[]{:S(2)}) %collective-permute-start.8) | collective-permute-done | bytes 131104 | tf_op jit(solution)/shard_map/ppermute | solution.py:495
  43.6 0.8 %maximum_select_fusion = bf16[256,512]{1,0:T(8,128)(2,1)} fusion(bf16[128,512]{1,0:T(8,128)(2,1)S(1)} %collective-permute-done.8, bf16[128,512]{1,0:T(8,128)(2,1)S(1)} %shard_map.113, pred[]{:T(512)S(6)} %eq.6), kind=kLoop, calls=%fused_computation.4 | loop fusion | flops 1179648 | bytes 524289 | tf_op jit(solution)/shard_map/jit(_where)/select_n | solution.py:496
  (22 shorter events, 0.1 us)
Async XLA Ops:
  0.6 6.6 %copy-start.1 = (bf16[8,128,512]{2,1,0:T(8,128)(2,1)S(1)}, bf16[8,128,512]{2,1,0:T(8,128)(2,1)}, u32[]{:S(2)}) copy-start(bf16[8,128,512]{2,1,0:T(8,128)(2,1)} %x.5) | copy-start | bytes 3145732
  2.8 21.4 %collective-permute-start.3 = (bf16[3,128,512]{2,1,0:T(8,128)(2,1)}, bf16[3,128,512]{2,1,0:T(8,128)(2,1)}, u32[]{:S(2)}, u32[]{:S(2)}) collective-permute-start(bf16[3,128,512]{2,1,0:T(8,128)(2,1)} %get-tuple-element.43), channel_id=1, source_target_pairs={{0,2},{2,0},{4,6},{6,4},{8,10},{10,8},{12,14},{14,12},{1,3},{3,1},... | collective-permute-start | bytes 1179656 | tf_op jit(solution)/shard_map/ppermute | solution.py:406
  5.8 18.5 %collective-permute-start.4 = (bf16[3,128,512]{2,1,0:T(8,128)(2,1)}, bf16[3,128,512]{2,1,0:T(8,128)(2,1)}, u32[]{:S(2)}, u32[]{:S(2)}) collective-permute-start(bf16[3,128,512]{2,1,0:T(8,128)(2,1)} %get-tuple-element.42), channel_id=1, source_target_pairs={{2,4},{4,2},{6,8},{8,6},{10,12},{12,10},{3,5},{5,3},{7,9},{9,7},{1... | collective-permute-start | bytes 1179656 | tf_op jit(solution)/shard_map/ppermute | solution.py:407
  7.2 1.4 %copy-start = (bf16[512,1536]{1,0:T(8,128)(2,1)S(1)}, bf16[512,1536]{1,0:T(8,128)(2,1)}, u32[]{:S(2)}) copy-start(bf16[512,1536]{1,0:T(8,128)(2,1)} %weights.7) | copy-start | bytes 4718596
  7.2 1.5 %copy-start.3 = (bf16[512,512]{1,0:T(8,128)(2,1)S(1)}, bf16[512,512]{1,0:T(8,128)(2,1)}, u32[]{:S(2)}) copy-start(bf16[512,512]{1,0:T(8,128)(2,1)} %asking_far.1) | copy-start | bytes 1572868
  7.2 1.6 %copy-start.5 = (bf16[256,512]{1,0:T(8,128)(2,1)S(1)}, bf16[256,512]{1,0:T(8,128)(2,1)}, u32[]{:S(2)}) copy-start(bf16[256,512]{1,0:T(8,128)(2,1)} %slots_far.1) | copy-start | bytes 786436
  7.2 1.5 %copy-start.6 = (f32[512]{0:T(512)S(1)}, f32[512]{0:T(512)}, u32[]{:S(2)}) copy-start(f32[512]{0:T(512)} %param.10) | copy-start | bytes 6148
  7.2 1.5 %copy-start.7 = (f32[8]{0:T(128)S(1)}, f32[8]{0:T(128)}, u32[]{:S(2)}) copy-start(f32[8]{0:T(128)} %scale.5) | copy-start | bytes 100
  7.3 1.5 %copy-start.8 = (f32[512]{0:T(512)S(1)}, f32[512]{0:T(512)}, u32[]{:S(2)}) copy-start(f32[512]{0:T(512)} %param.14) | copy-start | bytes 6148
  7.3 1.3 %collective-permute-start = (bf16[8,8,512]{2,1,0:T(8,128)(2,1)S(1)}, bf16[8,8,512]{2,1,0:T(8,128)(2,1)S(1)}, u32[]{:S(2)}, u32[]{:S(2)}) collective-permute-start(bf16[8,8,512]{2,1,0:T(8,128)(2,1)S(1)} %shard_map.104), channel_id=1, source_target_pairs={{0,1},{1,0},{2,3},{3,2},{4,5},{5,4},{6,7},{7,6},{8,9},{9,8},{10,11... | collective-permute-start | bytes 196616 | tf_op jit(solution)/shard_map/ppermute | solution.py:409
  15.4 1.4 %collective-permute-start.1 = (bf16[144,512]{1,0:T(8,128)(2,1)S(1)}, bf16[144,512]{1,0:T(8,128)(2,1)S(1)}, u32[]{:S(2)}, u32[]{:S(2)}) collective-permute-start(bf16[144,512]{1,0:T(8,128)(2,1)S(1)} %get-tuple-element.24), channel_id=1, source_target_pairs={{0,1},{1,0},{2,3},{3,2},{4,5},{5,4},{6,7},{7,6},{8,9},{9,8},{10,11... | collective-permute-start | bytes 442376 | tf_op jit(solution)/shard_map/ppermute | solution.py:442
  17.4 6.3 %collective-permute-start.2 = (bf16[144,512]{1,0:T(8,128)(2,1)S(1)}, bf16[144,512]{1,0:T(8,128)(2,1)S(1)}, u32[]{:S(2)}, u32[]{:S(2)}) collective-permute-start(bf16[144,512]{1,0:T(8,128)(2,1)S(1)} %shard_map.106.a), channel_id=1, source_target_pairs={{0,4},{2,6},{4,0},{6,2},{8,12},{10,14},{12,8},{14,10},{1,5},{3,7},... | collective-permute-start | bytes 442376 | tf_op jit(solution)/shard_map/ppermute | solution.py:453
  24.2 9.8 %collective-permute-start.5 = (bf16[144,512]{1,0:T(8,128)(2,1)S(1)}, bf16[144,512]{1,0:T(8,128)(2,1)S(1)}, u32[]{:S(2)}, u32[]{:S(2)}) collective-permute-start(bf16[144,512]{1,0:T(8,128)(2,1)S(1)} %shard_map.107.a), channel_id=1, source_target_pairs={{0,8},{2,10},{4,12},{6,14},{8,0},{10,2},{12,4},{14,6},{1,9},{3,11}... | collective-permute-start | bytes 442376 | tf_op jit(solution)/shard_map/ppermute | solution.py:453
  28.6 1.9 %copy-start.2 = (bf16[512,512]{1,0:T(8,128)(2,1)S(1)}, bf16[512,512]{1,0:T(8,128)(2,1)}, u32[]{:S(2)}) copy-start(bf16[512,512]{1,0:T(8,128)(2,1)} %exits.4) | copy-start | bytes 1572868
  28.7 1.8 %collective-permute-start.6 = (bf16[6,8,512]{2,1,0:T(8,128)(2,1)S(1)}, bf16[6,8,512]{2,1,0:T(8,128)(2,1)S(1)}, u32[]{:S(2)}, u32[]{:S(2)}) collective-permute-start(bf16[6,8,512]{2,1,0:T(8,128)(2,1)S(1)} %pad_maximum_fusion), channel_id=1, source_target_pairs={{0,1},{1,0},{2,3},{3,2},{4,5},{5,4},{6,7},{7,6},{8,9},{9,8},{10,11... | collective-permute-start | bytes 147464 | tf_op jit(solution)/shard_map/ppermute | solution.py:452
  34.6 7.0 %copy-start.4 = (bf16[512,512]{1,0:T(8,128)(2,1)S(1)}, bf16[512,512]{1,0:T(8,128)(2,1)}, u32[]{:S(2)}) copy-start(bf16[512,512]{1,0:T(8,128)(2,1)} %exits.5) | copy-start | bytes 1572868
  34.6 7.0 %collective-permute-start.7 = (bf16[144,512]{1,0:T(8,128)(2,1)S(1)}, bf16[144,512]{1,0:T(8,128)(2,1)S(1)}, u32[]{:S(2)}, u32[]{:S(2)}) collective-permute-start(bf16[144,512]{1,0:T(8,128)(2,1)S(1)} %shard_map.111.a), channel_id=1, source_target_pairs={{0,2},{2,0},{4,6},{6,4},{8,10},{10,8},{12,14},{14,12},{1,3},{3,1},... | collective-permute-start | bytes 442376 | tf_op jit(solution)/shard_map/ppermute | solution.py:488
  42.2 1.4 %collective-permute-start.8 = (bf16[128,512]{1,0:T(8,128)(2,1)S(1)}, bf16[128,512]{1,0:T(8,128)(2,1)S(1)}, u32[]{:S(2)}, u32[]{:S(2)}) collective-permute-start(bf16[128,512]{1,0:T(8,128)(2,1)S(1)} %shard_map.113), channel_id=1, source_target_pairs={{0,1},{1,0},{2,3},{3,2},{4,5},{5,4},{6,7},{7,6},{8,9},{9,8},{10,11... | collective-permute-start | bytes 393224 | tf_op jit(solution)/shard_map/ppermute | solution.py:495

commit v4 on v3

--- a/solution.py
+++ b/solution.py
@@ -49,46 +49,19 @@
 
 
 def latent_kernel(
-    scale,
-    place,
-    x_far,
-    gain,
-    weights_far,
-    slots_far,
-    slot_gain,
-    asking_far,
-    keys,
-    values,
-    mine,
-    other,
-    x,
-    weights,
-    slots,
-    asking,
-    sems,
+    scale, place, x, gain, weights, slots, slot_gain, asking, keys, values, mine, other
 ):
     rows, cols, width = x.shape
     heads = H
     channels = width // heads
     latents = slots.shape[0]
-    copies = [(slots_far, slots), (asking_far, asking)]
-    copies += [(weights_far.at[:, width:], weights), (x_far, x)]
-    copies = [
-        pltpu.make_async_copy(far, near, sems.at[n]) for n, (far, near) in enumerate(copies)
-    ]
-    for copy in copies:
-        copy.start()
     ones = head_ones(256, channels)
-    copies[0].wait()
-    copies[1].wait()
     slot_normed = token_norm(slots[...].astype(F32), slot_gain[...])
     asked = head_norm(dot(slot_normed, asking[...]), ones, channels).astype(BF16)
-    copies[2].wait()
-    copies[3].wait()
     for i in range(rows // 2):
         tokens = x[2 * i : 2 * i + 2].reshape(2 * cols, width).astype(F32)
         normed = token_norm(tokens, gain[...])
-        both = dot(normed, weights[...])
+        both = dot(normed, weights[:, width:])
         here = slice(2 * i * cols, (2 * i + 2) * cols)
         keys[here, :] = head_norm(both[:, :width], ones, channels).astype(BF16)
         values[here, :] = both[:, width:].astype(BF16)
@@ -248,48 +221,43 @@
 
 
 def halo_kernel(
-    scale,
-    place,
-    x,
-    corner,
-    gain,
-    weights,
-    exits,
-    queries,
-    key_win,
-    value_win,
-    key_rim,
-    value_rim,
-    *refs,
-    start,
-    stop,
+    scale, place, x, corner, gain, weights, exits, queries, key_win, value_win, key_rim, value_rim,
+    *refs, parts, stage
 ):
-    if start == 0:
-        attended, key_end, value_end = refs
-    else:
-        earlier, tokens_out, key_end, value_end, attended = refs
     rows, cols, width = x.shape
     channels = width // H
     ones = head_ones(256, channels)
     blocks = cols // BLK
     lines = rows + 2 * RIM
-
-    normed = token_norm(corner[...].reshape(2 * RIM * BLK, width).astype(F32), gain[...])
-    both = dot(normed, weights[:, width:])
-    corner_keys = head_norm(both[:, :width], ones, channels).reshape(2 * RIM, BLK, width)
-    corner_values = both[:, width:].reshape(2 * RIM, BLK, width)
-    sub = lax.broadcasted_iota(jnp.int32, (1, 16, 1), 1)
-    for block, beyond in ((0, sub >= 2 * BLK - RIM), (blocks - 1, sub < BLK + RIM)):
-        if not start <= block < stop:
-            continue
-        beyond = beyond & (sub >= BLK)
-        for rim, tile, end in (
-            (key_rim, corner_keys, key_end),
-            (value_rim, corner_values, value_end),
+    order = parts[stage]
+    if stage == 0:
+        (attended,), key_end, value_end = (refs, None, None)
+    else:
+        first, attended, first_out, key_end, value_end = refs
+        start = BLK * parts[0][0]
+        count = BLK * len(parts[0])
+        for i in range(rows // 4):
+            here = slice(4 * i, 4 * i + 4)
+            branch = dot(first[here].reshape(4 * count, width), exits[...])
+            total = x[here, start : start + count].astype(F32) + branch.reshape(4, count, width)
+            first_out[here] = total.astype(BF16)
+
+        normed = token_norm(corner[...].reshape(2 * RIM * BLK, width).astype(F32), gain[...])
+        both = dot(normed, weights[:, width:])
+        corner_keys = head_norm(both[:, :width], ones, channels).reshape(2 * RIM, BLK, width)
+        corner_values = both[:, width:].reshape(2 * RIM, BLK, width)
+        sub = lax.broadcasted_iota(jnp.int32, (1, 16, 1), 1)
+        for n, (block, beyond) in enumerate(
+            ((0, sub >= 2 * BLK - RIM), (blocks - 1, sub < BLK + RIM))
         ):
-            double = jnp.concatenate([tile, tile], axis=1)
-            kept = rim[:, block].astype(F32)
-            end[...] = jnp.where(beyond, double, kept).astype(BF16)
+            beyond = beyond & (sub >= BLK)
+            for rim, tile, end in (
+                (key_rim, corner_keys, key_end),
+                (value_rim, corner_values, value_end),
+            ):
+                double = jnp.concatenate([tile, tile], axis=1)
+                kept = rim[:, block].astype(F32)
+                end[n] = jnp.where(beyond, double, kept).astype(BF16)
 
     spot = lax.broadcasted_iota(jnp.int32, (1, lines * 16), 1)
     line, sub = (spot // 16, spot % 16)
@@ -316,7 +284,7 @@
 
             def around(win, rim, end):
                 if block == 0 or block == blocks - 1:
-                    far = end[:, :, at]
+                    far = end[min(block, 1), :, :, at]
                 else:
                     far = rim[:, block, :, at]
                 own = win[:, block, :, at].reshape(rows * 16, group)
@@ -343,28 +311,44 @@
             outs.append(out)
         return jnp.concatenate(outs, axis=1).reshape(BLK, BLK, width)
 
-    for i in range((stop - start) // 2):
-        block = start + 2 * i
-        pair = jnp.concatenate([one_block(block), one_block(block + 1)], axis=1)
+    for i in range(len(order) // 2):
+        pair = jnp.concatenate([one_block(order[2 * i]), one_block(order[2 * i + 1])], axis=1)
         attended[:, 16 * i : 16 * i + 16, :] = pair.astype(BF16)
-    if start == 0:
-        return
-    for part, at in ((earlier, slice(0, start * BLK)), (attended, slice(start * BLK, cols))):
-        count = at.stop - at.start
-        for i in range(rows // 4):
-            here = slice(4 * i, 4 * i + 4)
-            branch = dot(part[here].reshape(4 * count, width), exits[...])
-            total = x[here, at].astype(F32) + branch.reshape(4, count, width)
-            tokens_out[here, at] = total.astype(BF16)
-
-
-def call(kernel, outs, ins, scratch=(), megabytes=16, smem=0, far=(), flops=1000):
+
+
+def leave_kernel(x, exits, first, second, tokens_out, total, sems):
+    rows, cols, width = x.shape
+    count = second.shape[1] // 2
+    middle = slice(count, cols - count)
+    copies = [pltpu.make_async_copy(first, tokens_out.at[:, middle], sems.at[0])]
+    copies[0].start()
+    for i in range(rows // 4):
+        here = slice(4 * i, 4 * i + 4)
+        branch = dot(second[here].reshape(8 * count, width), exits[...])
+        branch = branch.reshape(4, 2 * count, width)
+        for n, at in enumerate((slice(0, count), slice(cols - count, cols))):
+            from_x = x[here, at].astype(F32)
+            total[here, n * count : (n + 1) * count] = (
+                from_x + branch[:, n * count : (n + 1) * count]
+            ).astype(BF16)
+            copy = pltpu.make_async_copy(
+                total.at[here, n * count : (n + 1) * count],
+                tokens_out.at[here, at],
+                sems.at[len(copies)],
+            )
+            copy.start()
+            copies.append(copy)
+    for copy in copies:
+        copy.wait()
+
+
+def call(kernel, outs, ins, scratch=(), megabytes=16, smem=0, far_outs=(), flops=1000):
     shapes = [jax.ShapeDtypeStruct(*o) for o in outs]
     return pl.pallas_call(
         kernel,
         out_shape=shapes,
-        in_specs=[SMEM if n < smem else HBM if n in far else VMEM for n in range(len(ins))],
-        out_specs=[VMEM] * len(shapes),
+        in_specs=[SMEM] * smem + [VMEM] * (len(ins) - smem),
+        out_specs=[HBM if n in far_outs else VMEM for n in range(len(outs))],
         scratch_shapes=list(scratch),
         compiler_params=pltpu.CompilerParams(vmem_limit_bytes=megabytes * 1024 * 1024),
         cost_estimate=pl.CostEstimate(flops=flops, bytes_accessed=1000, transcendentals=0),
@@ -387,14 +371,14 @@
     latents = memory_slots.shape[0]
     tall, wide = (lax.axis_size("rows"), lax.axis_size("cols"))
     row, col = (lax.axis_index("rows"), lax.axis_index("cols"))
-    place = jnp.stack([row > 0, row < tall - 1, col > 0, col < wide - 1, col > 0])
+    odd = row % 2 == 1
+    place = jnp.stack([row > 0, row < tall - 1, col > 0, col < wide - 1, col > 0, odd])
     place = place.astype(jnp.int32)
     scale = branch_logit_multiplier
     gain = pixel_layernorm_gain.reshape(1, width)
     slot_gain = memory_layernorm_gain.reshape(1, width)
     weights = triple_projection_matrix
 
-    odd = row % 2 == 1
     near = [(i, i ^ 1) for i in range(tall)]
     far = [(i, j) for i in range(tall) if 0 <= (j := i - 1 if i % 2 == 0 else i + 1) < tall]
     swap = [(0, 1), (1, 0)]
@@ -417,16 +401,8 @@
         latent_kernel,
         [((tokens, width), BF16), ((tokens, width), BF16), part, part],
         (scale, place, x, gain, weights, memory_slots, slot_gain, memory_asking_matrix),
-        scratch=[
-            pltpu.VMEM(x.shape, BF16),
-            pltpu.VMEM((width, 2 * width), BF16),
-            pltpu.VMEM(memory_slots.shape, BF16),
-            pltpu.VMEM(memory_asking_matrix.shape, BF16),
-            pltpu.SemaphoreType.DMA((4,)),
-        ],
         megabytes=24,
         smem=2,
-        far=(2, 4, 5, 7),
     )
     queries, key_win, value_win = call(
         own_kernel,
@@ -454,16 +430,21 @@
 
     rim = ((2 * RIM, blocks, 16, width), BF16)
     key_rim, value_rim = call(rim_kernel, [rim, rim], (up, down, gain, weights), megabytes=16)
-
-    def halo(start, stop, outs, earlier, more):
+    rest = blocks // 4
+    parts_of = (
+        list(range(rest, blocks - rest)),
+        list(range(rest)) + list(range(blocks - rest, blocks)),
+    )
+
+    def halo(stage, outs, earlier=()):
         return call(
-            functools.partial(halo_kernel, start=start, stop=stop),
-            outs,
+            functools.partial(halo_kernel, parts=parts_of, stage=stage),
+            [(shape, BF16) for shape in outs],
             (
                 scale,
                 place,
                 x,
-                corner,
+                corner if stage else gain,
                 gain,
                 weights,
                 halo_exit_matrix,
@@ -474,25 +455,36 @@
                 value_rim,
                 *earlier,
             ),
-            scratch=[pltpu.VMEM((2 * RIM, 16, width), BF16)] * 2 + more,
+            scratch=[pltpu.VMEM((2, 2 * RIM, 16, width), BF16)] * (2 * stage),
             megabytes=24,
             smem=2,
-        )[0]
-
-    middle = blocks // 4 * 2
-    half_shape = (rows, middle * BLK, width)
-    earlier = halo(0, middle, [(half_shape, BF16)], (), [])
-    parts[1], earlier = lax.optimization_barrier((parts[1], earlier))
+        )
+
+    inner = (rows, cols - 2 * rest * BLK, width)
+    outer = (rows, 2 * rest * BLK, width)
+    (first,) = halo(0, [inner])
+    parts[1], first, corner = lax.optimization_barrier((parts[1], first, corner))
     (whole,) = call(join_kernel, [part], parts, megabytes=4)
     pairs = [(i, i ^ steps[-1]) for i in range(tall)]
     got = lax.ppermute(whole, "rows", pairs)
-    rest = (rows, cols - middle * BLK, width)
-    tokens_out = halo(middle, blocks, [(x.shape, BF16)], (earlier,), [pltpu.VMEM(rest, BF16)])
-    whole, got, tokens_out = lax.optimization_barrier((whole, got, tokens_out))
+    second, first = halo(1, [outer, inner], (first,))
+    got, second = lax.optimization_barrier((got, second))
     (mixed,) = call(
         last_kernel, [((half, width), BF16)], (whole, got, memory_exit_matrix), megabytes=6
     )
+    (tokens_out,) = call(
+        leave_kernel,
+        [(x.shape, BF16)],
+        (x, halo_exit_matrix, first, second),
+        scratch=[
+            pltpu.VMEM(outer, BF16),
+            pltpu.SemaphoreType.DMA((1 + rows // 2,)),
+        ],
+        megabytes=12,
+        far_outs=(0,),
+    )
     theirs = lax.ppermute(mixed, "cols", swap)
+    theirs, tokens_out = lax.optimization_barrier((theirs, tokens_out))
     latent_mix = jnp.where(
         col == 0, jnp.concatenate([mixed, theirs]), jnp.concatenate([theirs, mixed])
     )

time: 44.6 us -> 43.5 us (0.975)
  Pallas kernels: 20.8 us -> 19.9 us
    ppermute x1, waiting for transfers between devices: 1.33 us -> 0.14 us  [per_device(): theirs = lax.ppermute(mixed, 'cols', swap)]
    pallas_call x10 -> x11, Pallas kernels: 20.8 us -> 19.9 us  [call(): pl.pallas_call(kernel, out_shape=shapes, in_specs=[SMEM] * smem + [VMEM]...]
    ppermute x2, waiting for transfers between devices: 1.84 us -> 2.44 us  [per_device(): parts = [whole, lax.ppermute(whole, 'rows', pairs)]]
  transfers between devices with their start and end apart: 9 -> 9, of which waited for: 5 -> 6; matrix products, arithmetic and copies ran while one was open for 3% -> 3% of each run, Pallas kernels for 44% -> 43%
where the time goes in v4:
time: 43.5 us; the launch traced here: 43.3 us
  Pallas kernels  19.9 us (46%)
  starting transfers between devices  12.6 us (29%)
  waiting for transfers between devices  5.47 us (13%)
  other arithmetic  4.12 us (9%)
  between operations  0.86 us (2%)
    pallas_call x11, Pallas kernels, call(): pl.pallas_call(kernel, out_shape=shapes, in_specs=[SMEM] * smem + [VMEM]...  19.9 us
    ppermute x2, starting transfers between devices, per_device(): parts = [whole, lax.ppermute(whole, 'rows', pairs)]  5.33 us
    ppermute x1, starting transfers between devices, per_device(): near_rim = lax.ppermute(jnp.where(odd, top, bottom), 'rows', near)  2.97 us
    ppermute x1, starting transfers between devices, per_device(): got = lax.ppermute(whole, 'rows', pairs)  2.62 us
    ppermute x2, waiting for transfers between devices, per_device(): parts = [whole, lax.ppermute(whole, 'rows', pairs)]  2.44 us
    select_n x1, other arithmetic, per_device(): far_rim = lax.ppermute(jnp.where(odd, bottom, top), 'rows', far)  2.15 us
    ppermute x1, starting transfers between devices, per_device(): far_rim = lax.ppermute(jnp.where(odd, bottom, top), 'rows', far)  1.41 us
    ppermute x1, waiting for transfers between devices, per_device(): parts = [mine, lax.ppermute(other, 'cols', swap)]  1.36 us
  transfers between devices with their start and end apart: 9, of which 6 were waited for; matrix products, arithmetic and copies ran while one was open for 3% of the time, Pallas kernels for 43%

profile of v4, /device:TPU:0, one launch (start us, length us, event | category | flops | bytes accessed | tf_op | source)
XLA Modules:
  0.0 43.3 jit_solution(13542457240882905842)
XLA Ops:
  0.7 2.2 %broadcast_select_fusion.2 = (bf16[3,128,512]{2,1,0:T(8,128)(2,1)}, bf16[3,128,512]{2,1,0:T(8,128)(2,1)}) fusion(pred[]{:T(512)} %eq.6, bf16[8,128,512]{2,1,0:T(8,128)(2,1)} %x.9), kind=kLoop, calls=%fused_computation.2 | loop fusion | flops 393216 | bytes 1572865 | tf_op jit(solution)/shard_map/jit(_where)/select_n | solution.py:391
  2.8 3.0 %collective-permute-start.3 = (bf16[3,128,512]{2,1,0:T(8,128)(2,1)}, bf16[3,128,512]{2,1,0:T(8,128)(2,1)}, u32[]{:S(2)}, u32[]{:S(2)}) collective-permute-start(bf16[3,128,512]{2,1,0:T(8,128)(2,1)} %get-tuple-element.51), channel_id=1, source_target_pairs={{0,2},{2,0},{4,6},{6,4},{8,10},{10,8},{12,14},{14,12},{1,3},{3,1},... | collective-permute-start | bytes 1179656 | tf_op jit(solution)/shard_map/ppermute | solution.py:390
  5.8 1.4 %collective-permute-start.4 = (bf16[3,128,512]{2,1,0:T(8,128)(2,1)}, bf16[3,128,512]{2,1,0:T(8,128)(2,1)}, u32[]{:S(2)}, u32[]{:S(2)}) collective-permute-start(bf16[3,128,512]{2,1,0:T(8,128)(2,1)} %get-tuple-element.50), channel_id=1, source_target_pairs={{2,4},{4,2},{6,8},{8,6},{10,12},{12,10},{3,5},{5,3},{7,9},{9,7},{1... | collective-permute-start | bytes 1179656 | tf_op jit(solution)/shard_map/ppermute | solution.py:391
  7.3 0.1 collective-permute-start
  7.4 0.1 stack.24
  7.5 1.1 %collective-permute-done.side = bf16[8,8,512]{2,1,0:T(8,128)(2,1)S(1)} collective-permute-done((bf16[8,8,512]{2,1,0:T(8,128)(2,1)S(1)}, bf16[8,8,512]{2,1,0:T(8,128)(2,1)S(1)}, u32[]{:S(2)}, u32[]{:S(2)}) %collective-permute-start) | collective-permute-done | bytes 65568 | tf_op jit(solution)/shard_map/ppermute | solution.py:393
  8.6 0.1 copy-done.3
  8.7 0.1 copy-done.5
  8.8 6.1 %shard_map.105 = (bf16[1024,512]{1,0:T(8,128)(2,1)S(1)}, bf16[1024,512]{1,0:T(8,128)(2,1)S(1)}, bf16[144,512]{1,0:T(8,128)(2,1)S(1)}, bf16[144,512]{1,0:T(8,128)(2,1)S(1)}) custom-call(f32[8]{0:T(128)S(1)} %copy-done.7, s32[6]{0:T(128)S(1)} %convert_element_type.3.place, bf16[8,128,512]{2,1,0:T(8,128)(2,1)S(1)} %copy-done.1, f32[1,512]{1,0:T(1,128)S(1)} %bitcast.7, ...), custom_call_target="tpu_custom_call" | custom-call | flops 1000 | bytes 1000 | tf_op jit(solution)/shard_map/pallas_call | solution.py:347
  14.8 0.1 collective-permute-start.1
  14.9 1.4 %collective-permute-done.1.b = bf16[144,512]{1,0:T(8,128)(2,1)S(1)} collective-permute-done((bf16[144,512]{1,0:T(8,128)(2,1)S(1)}, bf16[144,512]{1,0:T(8,128)(2,1)S(1)}, u32[]{:S(2)}, u32[]{:S(2)}) %collective-permute-start.1) | collective-permute-done | bytes 147488 | tf_op jit(solution)/shard_map/ppermute | solution.py:418
  16.3 0.5 %shard_map.106.a = bf16[144,512]{1,0:T(8,128)(2,1)S(1)} custom-call(bf16[144,512]{1,0:T(8,128)(2,1)S(1)} %get-tuple-element.27.a, bf16[144,512]{1,0:T(8,128)(2,1)S(1)} %collective-permute-done.1.b), custom_call_target="tpu_custom_call" | custom-call | flops 1000 | bytes 1000 | tf_op jit(solution)/shard_map/pallas_call | solution.py:347
  16.8 2.1 %collective-permute-start.2 = (bf16[144,512]{1,0:T(8,128)(2,1)S(1)}, bf16[144,512]{1,0:T(8,128)(2,1)S(1)}, u32[]{:S(2)}, u32[]{:S(2)}) collective-permute-start(bf16[144,512]{1,0:T(8,128)(2,1)S(1)} %shard_map.106.a), channel_id=1, source_target_pairs={{0,4},{2,6},{4,0},{6,2},{8,12},{10,14},{12,8},{14,10},{1,5},{3,7},... | collective-permute-start | bytes 442376 | tf_op jit(solution)/shard_map/ppermute | solution.py:429
  19.0 2.6 %shard_map.108 = (bf16[16,64,512]{2,1,0:T(8,128)(2,1)S(1)}, bf16[8,16,16,512]{3,2,1,0:T(8,128)(2,1)S(1)}, bf16[8,16,16,512]{3,2,1,0:T(8,128)(2,1)S(1)}) custom-call(bf16[8,128,512]{2,1,0:T(8,128)(2,1)S(1)} %copy-done.1, bf16[8,8,512]{2,1,0:T(8,128)(2,1)S(1)} %collective-permute-done.side, f32[1,512]{1,0:T(1,128)S(1)} %bitcast.8, ...), custom_call_target="tpu_custom_call" | custom-call | flops 1000 | bytes 1000 | tf_op jit(solution)/shard_map/pallas_call | solution.py:347
  21.6 1.5 %collective-permute-done.2.b = bf16[144,512]{1,0:T(8,128)(2,1)S(1)} collective-permute-done((bf16[144,512]{1,0:T(8,128)(2,1)S(1)}, bf16[144,512]{1,0:T(8,128)(2,1)S(1)}, u32[]{:S(2)}, u32[]{:S(2)}) %collective-permute-start.2) | collective-permute-done | bytes 147488 | tf_op jit(solution)/shard_map/ppermute | solution.py:429
  23.1 0.5 %shard_map.107.a = bf16[144,512]{1,0:T(8,128)(2,1)S(1)} custom-call(bf16[144,512]{1,0:T(8,128)(2,1)S(1)} %shard_map.106.a, bf16[144,512]{1,0:T(8,128)(2,1)S(1)} %collective-permute-done.2.b), custom_call_target="tpu_custom_call" | custom-call | flops 1000 | bytes 1000 | tf_op jit(solution)/shard_map/pallas_call | solution.py:347
  23.7 0.0 collective-permute-done.4
  23.7 3.2 %collective-permute-start.5 = (bf16[144,512]{1,0:T(8,128)(2,1)S(1)}, bf16[144,512]{1,0:T(8,128)(2,1)S(1)}, u32[]{:S(2)}, u32[]{:S(2)}) collective-permute-start(bf16[144,512]{1,0:T(8,128)(2,1)S(1)} %shard_map.107.a), channel_id=1, source_target_pairs={{0,8},{2,10},{4,12},{6,14},{8,0},{10,2},{12,4},{14,6},{1,9},{3,11}... | collective-permute-start | bytes 442376 | tf_op jit(solution)/shard_map/ppermute | solution.py:429
  26.9 1.2 %broadcast_select_fusion = (bf16[3,128,512]{2,1,0:T(8,128)(2,1)S(1)}, bf16[3,128,512]{2,1,0:T(8,128)(2,1)S(1)}) fusion(bf16[3,128,512]{2,1,0:T(8,128)(2,1)} %collective-permute-done.4, bf16[3,128,512]{2,1,0:T(8,128)(2,1)} %collective-permute-done.3, pred[]{:T(512)} %eq.6), kind=kLoop, calls=%fused_computation | loop fusion | flops 393216 | bytes 1572865 | tf_op jit(solution)/shard_map/jit(_where)/select_n | solution.py:427
  28.1 0.1 collective-permute-start.6
  28.2 1.7 %shard_map.109 = (bf16[6,16,16,512]{3,2,1,0:T(8,128)(2,1)S(1)}, bf16[6,16,16,512]{3,2,1,0:T(8,128)(2,1)S(1)}) custom-call(bf16[3,128,512]{2,1,0:T(8,128)(2,1)S(1)} %get-tuple-element.53.up, bf16[3,128,512]{2,1,0:T(8,128)(2,1)S(1)} %get-tuple-element.52.down, f32[1,512]{1,0:T(1,128)S(1)} %bitcast.9, bf16[512,1536]{1,0:T(8,128)(2,1)S(1)} %copy-done), custom_call_target="tpu_custom_call" | custom-call | flops 1000 | bytes 1000 | tf_op jit(solution)/shard_map/pallas_call | solution.py:347
  29.9 2.6 %shard_map.110.refs_0_ = bf16[8,64,512]{2,1,0:T(8,128)(2,1)S(1)} custom-call(f32[8]{0:T(128)S(1)} %copy-done.7, s32[6]{0:T(128)S(1)} %convert_element_type.3.place, bf16[8,128,512]{2,1,0:T(8,128)(2,1)S(1)} %copy-done.1, f32[1,512]{1,0:T(1,128)S(1)} %bitcast.10, f32[1,512]{1,0:T(1,128)S(1)} %bitcast.11, bf16[512,1536]{1,0:T(8,128)(2,1)S(1)} %copy-done, ...), custom_call_target="tpu_custom_call" | custom-call | flops 1000 | bytes 1000 | tf_op jit(solution)/shard_map/pallas_call | solution.py:347
  32.5 0.9 %collective-permute-done.5.b = bf16[144,512]{1,0:T(8,128)(2,1)S(1)} collective-permute-done((bf16[144,512]{1,0:T(8,128)(2,1)S(1)}, bf16[144,512]{1,0:T(8,128)(2,1)S(1)}, u32[]{:S(2)}, u32[]{:S(2)}) %collective-permute-start.5) | collective-permute-done | bytes 147488 | tf_op jit(solution)/shard_map/ppermute | solution.py:429
  33.5 0.7 %shard_map.111.a = bf16[144,512]{1,0:T(8,128)(2,1)S(1)} custom-call(bf16[144,512]{1,0:T(8,128)(2,1)S(1)} %shard_map.107.a, bf16[144,512]{1,0:T(8,128)(2,1)S(1)} %collective-permute-done.5.b), custom_call_target="tpu_custom_call" | custom-call | flops 1000 | bytes 1000 | tf_op jit(solution)/shard_map/pallas_call | solution.py:347
  34.2 2.6 %collective-permute-start.7 = (bf16[144,512]{1,0:T(8,128)(2,1)S(1)}, bf16[144,512]{1,0:T(8,128)(2,1)S(1)}, u32[]{:S(2)}, u32[]{:S(2)}) collective-permute-start(bf16[144,512]{1,0:T(8,128)(2,1)S(1)} %shard_map.111.a), channel_id=1, source_target_pairs={{0,2},{2,0},{4,6},{6,4},{8,10},{10,8},{12,14},{14,12},{1,3},{3,1},... | collective-permute-start | bytes 442376 | tf_op jit(solution)/shard_map/ppermute | solution.py:469
  36.8 3.2 %shard_map.112 = (bf16[8,64,512]{2,1,0:T(8,128)(2,1)S(1)}, bf16[8,64,512]{2,1,0:T(8,128)(2,1)S(1)}) custom-call(f32[8]{0:T(128)S(1)} %copy-done.7, s32[6]{0:T(128)S(1)} %convert_element_type.3.place, bf16[8,128,512]{2,1,0:T(8,128)(2,1)S(1)} %copy-done.1, bf16[6,8,512]{2,1,0:T(8,128)(2,1)S(1)} %collective-permute-done.6.corner, f32[1,512]{1,0:T(1,128)S(1)} %bitcast.12, ...), custom_call_target="tpu_custom_call" | custom-call | flops 1000 | bytes 1000 | tf_op jit(solution)/shard_map/pallas_call | solution.py:347
  40.1 0.4 collective-permute-done.7.b
  40.5 0.6 %shard_map.113 = bf16[128,512]{1,0:T(8,128)(2,1)S(1)} custom-call(bf16[144,512]{1,0:T(8,128)(2,1)S(1)} %shard_map.111.a, bf16[144,512]{1,0:T(8,128)(2,1)S(1)} %collective-permute-done.7.b, bf16[512,512]{1,0:T(8,128)(2,1)S(1)} %copy-done.4), custom_call_target="tpu_custom_call" | custom-call | flops 1000 | bytes 1000 | tf_op jit(solution)/shard_map/pallas_call | solution.py:347
  41.1 0.1 collective-permute-start.8
  41.2 1.2 %shard_map.114 = bf16[8,128,512]{2,1,0:T(8,128)(2,1)} custom-call(bf16[8,128,512]{2,1,0:T(8,128)(2,1)S(1)} %copy-done.1, bf16[512,512]{1,0:T(8,128)(2,1)S(1)} %copy-done.2, bf16[8,64,512]{2,1,0:T(8,128)(2,1)S(1)} %get-tuple-element.46.first, bf16[8,64,512]{2,1,0:T(8,128)(2,1)S(1)} %get-tuple-element.47.second), custom_call_target="tpu_custom_call" | custom-call | flops 1000 | bytes 1000 | tf_op jit(solution)/shard_map/pallas_call | solution.py:347
  42.4 0.1 collective-permute-done.8
  42.5 0.8 %maximum_select_fusion = bf16[256,512]{1,0:T(8,128)(2,1)} fusion(bf16[128,512]{1,0:T(8,128)(2,1)S(1)} %collective-permute-done.8, bf16[128,512]{1,0:T(8,128)(2,1)S(1)} %shard_map.113, pred[]{:T(512)S(6)} %eq.12), kind=kLoop, calls=%fused_computation.4 | loop fusion | flops 1179648 | bytes 524289 | tf_op jit(solution)/shard_map/jit(_where)/select_n | solution.py:488
  (23 shorter events, 0.1 us)
Async XLA Ops:
  0.6 6.6 %copy-start.1 = (bf16[8,128,512]{2,1,0:T(8,128)(2,1)S(1)}, bf16[8,128,512]{2,1,0:T(8,128)(2,1)}, u32[]{:S(2)}) copy-start(bf16[8,128,512]{2,1,0:T(8,128)(2,1)} %x.9) | copy-start | bytes 3145732
  2.8 20.9 %collective-permute-start.3 = (bf16[3,128,512]{2,1,0:T(8,128)(2,1)}, bf16[3,128,512]{2,1,0:T(8,128)(2,1)}, u32[]{:S(2)}, u32[]{:S(2)}) collective-permute-start(bf16[3,128,512]{2,1,0:T(8,128)(2,1)} %get-tuple-element.51), channel_id=1, source_target_pairs={{0,2},{2,0},{4,6},{6,4},{8,10},{10,8},{12,14},{14,12},{1,3},{3,1},... | collective-permute-start | bytes 1179656 | tf_op jit(solution)/shard_map/ppermute | solution.py:390
  5.8 17.9 %collective-permute-start.4 = (bf16[3,128,512]{2,1,0:T(8,128)(2,1)}, bf16[3,128,512]{2,1,0:T(8,128)(2,1)}, u32[]{:S(2)}, u32[]{:S(2)}) collective-permute-start(bf16[3,128,512]{2,1,0:T(8,128)(2,1)} %get-tuple-element.50), channel_id=1, source_target_pairs={{2,4},{4,2},{6,8},{8,6},{10,12},{12,10},{3,5},{5,3},{7,9},{9,7},{1... | collective-permute-start | bytes 1179656 | tf_op jit(solution)/shard_map/ppermute | solution.py:391
  7.2 1.4 %copy-start = (bf16[512,1536]{1,0:T(8,128)(2,1)S(1)}, bf16[512,1536]{1,0:T(8,128)(2,1)}, u32[]{:S(2)}) copy-start(bf16[512,1536]{1,0:T(8,128)(2,1)} %weights.9) | copy-start | bytes 4718596
  7.2 1.5 %copy-start.3 = (bf16[512,512]{1,0:T(8,128)(2,1)S(1)}, bf16[512,512]{1,0:T(8,128)(2,1)}, u32[]{:S(2)}) copy-start(bf16[512,512]{1,0:T(8,128)(2,1)} %asking.1) | copy-start | bytes 1572868
  7.2 1.6 %copy-start.5 = (bf16[256,512]{1,0:T(8,128)(2,1)S(1)}, bf16[256,512]{1,0:T(8,128)(2,1)}, u32[]{:S(2)}) copy-start(bf16[256,512]{1,0:T(8,128)(2,1)} %slots.1) | copy-start | bytes 786436
  7.2 1.5 %copy-start.6 = (f32[512]{0:T(512)S(1)}, f32[512]{0:T(512)}, u32[]{:S(2)}) copy-start(f32[512]{0:T(512)} %param.10) | copy-start | bytes 6148
  7.2 1.5 %copy-start.7 = (f32[8]{0:T(128)S(1)}, f32[8]{0:T(128)}, u32[]{:S(2)}) copy-start(f32[8]{0:T(128)} %scale.5) | copy-start | bytes 100
  7.3 1.5 %copy-start.8 = (f32[512]{0:T(512)S(1)}, f32[512]{0:T(512)}, u32[]{:S(2)}) copy-start(f32[512]{0:T(512)} %param.14) | copy-start | bytes 6148
  7.3 1.3 %collective-permute-start = (bf16[8,8,512]{2,1,0:T(8,128)(2,1)S(1)}, bf16[8,8,512]{2,1,0:T(8,128)(2,1)S(1)}, u32[]{:S(2)}, u32[]{:S(2)}) collective-permute-start(bf16[8,8,512]{2,1,0:T(8,128)(2,1)S(1)} %shard_map.104), channel_id=1, source_target_pairs={{0,1},{1,0},{2,3},{3,2},{4,5},{5,4},{6,7},{7,6},{8,9},{9,8},{10,11... | collective-permute-start | bytes 196616 | tf_op jit(solution)/shard_map/ppermute | solution.py:393
  14.8 1.4 %collective-permute-start.1 = (bf16[144,512]{1,0:T(8,128)(2,1)S(1)}, bf16[144,512]{1,0:T(8,128)(2,1)S(1)}, u32[]{:S(2)}, u32[]{:S(2)}) collective-permute-start(bf16[144,512]{1,0:T(8,128)(2,1)S(1)} %get-tuple-element.28), channel_id=1, source_target_pairs={{0,1},{1,0},{2,3},{3,2},{4,5},{5,4},{6,7},{7,6},{8,9},{9,8},{10,11... | collective-permute-start | bytes 442376 | tf_op jit(solution)/shard_map/ppermute | solution.py:418
  16.8 6.3 %collective-permute-start.2 = (bf16[144,512]{1,0:T(8,128)(2,1)S(1)}, bf16[144,512]{1,0:T(8,128)(2,1)S(1)}, u32[]{:S(2)}, u32[]{:S(2)}) collective-permute-start(bf16[144,512]{1,0:T(8,128)(2,1)S(1)} %shard_map.106.a), channel_id=1, source_target_pairs={{0,4},{2,6},{4,0},{6,2},{8,12},{10,14},{12,8},{14,10},{1,5},{3,7},... | collective-permute-start | bytes 442376 | tf_op jit(solution)/shard_map/ppermute | solution.py:429
  23.7 9.8 %collective-permute-start.5 = (bf16[144,512]{1,0:T(8,128)(2,1)S(1)}, bf16[144,512]{1,0:T(8,128)(2,1)S(1)}, u32[]{:S(2)}, u32[]{:S(2)}) collective-permute-start(bf16[144,512]{1,0:T(8,128)(2,1)S(1)} %shard_map.107.a), channel_id=1, source_target_pairs={{0,8},{2,10},{4,12},{6,14},{8,0},{10,2},{12,4},{14,6},{1,9},{3,11}... | collective-permute-start | bytes 442376 | tf_op jit(solution)/shard_map/ppermute | solution.py:429
  28.1 1.9 %copy-start.2 = (bf16[512,512]{1,0:T(8,128)(2,1)S(1)}, bf16[512,512]{1,0:T(8,128)(2,1)}, u32[]{:S(2)}) copy-start(bf16[512,512]{1,0:T(8,128)(2,1)} %exits.7) | copy-start | bytes 1572868
  28.1 4.4 %collective-permute-start.6 = (bf16[6,8,512]{2,1,0:T(8,128)(2,1)S(1)}, bf16[6,8,512]{2,1,0:T(8,128)(2,1)S(1)}, u32[]{:S(2)}, u32[]{:S(2)}) collective-permute-start(bf16[6,8,512]{2,1,0:T(8,128)(2,1)S(1)} %pad_maximum_fusion), channel_id=1, source_target_pairs={{0,1},{1,0},{2,3},{3,2},{4,5},{5,4},{6,7},{7,6},{8,9},{9,8},{10,11... | collective-permute-start | bytes 147464 | tf_op jit(solution)/shard_map/ppermute | solution.py:428
  34.2 6.3 %copy-start.4 = (bf16[512,512]{1,0:T(8,128)(2,1)S(1)}, bf16[512,512]{1,0:T(8,128)(2,1)}, u32[]{:S(2)}) copy-start(bf16[512,512]{1,0:T(8,128)(2,1)} %exits.6) | copy-start | bytes 1572868
  34.2 6.3 %collective-permute-start.7 = (bf16[144,512]{1,0:T(8,128)(2,1)S(1)}, bf16[144,512]{1,0:T(8,128)(2,1)S(1)}, u32[]{:S(2)}, u32[]{:S(2)}) collective-permute-start(bf16[144,512]{1,0:T(8,128)(2,1)S(1)} %shard_map.111.a), channel_id=1, source_target_pairs={{0,2},{2,0},{4,6},{6,4},{8,10},{10,8},{12,14},{14,12},{1,3},{3,1},... | collective-permute-start | bytes 442376 | tf_op jit(solution)/shard_map/ppermute | solution.py:469
  41.1 1.4 %collective-permute-start.8 = (bf16[128,512]{1,0:T(8,128)(2,1)S(1)}, bf16[128,512]{1,0:T(8,128)(2,1)S(1)}, u32[]{:S(2)}, u32[]{:S(2)}) collective-permute-start(bf16[128,512]{1,0:T(8,128)(2,1)S(1)} %shard_map.113), channel_id=1, source_target_pairs={{0,1},{1,0},{2,3},{3,2},{4,5},{5,4},{6,7},{7,6},{8,9},{9,8},{10,11... | collective-permute-start | bytes 393224 | tf_op jit(solution)/shard_map/ppermute | solution.py:486

commit v5 on v4

--- a/solution.py
+++ b/solution.py
@@ -386,12 +386,12 @@
     def edge(array):
         return jnp.where(col == 0, array[:, cols - BLK :], array[:, :BLK])
 
-    top, bottom = (x[:RIM], x[rows - RIM :])
+    (side,) = call(copy_kernel, [((rows, BLK, width), BF16)], (edge(x),), megabytes=2, flops=10**10)
+    place, after, side = lax.optimization_barrier((place, x, side))
+    top, bottom = (after[:RIM], after[rows - RIM :])
     near_rim = lax.ppermute(jnp.where(odd, top, bottom), "rows", near)
     far_rim = lax.ppermute(jnp.where(odd, bottom, top), "rows", far)
-    (side,) = call(copy_kernel, [((rows, BLK, width), BF16)], (edge(x),), megabytes=2, flops=10**10)
     side = lax.ppermute(side, "cols", swap)
-    place, side = lax.optimization_barrier((place, side))
 
     half = latents // 2
     tokens = rows * cols

time: 43.5 us -> 42.6 us (0.979)
  other arithmetic: 4.12 us -> 1.79 us
  local copies, waits for them, and re-layouts: 0.33 us -> 1.32 us
  starting transfers between devices: 12.6 us -> 13.1 us
    select_n x1, other arithmetic: 2.15 us -> 0.06 us  [per_device(): far_rim = lax.ppermute(jnp.where(odd, bottom, top), 'rows', far)]
    select_n x1, other arithmetic: 1.17 us -> 0.06 us  [per_device(): down = jnp.where(odd, far_rim, near_rim)]
    ppermute x2, starting transfers between devices: 5.33 us -> 6.41 us  [per_device(): parts = [whole, lax.ppermute(whole, 'rows', pairs)]]
    unnamed x18, local copies, waits for them, and re-layouts: 0.22 us -> 1.22 us
    select_n x2, other arithmetic: 0.02 us -> 0.9 us  [edge(): return jnp.where(col == 0, array[:, cols - BLK:], array[:, :BLK])]
    ppermute x1, starting transfers between devices: 1.41 us -> 0.67 us  [per_device(): far_rim = lax.ppermute(jnp.where(odd, bottom, top), 'rows', far)]
    ppermute x2, waiting for transfers between devices: 2.44 us -> 1.99 us  [per_device(): parts = [whole, lax.ppermute(whole, 'rows', pairs)]]
  transfers between devices with their start and end apart: 9 -> 9, of which waited for: 6 -> 7; matrix products, arithmetic and copies ran while one was open for 3% -> 0% of each run, Pallas kernels for 43% -> 44%
where the time goes in v5:
time: 42.6 us; the launch traced here: 42.4 us
  Pallas kernels  20.1 us (47%)
  starting transfers between devices  13.1 us (31%)
  waiting for transfers between devices  5.2 us (12%)
  other arithmetic  1.79 us (4%)
  local copies, waits for them, and re-layouts  1.32 us (3%)
  between operations  0.88 us (2%)
    pallas_call x11, Pallas kernels, call(): pl.pallas_call(kernel, out_shape=shapes, in_specs=[SMEM] * smem + [VMEM]...  20.1 us
    ppermute x2, starting transfers between devices, per_device(): parts = [whole, lax.ppermute(whole, 'rows', pairs)]  6.41 us
    ppermute x1, starting transfers between devices, per_device(): near_rim = lax.ppermute(jnp.where(odd, top, bottom), 'rows', near)  3.03 us
    ppermute x1, starting transfers between devices, per_device(): got = lax.ppermute(whole, 'rows', pairs)  2.72 us
    ppermute x2, waiting for transfers between devices, per_device(): parts = [whole, lax.ppermute(whole, 'rows', pairs)]  1.99 us
    ppermute x1, waiting for transfers between devices, per_device(): parts = [mine, lax.ppermute(other, 'cols', swap)]  1.36 us
    ppermute x1, waiting for transfers between devices, per_device(): side = lax.ppermute(side, 'cols', swap)  1.25 us
    unnamed x18, local copies, waits for them, and re-layouts  1.22 us
  transfers between devices with their start and end apart: 9, of which 7 were waited for; matrix products, arithmetic and copies ran while one was open for 0% of the time, Pallas kernels for 44%

profile of v5, /device:TPU:0, one launch (start us, length us, event | category | flops | bytes accessed | tf_op | source)
XLA Modules:
  0.0 42.4 jit_solution(8729852482555461842)
XLA Ops:
  0.7 0.1 stack.24
  0.8 0.9 %slice_select_fusion.a = bf16[8,8,512]{2,1,0:T(8,128)(2,1)S(1)} fusion(bf16[8,128,512]{2,1,0:T(8,128)(2,1)} %x.9, pred[]{:T(512)S(6)} %eq.12), kind=kLoop, calls=%fused_computation.5 | loop fusion | flops 32768 | bytes 196609 | tf_op jit(solution)/shard_map/jit(_where)/select_n | solution.py:387
  1.7 0.0 copy-start.5
  1.7 1.2 %copy-done.1 = bf16[8,128,512]{2,1,0:T(8,128)(2,1)S(1)} copy-done((bf16[8,128,512]{2,1,0:T(8,128)(2,1)S(1)}, bf16[8,128,512]{2,1,0:T(8,128)(2,1)}, u32[]{:S(2)}) %copy-start.1) | copy-done | bytes 1048600
  2.9 0.1 broadcast_select_fusion.2
  3.0 3.0 %collective-permute-start.2 = (bf16[3,128,512]{2,1,0:T(8,128)(2,1)S(1)}, bf16[3,128,512]{2,1,0:T(8,128)(2,1)S(1)}, u32[]{:S(2)}, u32[]{:S(2)}) collective-permute-start(bf16[3,128,512]{2,1,0:T(8,128)(2,1)S(1)} %get-tuple-element.53), channel_id=1, source_target_pairs={{0,2},{2,0},{4,6},{6,4},{8,10},{10,8},{12,14},{14,12},{1,3},{3,1},... | collective-permute-start | bytes 1179656 | tf_op jit(solution)/shard_map/ppermute | solution.py:392
  6.0 0.7 %collective-permute-start.3 = (bf16[3,128,512]{2,1,0:T(8,128)(2,1)S(1)}, bf16[3,128,512]{2,1,0:T(8,128)(2,1)S(1)}, u32[]{:S(2)}, u32[]{:S(2)}) collective-permute-start(bf16[3,128,512]{2,1,0:T(8,128)(2,1)S(1)} %get-tuple-element.52), channel_id=1, source_target_pairs={{2,4},{4,2},{6,8},{8,6},{10,12},{12,10},{3,5},{5,3},{7,9},{9,7},{1... | collective-permute-start | bytes 1179656 | tf_op jit(solution)/shard_map/ppermute | solution.py:393
  6.7 6.2 %shard_map.105 = (bf16[1024,512]{1,0:T(8,128)(2,1)S(1)}, bf16[1024,512]{1,0:T(8,128)(2,1)S(1)}, bf16[144,512]{1,0:T(8,128)(2,1)S(1)}, bf16[144,512]{1,0:T(8,128)(2,1)S(1)}) custom-call(f32[8]{0:T(128)S(1)} %copy-done.7, s32[6]{0:T(128)S(1)} %convert_element_type.3.place, bf16[8,128,512]{2,1,0:T(8,128)(2,1)S(1)} %copy-done.1, f32[1,512]{1,0:T(1,128)S(1)} %bitcast.7, ...), custom_call_target="tpu_custom_call" | custom-call | flops 1000 | bytes 1000 | tf_op jit(solution)/shard_map/pallas_call | solution.py:347
  13.0 0.1 collective-permute-start
  13.1 1.4 %collective-permute-done.b = bf16[144,512]{1,0:T(8,128)(2,1)S(1)} collective-permute-done((bf16[144,512]{1,0:T(8,128)(2,1)S(1)}, bf16[144,512]{1,0:T(8,128)(2,1)S(1)}, u32[]{:S(2)}, u32[]{:S(2)}) %collective-permute-start) | collective-permute-done | bytes 147488 | tf_op jit(solution)/shard_map/ppermute | solution.py:418
  14.4 0.5 %shard_map.106.a = bf16[144,512]{1,0:T(8,128)(2,1)S(1)} custom-call(bf16[144,512]{1,0:T(8,128)(2,1)S(1)} %get-tuple-element.28.a, bf16[144,512]{1,0:T(8,128)(2,1)S(1)} %collective-permute-done.b), custom_call_target="tpu_custom_call" | custom-call | flops 1000 | bytes 1000 | tf_op jit(solution)/shard_map/pallas_call | solution.py:347
  15.0 2.9 %collective-permute-start.1 = (bf16[144,512]{1,0:T(8,128)(2,1)S(1)}, bf16[144,512]{1,0:T(8,128)(2,1)S(1)}, u32[]{:S(2)}, u32[]{:S(2)}) collective-permute-start(bf16[144,512]{1,0:T(8,128)(2,1)S(1)} %shard_map.106.a), channel_id=1, source_target_pairs={{0,4},{2,6},{4,0},{6,2},{8,12},{10,14},{12,8},{14,10},{1,5},{3,7},... | collective-permute-start | bytes 442376 | tf_op jit(solution)/shard_map/ppermute | solution.py:429
  17.8 1.3 %collective-permute-done.4.side = bf16[8,8,512]{2,1,0:T(8,128)(2,1)S(1)} collective-permute-done((bf16[8,8,512]{2,1,0:T(8,128)(2,1)S(1)}, bf16[8,8,512]{2,1,0:T(8,128)(2,1)S(1)}, u32[]{:S(2)}, u32[]{:S(2)}) %collective-permute-start.4) | collective-permute-done | bytes 65568 | tf_op jit(solution)/shard_map/ppermute | solution.py:394
  19.1 2.7 %shard_map.108 = (bf16[16,64,512]{2,1,0:T(8,128)(2,1)S(1)}, bf16[8,16,16,512]{3,2,1,0:T(8,128)(2,1)S(1)}, bf16[8,16,16,512]{3,2,1,0:T(8,128)(2,1)S(1)}) custom-call(bf16[8,128,512]{2,1,0:T(8,128)(2,1)S(1)} %copy-done.1, bf16[8,8,512]{2,1,0:T(8,128)(2,1)S(1)} %collective-permute-done.4.side, f32[1,512]{1,0:T(1,128)S(1)} %bitcast.8, ...), custom_call_target="tpu_custom_call" | custom-call | flops 1000 | bytes 1000 | tf_op jit(solution)/shard_map/pallas_call | solution.py:347
  21.8 0.2 collective-permute-done.1.b
  22.0 0.5 %shard_map.107.a = bf16[144,512]{1,0:T(8,128)(2,1)S(1)} custom-call(bf16[144,512]{1,0:T(8,128)(2,1)S(1)} %shard_map.106.a, bf16[144,512]{1,0:T(8,128)(2,1)S(1)} %collective-permute-done.1.b), custom_call_target="tpu_custom_call" | custom-call | flops 1000 | bytes 1000 | tf_op jit(solution)/shard_map/pallas_call | solution.py:347
  22.5 0.3 collective-permute-done.2
  22.8 3.6 %collective-permute-start.5 = (bf16[144,512]{1,0:T(8,128)(2,1)S(1)}, bf16[144,512]{1,0:T(8,128)(2,1)S(1)}, u32[]{:S(2)}, u32[]{:S(2)}) collective-permute-start(bf16[144,512]{1,0:T(8,128)(2,1)S(1)} %shard_map.107.a), channel_id=1, source_target_pairs={{0,8},{2,10},{4,12},{6,14},{8,0},{10,2},{12,4},{14,6},{1,9},{3,11}... | collective-permute-start | bytes 442376 | tf_op jit(solution)/shard_map/ppermute | solution.py:429
  26.3 0.1 broadcast_select_fusion
  26.4 0.1 collective-permute-start.6
  26.5 1.7 %shard_map.109 = (bf16[6,16,16,512]{3,2,1,0:T(8,128)(2,1)S(1)}, bf16[6,16,16,512]{3,2,1,0:T(8,128)(2,1)S(1)}) custom-call(bf16[3,128,512]{2,1,0:T(8,128)(2,1)S(1)} %get-tuple-element.55.up, bf16[3,128,512]{2,1,0:T(8,128)(2,1)S(1)} %get-tuple-element.54.down, f32[1,512]{1,0:T(1,128)S(1)} %bitcast.9, bf16[512,1536]{1,0:T(8,128)(2,1)S(1)} %copy-done), custom_call_target="tpu_custom_call" | custom-call | flops 1000 | bytes 1000 | tf_op jit(solution)/shard_map/pallas_call | solution.py:347
  28.3 2.6 %shard_map.110.refs_0_ = bf16[8,64,512]{2,1,0:T(8,128)(2,1)S(1)} custom-call(f32[8]{0:T(128)S(1)} %copy-done.7, s32[6]{0:T(128)S(1)} %convert_element_type.3.place, bf16[8,128,512]{2,1,0:T(8,128)(2,1)S(1)} %copy-done.1, f32[1,512]{1,0:T(1,128)S(1)} %bitcast.10, f32[1,512]{1,0:T(1,128)S(1)} %bitcast.11, bf16[512,1536]{1,0:T(8,128)(2,1)S(1)} %copy-done, ...), custom_call_target="tpu_custom_call" | custom-call | flops 1000 | bytes 1000 | tf_op jit(solution)/shard_map/pallas_call | solution.py:347
  30.9 1.8 %collective-permute-done.5.b = bf16[144,512]{1,0:T(8,128)(2,1)S(1)} collective-permute-done((bf16[144,512]{1,0:T(8,128)(2,1)S(1)}, bf16[144,512]{1,0:T(8,128)(2,1)S(1)}, u32[]{:S(2)}, u32[]{:S(2)}) %collective-permute-start.5) | collective-permute-done | bytes 147488 | tf_op jit(solution)/shard_map/ppermute | solution.py:429
  32.7 0.7 %shard_map.111.a = bf16[144,512]{1,0:T(8,128)(2,1)S(1)} custom-call(bf16[144,512]{1,0:T(8,128)(2,1)S(1)} %shard_map.107.a, bf16[144,512]{1,0:T(8,128)(2,1)S(1)} %collective-permute-done.5.b), custom_call_target="tpu_custom_call" | custom-call | flops 1000 | bytes 1000 | tf_op jit(solution)/shard_map/pallas_call | solution.py:347
  33.4 2.7 %collective-permute-start.7 = (bf16[144,512]{1,0:T(8,128)(2,1)S(1)}, bf16[144,512]{1,0:T(8,128)(2,1)S(1)}, u32[]{:S(2)}, u32[]{:S(2)}) collective-permute-start(bf16[144,512]{1,0:T(8,128)(2,1)S(1)} %shard_map.111.a), channel_id=1, source_target_pairs={{0,2},{2,0},{4,6},{6,4},{8,10},{10,8},{12,14},{14,12},{1,3},{3,1},... | collective-permute-start | bytes 442376 | tf_op jit(solution)/shard_map/ppermute | solution.py:469
  36.1 3.2 %shard_map.112 = (bf16[8,64,512]{2,1,0:T(8,128)(2,1)S(1)}, bf16[8,64,512]{2,1,0:T(8,128)(2,1)S(1)}) custom-call(f32[8]{0:T(128)S(1)} %copy-done.7, s32[6]{0:T(128)S(1)} %convert_element_type.3.place, bf16[8,128,512]{2,1,0:T(8,128)(2,1)S(1)} %copy-done.1, bf16[6,8,512]{2,1,0:T(8,128)(2,1)S(1)} %collective-permute-done.6.corner, f32[1,512]{1,0:T(1,128)S(1)} %bitcast.12, ...), custom_call_target="tpu_custom_call" | custom-call | flops 1000 | bytes 1000 | tf_op jit(solution)/shard_map/pallas_call | solution.py:347
  39.4 0.2 collective-permute-done.7.b
  39.6 0.6 %shard_map.113 = bf16[128,512]{1,0:T(8,128)(2,1)S(1)} custom-call(bf16[144,512]{1,0:T(8,128)(2,1)S(1)} %shard_map.111.a, bf16[144,512]{1,0:T(8,128)(2,1)S(1)} %collective-permute-done.7.b, bf16[512,512]{1,0:T(8,128)(2,1)S(1)} %copy-done.4), custom_call_target="tpu_custom_call" | custom-call | flops 1000 | bytes 1000 | tf_op jit(solution)/shard_map/pallas_call | solution.py:347
  40.2 0.1 collective-permute-start.8
  40.3 1.2 %shard_map.114 = bf16[8,128,512]{2,1,0:T(8,128)(2,1)} custom-call(bf16[8,128,512]{2,1,0:T(8,128)(2,1)S(1)} %copy-done.1, bf16[512,512]{1,0:T(8,128)(2,1)S(1)} %copy-done.2, bf16[8,64,512]{2,1,0:T(8,128)(2,1)S(1)} %get-tuple-element.48.first, bf16[8,64,512]{2,1,0:T(8,128)(2,1)S(1)} %get-tuple-element.49.second), custom_call_target="tpu_custom_call" | custom-call | flops 1000 | bytes 1000 | tf_op jit(solution)/shard_map/pallas_call | solution.py:347
  41.5 0.1 collective-permute-done.8
  41.6 0.8 %maximum_select_fusion = bf16[256,512]{1,0:T(8,128)(2,1)} fusion(bf16[128,512]{1,0:T(8,128)(2,1)S(1)} %collective-permute-done.8, bf16[128,512]{1,0:T(8,128)(2,1)S(1)} %shard_map.113, pred[]{:T(512)S(6)} %eq.12), kind=kLoop, calls=%fused_computation.4 | loop fusion | flops 1179648 | bytes 524289 | tf_op jit(solution)/shard_map/jit(_where)/select_n | solution.py:488
  (23 shorter events, 0.1 us)
Async XLA Ops:
  1.6 1.2 %copy-start.1 = (bf16[8,128,512]{2,1,0:T(8,128)(2,1)S(1)}, bf16[8,128,512]{2,1,0:T(8,128)(2,1)}, u32[]{:S(2)}) copy-start(bf16[8,128,512]{2,1,0:T(8,128)(2,1)} %x.9) | copy-start | bytes 3145732
  1.7 5.0 %copy-start.3 = (bf16[512,512]{1,0:T(8,128)(2,1)S(1)}, bf16[512,512]{1,0:T(8,128)(2,1)}, u32[]{:S(2)}) copy-start(bf16[512,512]{1,0:T(8,128)(2,1)} %asking.1) | copy-start | bytes 1572868
  1.7 5.0 %copy-start.5 = (bf16[256,512]{1,0:T(8,128)(2,1)S(1)}, bf16[256,512]{1,0:T(8,128)(2,1)}, u32[]{:S(2)}) copy-start(bf16[256,512]{1,0:T(8,128)(2,1)} %slots.1) | copy-start | bytes 786436
  2.9 3.8 %copy-start = (bf16[512,1536]{1,0:T(8,128)(2,1)S(1)}, bf16[512,1536]{1,0:T(8,128)(2,1)}, u32[]{:S(2)}) copy-start(bf16[512,1536]{1,0:T(8,128)(2,1)} %weights.9) | copy-start | bytes 4718596
  2.9 3.8 %copy-start.6 = (f32[512]{0:T(512)S(1)}, f32[512]{0:T(512)}, u32[]{:S(2)}) copy-start(f32[512]{0:T(512)} %param.10) | copy-start | bytes 6148
  2.9 3.8 %copy-start.7 = (f32[8]{0:T(128)S(1)}, f32[8]{0:T(128)}, u32[]{:S(2)}) copy-start(f32[8]{0:T(128)} %scale.5) | copy-start | bytes 100
  2.9 3.8 %copy-start.8 = (f32[512]{0:T(512)S(1)}, f32[512]{0:T(512)}, u32[]{:S(2)}) copy-start(f32[512]{0:T(512)} %param.14) | copy-start | bytes 6148
  3.0 19.8 %collective-permute-start.2 = (bf16[3,128,512]{2,1,0:T(8,128)(2,1)S(1)}, bf16[3,128,512]{2,1,0:T(8,128)(2,1)S(1)}, u32[]{:S(2)}, u32[]{:S(2)}) collective-permute-start(bf16[3,128,512]{2,1,0:T(8,128)(2,1)S(1)} %get-tuple-element.53), channel_id=1, source_target_pairs={{0,2},{2,0},{4,6},{6,4},{8,10},{10,8},{12,14},{14,12},{1,3},{3,1},... | collective-permute-start | bytes 1179656 | tf_op jit(solution)/shard_map/ppermute | solution.py:392
  6.0 16.8 %collective-permute-start.3 = (bf16[3,128,512]{2,1,0:T(8,128)(2,1)S(1)}, bf16[3,128,512]{2,1,0:T(8,128)(2,1)S(1)}, u32[]{:S(2)}, u32[]{:S(2)}) collective-permute-start(bf16[3,128,512]{2,1,0:T(8,128)(2,1)S(1)} %get-tuple-element.52), channel_id=1, source_target_pairs={{2,4},{4,2},{6,8},{8,6},{10,12},{12,10},{3,5},{5,3},{7,9},{9,7},{1... | collective-permute-start | bytes 1179656 | tf_op jit(solution)/shard_map/ppermute | solution.py:393
  13.0 1.4 %collective-permute-start = (bf16[144,512]{1,0:T(8,128)(2,1)S(1)}, bf16[144,512]{1,0:T(8,128)(2,1)S(1)}, u32[]{:S(2)}, u32[]{:S(2)}) collective-permute-start(bf16[144,512]{1,0:T(8,128)(2,1)S(1)} %get-tuple-element.29), channel_id=1, source_target_pairs={{0,1},{1,0},{2,3},{3,2},{4,5},{5,4},{6,7},{7,6},{8,9},{9,8},{10,11... | collective-permute-start | bytes 442376 | tf_op jit(solution)/shard_map/ppermute | solution.py:418
  15.0 7.0 %collective-permute-start.1 = (bf16[144,512]{1,0:T(8,128)(2,1)S(1)}, bf16[144,512]{1,0:T(8,128)(2,1)S(1)}, u32[]{:S(2)}, u32[]{:S(2)}) collective-permute-start(bf16[144,512]{1,0:T(8,128)(2,1)S(1)} %shard_map.106.a), channel_id=1, source_target_pairs={{0,4},{2,6},{4,0},{6,2},{8,12},{10,14},{12,8},{14,10},{1,5},{3,7},... | collective-permute-start | bytes 442376 | tf_op jit(solution)/shard_map/ppermute | solution.py:429
  17.8 1.3 %collective-permute-start.4 = (bf16[8,8,512]{2,1,0:T(8,128)(2,1)S(1)}, bf16[8,8,512]{2,1,0:T(8,128)(2,1)S(1)}, u32[]{:S(2)}, u32[]{:S(2)}) collective-permute-start(bf16[8,8,512]{2,1,0:T(8,128)(2,1)S(1)} %shard_map.104), channel_id=1, source_target_pairs={{0,1},{1,0},{2,3},{3,2},{4,5},{5,4},{6,7},{7,6},{8,9},{9,8},{10,11... | collective-permute-start | bytes 196616 | tf_op jit(solution)/shard_map/ppermute | solution.py:394
  22.8 9.9 %collective-permute-start.5 = (bf16[144,512]{1,0:T(8,128)(2,1)S(1)}, bf16[144,512]{1,0:T(8,128)(2,1)S(1)}, u32[]{:S(2)}, u32[]{:S(2)}) collective-permute-start(bf16[144,512]{1,0:T(8,128)(2,1)S(1)} %shard_map.107.a), channel_id=1, source_target_pairs={{0,8},{2,10},{4,12},{6,14},{8,0},{10,2},{12,4},{14,6},{1,9},{3,11}... | collective-permute-start | bytes 442376 | tf_op jit(solution)/shard_map/ppermute | solution.py:429
  26.4 1.9 %copy-start.2 = (bf16[512,512]{1,0:T(8,128)(2,1)S(1)}, bf16[512,512]{1,0:T(8,128)(2,1)}, u32[]{:S(2)}) copy-start(bf16[512,512]{1,0:T(8,128)(2,1)} %exits.7) | copy-start | bytes 1572868
  26.4 4.5 %collective-permute-start.6 = (bf16[6,8,512]{2,1,0:T(8,128)(2,1)S(1)}, bf16[6,8,512]{2,1,0:T(8,128)(2,1)S(1)}, u32[]{:S(2)}, u32[]{:S(2)}) collective-permute-start(bf16[6,8,512]{2,1,0:T(8,128)(2,1)S(1)} %pad_maximum_fusion), channel_id=1, source_target_pairs={{0,1},{1,0},{2,3},{3,2},{4,5},{5,4},{6,7},{7,6},{8,9},{9,8},{10,11... | collective-permute-start | bytes 147464 | tf_op jit(solution)/shard_map/ppermute | solution.py:428
  33.4 6.2 %copy-start.4 = (bf16[512,512]{1,0:T(8,128)(2,1)S(1)}, bf16[512,512]{1,0:T(8,128)(2,1)}, u32[]{:S(2)}) copy-start(bf16[512,512]{1,0:T(8,128)(2,1)} %exits.6) | copy-start | bytes 1572868
  33.4 6.2 %collective-permute-start.7 = (bf16[144,512]{1,0:T(8,128)(2,1)S(1)}, bf16[144,512]{1,0:T(8,128)(2,1)S(1)}, u32[]{:S(2)}, u32[]{:S(2)}) collective-permute-start(bf16[144,512]{1,0:T(8,128)(2,1)S(1)} %shard_map.111.a), channel_id=1, source_target_pairs={{0,2},{2,0},{4,6},{6,4},{8,10},{10,8},{12,14},{14,12},{1,3},{3,1},... | collective-permute-start | bytes 442376 | tf_op jit(solution)/shard_map/ppermute | solution.py:469
  40.2 1.4 %collective-permute-start.8 = (bf16[128,512]{1,0:T(8,128)(2,1)S(1)}, bf16[128,512]{1,0:T(8,128)(2,1)S(1)}, u32[]{:S(2)}, u32[]{:S(2)}) collective-permute-start(bf16[128,512]{1,0:T(8,128)(2,1)S(1)} %shard_map.113), channel_id=1, source_target_pairs={{0,1},{1,0},{2,3},{3,2},{4,5},{5,4},{6,7},{7,6},{8,9},{9,8},{10,11... | collective-permute-start | bytes 393224 | tf_op jit(solution)/shard_map/ppermute | solution.py:486

commit v6 on v5

--- a/solution.py
+++ b/solution.py
@@ -307,7 +307,7 @@
             mixed = dot(jnp.concatenate(expos, axis=0), value)
             out = jnp.zeros((n, group), F32)
             for h in range(per):
-                out = jnp.where(owner == h, mixed[h * n : (h + 1) * n] / totals[h], out)
+                out = jnp.where(owner == h, mixed[h * n : (h + 1) * n] * (1.0 / totals[h]), out)
             outs.append(out)
         return jnp.concatenate(outs, axis=1).reshape(BLK, BLK, width)
 

time: 42.6 us -> 42.6 us (level)
  no operation moved by 1% of the time
where the time goes in v6:
time: 42.6 us; the launch traced here: 42.4 us
  Pallas kernels  20.1 us (47%)
  starting transfers between devices  13.1 us (31%)
  waiting for transfers between devices  5.2 us (12%)
  other arithmetic  1.79 us (4%)
  local copies, waits for them, and re-layouts  1.32 us (3%)
  between operations  0.88 us (2%)
    pallas_call x11, Pallas kernels, call(): pl.pallas_call(kernel, out_shape=shapes, in_specs=[SMEM] * smem + [VMEM]...  20.1 us
    ppermute x2, starting transfers between devices, per_device(): parts = [whole, lax.ppermute(whole, 'rows', pairs)]  6.41 us
    ppermute x1, starting transfers between devices, per_device(): near_rim = lax.ppermute(jnp.where(odd, top, bottom), 'rows', near)  3.03 us
    ppermute x1, starting transfers between devices, per_device(): got = lax.ppermute(whole, 'rows', pairs)  2.72 us
    ppermute x2, waiting for transfers between devices, per_device(): parts = [whole, lax.ppermute(whole, 'rows', pairs)]  1.99 us
    ppermute x1, waiting for transfers between devices, per_device(): parts = [mine, lax.ppermute(other, 'cols', swap)]  1.36 us
    ppermute x1, waiting for transfers between devices, per_device(): side = lax.ppermute(side, 'cols', swap)  1.25 us
    unnamed x18, local copies, waits for them, and re-layouts  1.22 us
  transfers between devices with their start and end apart: 9, of which 7 were waited for; matrix products, arithmetic and copies ran while one was open for 0% of the time, Pallas kernels for 44%

profile of v6, /device:TPU:0, one launch (start us, length us, event | category | flops | bytes accessed | tf_op | source)
XLA Modules:
  0.0 42.4 jit_solution(8729852482555461842)
XLA Ops:
  0.7 0.1 stack.24
  0.8 0.9 %slice_select_fusion.a = bf16[8,8,512]{2,1,0:T(8,128)(2,1)S(1)} fusion(bf16[8,128,512]{2,1,0:T(8,128)(2,1)} %x.9, pred[]{:T(512)S(6)} %eq.12), kind=kLoop, calls=%fused_computation.5 | loop fusion | flops 32768 | bytes 196609 | tf_op jit(solution)/shard_map/jit(_where)/select_n | solution.py:387
  1.7 0.0 copy-start.5
  1.7 1.2 %copy-done.1 = bf16[8,128,512]{2,1,0:T(8,128)(2,1)S(1)} copy-done((bf16[8,128,512]{2,1,0:T(8,128)(2,1)S(1)}, bf16[8,128,512]{2,1,0:T(8,128)(2,1)}, u32[]{:S(2)}) %copy-start.1) | copy-done | bytes 1048600
  2.9 0.1 broadcast_select_fusion.2
  3.0 3.0 %collective-permute-start.2 = (bf16[3,128,512]{2,1,0:T(8,128)(2,1)S(1)}, bf16[3,128,512]{2,1,0:T(8,128)(2,1)S(1)}, u32[]{:S(2)}, u32[]{:S(2)}) collective-permute-start(bf16[3,128,512]{2,1,0:T(8,128)(2,1)S(1)} %get-tuple-element.53), channel_id=1, source_target_pairs={{0,2},{2,0},{4,6},{6,4},{8,10},{10,8},{12,14},{14,12},{1,3},{3,1},... | collective-permute-start | bytes 1179656 | tf_op jit(solution)/shard_map/ppermute | solution.py:392
  6.0 0.7 %collective-permute-start.3 = (bf16[3,128,512]{2,1,0:T(8,128)(2,1)S(1)}, bf16[3,128,512]{2,1,0:T(8,128)(2,1)S(1)}, u32[]{:S(2)}, u32[]{:S(2)}) collective-permute-start(bf16[3,128,512]{2,1,0:T(8,128)(2,1)S(1)} %get-tuple-element.52), channel_id=1, source_target_pairs={{2,4},{4,2},{6,8},{8,6},{10,12},{12,10},{3,5},{5,3},{7,9},{9,7},{1... | collective-permute-start | bytes 1179656 | tf_op jit(solution)/shard_map/ppermute | solution.py:393
  6.7 6.2 %shard_map.105 = (bf16[1024,512]{1,0:T(8,128)(2,1)S(1)}, bf16[1024,512]{1,0:T(8,128)(2,1)S(1)}, bf16[144,512]{1,0:T(8,128)(2,1)S(1)}, bf16[144,512]{1,0:T(8,128)(2,1)S(1)}) custom-call(f32[8]{0:T(128)S(1)} %copy-done.7, s32[6]{0:T(128)S(1)} %convert_element_type.3.place, bf16[8,128,512]{2,1,0:T(8,128)(2,1)S(1)} %copy-done.1, f32[1,512]{1,0:T(1,128)S(1)} %bitcast.7, ...), custom_call_target="tpu_custom_call" | custom-call | flops 1000 | bytes 1000 | tf_op jit(solution)/shard_map/pallas_call | solution.py:347
  13.0 0.1 collective-permute-start
  13.1 1.4 %collective-permute-done.b = bf16[144,512]{1,0:T(8,128)(2,1)S(1)} collective-permute-done((bf16[144,512]{1,0:T(8,128)(2,1)S(1)}, bf16[144,512]{1,0:T(8,128)(2,1)S(1)}, u32[]{:S(2)}, u32[]{:S(2)}) %collective-permute-start) | collective-permute-done | bytes 147488 | tf_op jit(solution)/shard_map/ppermute | solution.py:418
  14.4 0.5 %shard_map.106.a = bf16[144,512]{1,0:T(8,128)(2,1)S(1)} custom-call(bf16[144,512]{1,0:T(8,128)(2,1)S(1)} %get-tuple-element.28.a, bf16[144,512]{1,0:T(8,128)(2,1)S(1)} %collective-permute-done.b), custom_call_target="tpu_custom_call" | custom-call | flops 1000 | bytes 1000 | tf_op jit(solution)/shard_map/pallas_call | solution.py:347
  15.0 2.9 %collective-permute-start.1 = (bf16[144,512]{1,0:T(8,128)(2,1)S(1)}, bf16[144,512]{1,0:T(8,128)(2,1)S(1)}, u32[]{:S(2)}, u32[]{:S(2)}) collective-permute-start(bf16[144,512]{1,0:T(8,128)(2,1)S(1)} %shard_map.106.a), channel_id=1, source_target_pairs={{0,4},{2,6},{4,0},{6,2},{8,12},{10,14},{12,8},{14,10},{1,5},{3,7},... | collective-permute-start | bytes 442376 | tf_op jit(solution)/shard_map/ppermute | solution.py:429
  17.8 1.3 %collective-permute-done.4.side = bf16[8,8,512]{2,1,0:T(8,128)(2,1)S(1)} collective-permute-done((bf16[8,8,512]{2,1,0:T(8,128)(2,1)S(1)}, bf16[8,8,512]{2,1,0:T(8,128)(2,1)S(1)}, u32[]{:S(2)}, u32[]{:S(2)}) %collective-permute-start.4) | collective-permute-done | bytes 65568 | tf_op jit(solution)/shard_map/ppermute | solution.py:394
  19.1 2.7 %shard_map.108 = (bf16[16,64,512]{2,1,0:T(8,128)(2,1)S(1)}, bf16[8,16,16,512]{3,2,1,0:T(8,128)(2,1)S(1)}, bf16[8,16,16,512]{3,2,1,0:T(8,128)(2,1)S(1)}) custom-call(bf16[8,128,512]{2,1,0:T(8,128)(2,1)S(1)} %copy-done.1, bf16[8,8,512]{2,1,0:T(8,128)(2,1)S(1)} %collective-permute-done.4.side, f32[1,512]{1,0:T(1,128)S(1)} %bitcast.8, ...), custom_call_target="tpu_custom_call" | custom-call | flops 1000 | bytes 1000 | tf_op jit(solution)/shard_map/pallas_call | solution.py:347
  21.8 0.2 collective-permute-done.1.b
  22.0 0.5 %shard_map.107.a = bf16[144,512]{1,0:T(8,128)(2,1)S(1)} custom-call(bf16[144,512]{1,0:T(8,128)(2,1)S(1)} %shard_map.106.a, bf16[144,512]{1,0:T(8,128)(2,1)S(1)} %collective-permute-done.1.b), custom_call_target="tpu_custom_call" | custom-call | flops 1000 | bytes 1000 | tf_op jit(solution)/shard_map/pallas_call | solution.py:347
  22.5 0.3 collective-permute-done.2
  22.8 3.6 %collective-permute-start.5 = (bf16[144,512]{1,0:T(8,128)(2,1)S(1)}, bf16[144,512]{1,0:T(8,128)(2,1)S(1)}, u32[]{:S(2)}, u32[]{:S(2)}) collective-permute-start(bf16[144,512]{1,0:T(8,128)(2,1)S(1)} %shard_map.107.a), channel_id=1, source_target_pairs={{0,8},{2,10},{4,12},{6,14},{8,0},{10,2},{12,4},{14,6},{1,9},{3,11}... | collective-permute-start | bytes 442376 | tf_op jit(solution)/shard_map/ppermute | solution.py:429
  26.3 0.1 broadcast_select_fusion
  26.4 0.1 collective-permute-start.6
  26.5 1.7 %shard_map.109 = (bf16[6,16,16,512]{3,2,1,0:T(8,128)(2,1)S(1)}, bf16[6,16,16,512]{3,2,1,0:T(8,128)(2,1)S(1)}) custom-call(bf16[3,128,512]{2,1,0:T(8,128)(2,1)S(1)} %get-tuple-element.55.up, bf16[3,128,512]{2,1,0:T(8,128)(2,1)S(1)} %get-tuple-element.54.down, f32[1,512]{1,0:T(1,128)S(1)} %bitcast.9, bf16[512,1536]{1,0:T(8,128)(2,1)S(1)} %copy-done), custom_call_target="tpu_custom_call" | custom-call | flops 1000 | bytes 1000 | tf_op jit(solution)/shard_map/pallas_call | solution.py:347
  28.3 2.6 %shard_map.110.refs_0_ = bf16[8,64,512]{2,1,0:T(8,128)(2,1)S(1)} custom-call(f32[8]{0:T(128)S(1)} %copy-done.7, s32[6]{0:T(128)S(1)} %convert_element_type.3.place, bf16[8,128,512]{2,1,0:T(8,128)(2,1)S(1)} %copy-done.1, f32[1,512]{1,0:T(1,128)S(1)} %bitcast.10, f32[1,512]{1,0:T(1,128)S(1)} %bitcast.11, bf16[512,1536]{1,0:T(8,128)(2,1)S(1)} %copy-done, ...), custom_call_target="tpu_custom_call" | custom-call | flops 1000 | bytes 1000 | tf_op jit(solution)/shard_map/pallas_call | solution.py:347
  30.9 1.8 %collective-permute-done.5.b = bf16[144,512]{1,0:T(8,128)(2,1)S(1)} collective-permute-done((bf16[144,512]{1,0:T(8,128)(2,1)S(1)}, bf16[144,512]{1,0:T(8,128)(2,1)S(1)}, u32[]{:S(2)}, u32[]{:S(2)}) %collective-permute-start.5) | collective-permute-done | bytes 147488 | tf_op jit(solution)/shard_map/ppermute | solution.py:429
  32.7 0.7 %shard_map.111.a = bf16[144,512]{1,0:T(8,128)(2,1)S(1)} custom-call(bf16[144,512]{1,0:T(8,128)(2,1)S(1)} %shard_map.107.a, bf16[144,512]{1,0:T(8,128)(2,1)S(1)} %collective-permute-done.5.b), custom_call_target="tpu_custom_call" | custom-call | flops 1000 | bytes 1000 | tf_op jit(solution)/shard_map/pallas_call | solution.py:347
  33.4 2.7 %collective-permute-start.7 = (bf16[144,512]{1,0:T(8,128)(2,1)S(1)}, bf16[144,512]{1,0:T(8,128)(2,1)S(1)}, u32[]{:S(2)}, u32[]{:S(2)}) collective-permute-start(bf16[144,512]{1,0:T(8,128)(2,1)S(1)} %shard_map.111.a), channel_id=1, source_target_pairs={{0,2},{2,0},{4,6},{6,4},{8,10},{10,8},{12,14},{14,12},{1,3},{3,1},... | collective-permute-start | bytes 442376 | tf_op jit(solution)/shard_map/ppermute | solution.py:469
  36.1 3.2 %shard_map.112 = (bf16[8,64,512]{2,1,0:T(8,128)(2,1)S(1)}, bf16[8,64,512]{2,1,0:T(8,128)(2,1)S(1)}) custom-call(f32[8]{0:T(128)S(1)} %copy-done.7, s32[6]{0:T(128)S(1)} %convert_element_type.3.place, bf16[8,128,512]{2,1,0:T(8,128)(2,1)S(1)} %copy-done.1, bf16[6,8,512]{2,1,0:T(8,128)(2,1)S(1)} %collective-permute-done.6.corner, f32[1,512]{1,0:T(1,128)S(1)} %bitcast.12, ...), custom_call_target="tpu_custom_call" | custom-call | flops 1000 | bytes 1000 | tf_op jit(solution)/shard_map/pallas_call | solution.py:347
  39.4 0.2 collective-permute-done.7.b
  39.6 0.6 %shard_map.113 = bf16[128,512]{1,0:T(8,128)(2,1)S(1)} custom-call(bf16[144,512]{1,0:T(8,128)(2,1)S(1)} %shard_map.111.a, bf16[144,512]{1,0:T(8,128)(2,1)S(1)} %collective-permute-done.7.b, bf16[512,512]{1,0:T(8,128)(2,1)S(1)} %copy-done.4), custom_call_target="tpu_custom_call" | custom-call | flops 1000 | bytes 1000 | tf_op jit(solution)/shard_map/pallas_call | solution.py:347
  40.2 0.1 collective-permute-start.8
  40.3 1.2 %shard_map.114 = bf16[8,128,512]{2,1,0:T(8,128)(2,1)} custom-call(bf16[8,128,512]{2,1,0:T(8,128)(2,1)S(1)} %copy-done.1, bf16[512,512]{1,0:T(8,128)(2,1)S(1)} %copy-done.2, bf16[8,64,512]{2,1,0:T(8,128)(2,1)S(1)} %get-tuple-element.48.first, bf16[8,64,512]{2,1,0:T(8,128)(2,1)S(1)} %get-tuple-element.49.second), custom_call_target="tpu_custom_call" | custom-call | flops 1000 | bytes 1000 | tf_op jit(solution)/shard_map/pallas_call | solution.py:347
  41.5 0.1 collective-permute-done.8
  41.6 0.8 %maximum_select_fusion = bf16[256,512]{1,0:T(8,128)(2,1)} fusion(bf16[128,512]{1,0:T(8,128)(2,1)S(1)} %collective-permute-done.8, bf16[128,512]{1,0:T(8,128)(2,1)S(1)} %shard_map.113, pred[]{:T(512)S(6)} %eq.12), kind=kLoop, calls=%fused_computation.4 | loop fusion | flops 1179648 | bytes 524289 | tf_op jit(solution)/shard_map/jit(_where)/select_n | solution.py:488
  (23 shorter events, 0.1 us)
Async XLA Ops:
  1.6 1.2 %copy-start.1 = (bf16[8,128,512]{2,1,0:T(8,128)(2,1)S(1)}, bf16[8,128,512]{2,1,0:T(8,128)(2,1)}, u32[]{:S(2)}) copy-start(bf16[8,128,512]{2,1,0:T(8,128)(2,1)} %x.9) | copy-start | bytes 3145732
  1.7 5.0 %copy-start.3 = (bf16[512,512]{1,0:T(8,128)(2,1)S(1)}, bf16[512,512]{1,0:T(8,128)(2,1)}, u32[]{:S(2)}) copy-start(bf16[512,512]{1,0:T(8,128)(2,1)} %asking.1) | copy-start | bytes 1572868
  1.7 5.0 %copy-start.5 = (bf16[256,512]{1,0:T(8,128)(2,1)S(1)}, bf16[256,512]{1,0:T(8,128)(2,1)}, u32[]{:S(2)}) copy-start(bf16[256,512]{1,0:T(8,128)(2,1)} %slots.1) | copy-start | bytes 786436
  2.9 3.8 %copy-start = (bf16[512,1536]{1,0:T(8,128)(2,1)S(1)}, bf16[512,1536]{1,0:T(8,128)(2,1)}, u32[]{:S(2)}) copy-start(bf16[512,1536]{1,0:T(8,128)(2,1)} %weights.9) | copy-start | bytes 4718596
  2.9 3.8 %copy-start.6 = (f32[512]{0:T(512)S(1)}, f32[512]{0:T(512)}, u32[]{:S(2)}) copy-start(f32[512]{0:T(512)} %param.10) | copy-start | bytes 6148
  2.9 3.8 %copy-start.7 = (f32[8]{0:T(128)S(1)}, f32[8]{0:T(128)}, u32[]{:S(2)}) copy-start(f32[8]{0:T(128)} %scale.5) | copy-start | bytes 100
  2.9 3.8 %copy-start.8 = (f32[512]{0:T(512)S(1)}, f32[512]{0:T(512)}, u32[]{:S(2)}) copy-start(f32[512]{0:T(512)} %param.14) | copy-start | bytes 6148
  3.0 19.8 %collective-permute-start.2 = (bf16[3,128,512]{2,1,0:T(8,128)(2,1)S(1)}, bf16[3,128,512]{2,1,0:T(8,128)(2,1)S(1)}, u32[]{:S(2)}, u32[]{:S(2)}) collective-permute-start(bf16[3,128,512]{2,1,0:T(8,128)(2,1)S(1)} %get-tuple-element.53), channel_id=1, source_target_pairs={{0,2},{2,0},{4,6},{6,4},{8,10},{10,8},{12,14},{14,12},{1,3},{3,1},... | collective-permute-start | bytes 1179656 | tf_op jit(solution)/shard_map/ppermute | solution.py:392
  6.0 16.8 %collective-permute-start.3 = (bf16[3,128,512]{2,1,0:T(8,128)(2,1)S(1)}, bf16[3,128,512]{2,1,0:T(8,128)(2,1)S(1)}, u32[]{:S(2)}, u32[]{:S(2)}) collective-permute-start(bf16[3,128,512]{2,1,0:T(8,128)(2,1)S(1)} %get-tuple-element.52), channel_id=1, source_target_pairs={{2,4},{4,2},{6,8},{8,6},{10,12},{12,10},{3,5},{5,3},{7,9},{9,7},{1... | collective-permute-start | bytes 1179656 | tf_op jit(solution)/shard_map/ppermute | solution.py:393
  13.0 1.4 %collective-permute-start = (bf16[144,512]{1,0:T(8,128)(2,1)S(1)}, bf16[144,512]{1,0:T(8,128)(2,1)S(1)}, u32[]{:S(2)}, u32[]{:S(2)}) collective-permute-start(bf16[144,512]{1,0:T(8,128)(2,1)S(1)} %get-tuple-element.29), channel_id=1, source_target_pairs={{0,1},{1,0},{2,3},{3,2},{4,5},{5,4},{6,7},{7,6},{8,9},{9,8},{10,11... | collective-permute-start | bytes 442376 | tf_op jit(solution)/shard_map/ppermute | solution.py:418
  15.0 7.0 %collective-permute-start.1 = (bf16[144,512]{1,0:T(8,128)(2,1)S(1)}, bf16[144,512]{1,0:T(8,128)(2,1)S(1)}, u32[]{:S(2)}, u32[]{:S(2)}) collective-permute-start(bf16[144,512]{1,0:T(8,128)(2,1)S(1)} %shard_map.106.a), channel_id=1, source_target_pairs={{0,4},{2,6},{4,0},{6,2},{8,12},{10,14},{12,8},{14,10},{1,5},{3,7},... | collective-permute-start | bytes 442376 | tf_op jit(solution)/shard_map/ppermute | solution.py:429
  17.8 1.3 %collective-permute-start.4 = (bf16[8,8,512]{2,1,0:T(8,128)(2,1)S(1)}, bf16[8,8,512]{2,1,0:T(8,128)(2,1)S(1)}, u32[]{:S(2)}, u32[]{:S(2)}) collective-permute-start(bf16[8,8,512]{2,1,0:T(8,128)(2,1)S(1)} %shard_map.104), channel_id=1, source_target_pairs={{0,1},{1,0},{2,3},{3,2},{4,5},{5,4},{6,7},{7,6},{8,9},{9,8},{10,11... | collective-permute-start | bytes 196616 | tf_op jit(solution)/shard_map/ppermute | solution.py:394
  22.8 9.9 %collective-permute-start.5 = (bf16[144,512]{1,0:T(8,128)(2,1)S(1)}, bf16[144,512]{1,0:T(8,128)(2,1)S(1)}, u32[]{:S(2)}, u32[]{:S(2)}) collective-permute-start(bf16[144,512]{1,0:T(8,128)(2,1)S(1)} %shard_map.107.a), channel_id=1, source_target_pairs={{0,8},{2,10},{4,12},{6,14},{8,0},{10,2},{12,4},{14,6},{1,9},{3,11}... | collective-permute-start | bytes 442376 | tf_op jit(solution)/shard_map/ppermute | solution.py:429
  26.4 1.9 %copy-start.2 = (bf16[512,512]{1,0:T(8,128)(2,1)S(1)}, bf16[512,512]{1,0:T(8,128)(2,1)}, u32[]{:S(2)}) copy-start(bf16[512,512]{1,0:T(8,128)(2,1)} %exits.7) | copy-start | bytes 1572868
  26.4 4.5 %collective-permute-start.6 = (bf16[6,8,512]{2,1,0:T(8,128)(2,1)S(1)}, bf16[6,8,512]{2,1,0:T(8,128)(2,1)S(1)}, u32[]{:S(2)}, u32[]{:S(2)}) collective-permute-start(bf16[6,8,512]{2,1,0:T(8,128)(2,1)S(1)} %pad_maximum_fusion), channel_id=1, source_target_pairs={{0,1},{1,0},{2,3},{3,2},{4,5},{5,4},{6,7},{7,6},{8,9},{9,8},{10,11... | collective-permute-start | bytes 147464 | tf_op jit(solution)/shard_map/ppermute | solution.py:428
  33.4 6.2 %copy-start.4 = (bf16[512,512]{1,0:T(8,128)(2,1)S(1)}, bf16[512,512]{1,0:T(8,128)(2,1)}, u32[]{:S(2)}) copy-start(bf16[512,512]{1,0:T(8,128)(2,1)} %exits.6) | copy-start | bytes 1572868
  33.4 6.2 %collective-permute-start.7 = (bf16[144,512]{1,0:T(8,128)(2,1)S(1)}, bf16[144,512]{1,0:T(8,128)(2,1)S(1)}, u32[]{:S(2)}, u32[]{:S(2)}) collective-permute-start(bf16[144,512]{1,0:T(8,128)(2,1)S(1)} %shard_map.111.a), channel_id=1, source_target_pairs={{0,2},{2,0},{4,6},{6,4},{8,10},{10,8},{12,14},{14,12},{1,3},{3,1},... | collective-permute-start | bytes 442376 | tf_op jit(solution)/shard_map/ppermute | solution.py:469
  40.2 1.4 %collective-permute-start.8 = (bf16[128,512]{1,0:T(8,128)(2,1)S(1)}, bf16[128,512]{1,0:T(8,128)(2,1)S(1)}, u32[]{:S(2)}, u32[]{:S(2)}) collective-permute-start(bf16[128,512]{1,0:T(8,128)(2,1)S(1)} %shard_map.113), channel_id=1, source_target_pairs={{0,1},{1,0},{2,3},{3,2},{4,5},{5,4},{6,7},{7,6},{8,9},{9,8},{10,11... | collective-permute-start | bytes 393224 | tf_op jit(solution)/shard_map/ppermute | solution.py:486
